TPU v7x, 256 devices: a whole 4x4x8 slice. The times are simulated.
256 devices in a mesh: chan: 64 (over y, z, x_lo), win: 4 (over x_hi, core).
Axes of the slice: x: 4 (x_hi: 2, x_lo: 2; x = x_hi * 2 + x_lo), y: 4, z: 8, core: 2. Of those that a mesh axis runs over, the one named last changes fastest.
Arguments:
- source_spectra: bfloat16 [64, 256, 8, 2048], P('chan', None, 'win'), may hold values from -6 to 6
- receiver_spectra: bfloat16 [512, 8, 2048], P('chan', 'win'), may hold values from -6 to 6
- block_order: int32 [2], replicated, may hold values from 0 to 63
- source_mask: int32 [64, 256], P('chan'), may hold values 0 or 1
- receiver_mask: int32 [512], P('chan'), may hold values 0 or 1
Outputs:
- correlations: bfloat16 [2, 256, 512, 2048], P(None, 'win', 'chan')
All inputs are finite; a program needn't handle non-finite values. No bound on the sum of `source_mask` or of `receiver_mask` on one device may be relied on, other than what follows from the above.
Results may differ from a plain program's by a relative error of at most 0.0058.
Values may be sent and summed in bfloat16 or wider, within the bound.
No kernel may reach another device: no remote copies, remote signals or barrier semaphores. Data moves between devices by JAX's collectives and lax.ppermute only.
A program may use at most 192 MiB of HBM per device.

v0:
```python
import math

import jax
import jax.numpy as jnp
from jax import lax
from jax.sharding import PartitionSpec as P


def broadcast(value, axis, source):
    kept = jnp.where(lax.axis_index(axis) == source, value, 0).astype(value.dtype)
    return lax.psum(kept, axis)


def lag_table(freqs):
    nfft = 2 * freqs
    bins = jnp.arange(freqs, dtype=jnp.int32)[:, None]
    lags = jnp.arange(nfft, dtype=jnp.int32)[None, :] - freqs
    phase = jnp.mod(bins * lags, nfft).astype(jnp.float32) * (2.0 * math.pi / nfft)
    weight = jnp.where(bins == 0, 1.0, 2.0).astype(jnp.float32) / math.sqrt(nfft)
    table = jnp.concatenate([weight * jnp.cos(phase), -weight * jnp.sin(phase)], axis=0)
    return table.astype(jnp.bfloat16)


def cross_sum(sources, receivers):
    half = sources.shape[2] // 2
    s_re = sources[..., :half]
    s_im = sources[..., half:]
    r_re = receivers[..., :half]
    r_im = receivers[..., half:]
    real = jnp.einsum("swk,rwk->srk", s_re, r_re, preferred_element_type=jnp.float32)
    real = real + jnp.einsum("swk,rwk->srk", s_im, r_im, preferred_element_type=jnp.float32)
    imag = jnp.einsum("swk,rwk->srk", s_re, r_im, preferred_element_type=jnp.float32)
    imag = imag - jnp.einsum("swk,rwk->srk", s_im, r_re, preferred_element_type=jnp.float32)
    return jnp.concatenate([real, imag], axis=-1)


def on_device(source_spectra, receiver_spectra, block_order, source_mask, receiver_mask):
    freqs = receiver_spectra.shape[2] // 2
    windows = receiver_spectra.shape[1] * lax.axis_size("win")
    table = lag_table(freqs)
    owned = source_spectra[0] * source_mask[0][:, None, None].astype(jnp.bfloat16)
    receivers = receiver_spectra * receiver_mask[:, None, None].astype(jnp.bfloat16)
    steps = block_order.shape[0]
    results = []
    for step in range(steps):
        partial_stack = cross_sum(broadcast(owned, "chan", block_order[step]), receivers)
        share = lax.psum_scatter(partial_stack, "win", scatter_dimension=0, tiled=True)
        part = (share / windows).astype(jnp.bfloat16)
        rows = part.reshape(part.shape[0] * part.shape[1], part.shape[2])
        corr = jnp.dot(rows, table, preferred_element_type=jnp.float32).astype(jnp.bfloat16)
        results.append(corr.reshape(part.shape[0], part.shape[1], table.shape[1]))
    return jnp.stack(results)


def solution(mesh):
    return jax.shard_map(
        on_device,
        mesh=mesh,
        in_specs=(
            P("chan", None, "win", None),
            P("chan", "win", None),
            P(),
            P("chan", None),
            P("chan"),
        ),
        out_specs=P(None, "win", "chan", None),
        check_vma=False,
    )
```

profile of v0, /device:TPU:10, one launch (start us, length us, event | category | flops | bytes accessed | tf_op | source)
XLA Modules:
  0.0 975.6 jit_solution(6525149867481223786)
XLA Ops:
  6.5 0.0 copy-start.3
  6.5 0.0 copy-start.2
  6.5 0.0 all-reduce.3.cloned.1.call-start
  6.5 1.4 fusion.36
  9.3 8.3 copy.23
  17.5 0.7 convert_reduce_fusion
  18.2 4.6 broadcast_select_fusion.1
  22.8 0.0 all-reduce.3.cloned.1.call-update
  22.8 0.0 reduce-scatter.3.cloned.1.call-start
  22.9 0.0 copy-done.3
  22.9 0.0 copy-done.2
  22.9 0.1 copy_multiply_fusion
  23.0 0.4 copy.24
  23.4 0.4 copy.25
  23.8 600.3 %all-reduce.3.cloned.1.call-done = (bf16[256,2,2048]{0,1,2:T(2,128)(2,1)}, bf16[256,2,2048]{0,1,2:T(2,128)(2,1)}) async-done(((bf16[256,2,2048]{0,1,2:T(2,128)(2,1)}, bf16[256,2,2048]{0,1,2:T(2,128)(2,1)}), (bf16[256,2,2048]{0,1,2:T(2,128)(2,1)}, bf16[256,2,2048]{0,1,2:T(2,128)(2,1)})) %all-reduce.3.cloned.1.call-update) | async-done | bytes 4194320 | tf_op jit(solution)/shard_map/psum | solution.py:11
  624.1 0.0 copy-start.1
  624.1 2.8 fusion.28
  626.9 0.0 copy-done.1
  626.9 1.4 fusion.26
  628.4 1.8 add_bitcast_fusion.1
  630.2 1.8 subtract_bitcast_fusion.1
  632.0 11.7 %pad_maximum_fusion = f32[256,8,2048]{0,1,2:T(8,128)} fusion(f32[256,8,1024]{0,1,2:T(8,128)S(1)} %subtract_bitcast_fusion.1, f32[256,8,1024]{0,1,2:T(8,128)S(1)} %add_bitcast_fusion.1), kind=kLoop, calls=%fused_computation | loop fusion | flops 4194304 | bytes 33554432 | tf_op jit(solution)/shard_map/concatenate | solution.py:34
  643.6 18.2 %copy.28 = f32[256,8,2048]{2,1,0:T(8,128)} copy(f32[256,8,2048]{0,1,2:T(8,128)} %pad_maximum_fusion) | data formatting | bytes 33554432 | tf_op jit(solution)/shard_map/concatenate | solution.py:34
  661.8 0.0 copy-start
  661.8 0.0 reduce-scatter.3.cloned.1.call-update
  661.9 0.2 reduce-scatter.5.cloned.1.call-start
  662.1 1.3 copy-done
  663.4 1.4 fusion.22
  664.8 1.4 fusion.20
  666.3 1.9 add_bitcast_fusion
  668.1 1.8 subtract_bitcast_fusion
  670.0 11.7 %pad_maximum_fusion.1 = f32[256,8,2048]{0,1,2:T(8,128)} fusion(f32[256,8,1024]{0,1,2:T(8,128)S(1)} %subtract_bitcast_fusion, f32[256,8,1024]{0,1,2:T(8,128)S(1)} %add_bitcast_fusion), kind=kLoop, calls=%fused_computation.1 | loop fusion | flops 4194304 | bytes 33554432 | tf_op jit(solution)/shard_map/concatenate | solution.py:34
  681.7 19.0 %copy.33 = f32[256,8,2048]{2,1,0:T(8,128)} copy(f32[256,8,2048]{0,1,2:T(8,128)} %pad_maximum_fusion.1) | data formatting | bytes 33554432 | tf_op jit(solution)/shard_map/concatenate | solution.py:34
  700.6 0.0 reduce-scatter.5.cloned.1.call-update
  700.7 35.0 %multiply_convert_fusion.1 = (bf16[1024,2048]{1,0:T(8,128)(2,1)}, bf16[1024,2048]{1,0:T(8,128)(2,1)}) fusion(s32[2048]{0:T(1024)S(1)} %iota_add_fusion, f32[1024]{0:T(1024)S(1)} %get-tuple-element.15, f32[1024]{0:T(1024)S(1)} %get-tuple-element.16), kind=kLoop, calls=%fused_computation.12 | loop fusion | flops 37748736 | bytes 8404992 | tf_op jit(solution)/shard_map/convert
  735.7 81.3 %reduce-scatter.3.cloned.1.call-done = f32[64,8,2048]{2,1,0:T(8,128)} async-done(((f32[256,8,2048]{2,1,0:T(8,128)}), f32[64,8,2048]{2,1,0:T(8,128)}) %reduce-scatter.3.cloned.1.call-update) | async-done | bytes 4194320 | tf_op jit(solution)/shard_map/reduce_scatter | solution.py:47
  817.1 9.1 fusion.11
  826.2 131.3 %reduce-scatter.5.cloned.1.call-done = f32[64,8,2048]{2,1,0:T(8,128)} async-done(((f32[256,8,2048]{2,1,0:T(8,128)}), f32[64,8,2048]{2,1,0:T(8,128)}) %reduce-scatter.5.cloned.1.call-update) | async-done | bytes 4194320 | tf_op jit(solution)/shard_map/reduce_scatter | solution.py:47
  957.5 9.1 fusion.10
  966.7 2.4 pad_maximum_fusion.5
  (4 shorter events, 0.0 us)
Async XLA Ops:
  6.5 16.4 %copy-start.3 = (s32[8]{0:T(128)S(1)}, s32[8]{0:T(128)}, u32[]{:S(2)}) copy-start(s32[8]{0:T(128)} %param.9) | copy-start | bytes 100
  6.5 16.4 %copy-start.2 = (bf16[8,2,2048]{2,1,0:T(2,128)(2,1)S(1)}, bf16[8,2,2048]{2,1,0:T(2,128)(2,1)}, u32[]{:S(2)}) copy-start(bf16[8,2,2048]{2,1,0:T(2,128)(2,1)} %param.6) | copy-start | bytes 196612
  6.5 617.6 %all-reduce.3.cloned.1.call-start = ((), (), s32[]{:S(2)}) async-start(), calls=%async_computation.4 | async-start | bytes 8388608 | tf_op jit(solution)/shard_map/psum | solution.py:11
  22.8 794.2 %reduce-scatter.3.cloned.1.call-start = ((), (), s32[]{:S(2)}) async-start(), calls=%async_computation.2 | async-start | bytes 20971520 | tf_op jit(solution)/shard_map/reduce_scatter | solution.py:47
  624.1 2.8 copy-start.1
  661.8 1.6 copy-start
  661.9 295.6 %reduce-scatter.5.cloned.1.call-start = ((), (), s32[]{:S(2)}) async-start(), calls=%async_computation.3 | async-start | bytes 20971520 | tf_op jit(solution)/shard_map/reduce_scatter | solution.py:47
Sparse Core Ops, SparseCore 0:
  23.0 601.1 all-reduce.2
  662.0 155.0 reduce-scatter.2
  819.9 137.5 reduce-scatter.4
where the time goes:
time: 978 us; the launch traced here: 976 us
  waiting for transfers between devices  813 us (83%)
  other arithmetic  66.1 us (7%)
  local copies, waits for them, and re-layouts  49 us (5%)
  matrix products  32.6 us (3%)
  between operations  14.6 us (1%)
    psum x1, waiting for transfers between devices, broadcast(): return lax.psum(kept, axis)  600 us
    reduce_scatter x2, waiting for transfers between devices, on_device(): lax.psum_scatter(partial_stack, 'win', scatter_dimension=0, tiled=True)  213 us
    concatenate x2, local copies, waits for them, and re-layouts, cross_sum(): return jnp.concatenate([real, imag], axis=-1)  37.2 us
    another operation x1, other arithmetic  35 us
    concatenate x2, other arithmetic, cross_sum(): return jnp.concatenate([real, imag], axis=-1)  23.4 us
  transfers between devices with their start and end apart: 3, of which 3 were waited for; matrix products, arithmetic and copies ran while one was open for 8% of the time, Pallas kernels for 0%

commit v1 on v0

v1 whole, which is shorter than its diff:
```python
import functools
import math

import jax
import jax.numpy as jnp
from jax import lax
from jax.experimental import pallas as pl
from jax.experimental.pallas import tpu as pltpu
from jax.sharding import PartitionSpec as P

NY, NZ, NX = 4, 8, 2


def chan_pairs(dy, dz, dx):
    pairs = []
    for y in range(NY):
        for z in range(NZ):
            for x in range(NX):
                target = (((y + dy) % NY) * NZ + (z + dz) % NZ) * NX + (x + dx) % NX
                pairs.append(((y * NZ + z) * NX + x, target))
    return pairs


def shift(value, dy=0, dz=0, dx=0):
    return lax.ppermute(value, "chan", chan_pairs(dy, dz, dx))


def half_table(freqs, parity):
    nfft = 2 * freqs
    bins = 2 * jnp.arange(freqs // 2, dtype=jnp.int32)[:, None] + parity
    lags = jnp.arange(freqs, dtype=jnp.int32)[None, :] - freqs
    phase = jnp.mod(bins * lags, nfft).astype(jnp.float32) * (2.0 * math.pi / nfft)
    weight = jnp.where(bins == 0, 1.0, 2.0).astype(jnp.float32) / math.sqrt(nfft)
    table = jnp.concatenate([weight * jnp.cos(phase), -weight * jnp.sin(phase)], axis=0)
    return table.astype(jnp.bfloat16)


def split_matrix(width):
    row = jnp.arange(width, dtype=jnp.int32)[:, None]
    column = jnp.arange(width, dtype=jnp.int32)[None, :]
    half = width // 2
    source = jnp.where(column < half, 2 * column, 2 * (column - half) + 1)
    return (row == source).astype(jnp.bfloat16)


def corr_kernel(n_pieces, windows, place, *refs):
    pieces = refs[:n_pieces]
    receivers, split, even, odd = refs[n_pieces : n_pieces + 4]
    out, wide, cross = refs[-3:]
    freqs = even.shape[1]
    lane = 128
    scale = 1.0 / windows
    x = place[place.shape[0] - 1]
    wide[...] = receivers[...].astype(jnp.float32)
    at = 0
    for piece in pieces:
        pairs = piece.shape[0] // 2

        def one_pair(i, _, piece=piece, at=at):
            row = pl.multiple_of(place[at + i] * 16, 16)
            for tile in range(freqs // lane):
                re = pl.ds(tile * lane, lane)
                im = pl.ds(freqs + tile * lane, lane)
                halves_re, halves_im = [], []
                for parity in range(2):
                    spectrum = piece.at[2 * i + (x + parity) % 2]
                    s_re = spectrum[:, re].astype(jnp.float32)
                    s_im = spectrum[:, im].astype(jnp.float32)
                    real = imag = None
                    for w in range(windows):
                        a = jnp.broadcast_to(s_re[w : w + 1], (8, lane))
                        b = jnp.broadcast_to(s_im[w : w + 1], (8, lane))
                        c = wide[w, :, re]
                        d = wide[w, :, im]
                        p = a * c + b * d
                        q = a * d - b * c
                        real = p if real is None else real + p
                        imag = q if imag is None else imag + q
                    halves_re.append(real)
                    halves_im.append(imag)
                cross[pl.ds(row, 16), re] = (jnp.concatenate(halves_re) * scale).astype(jnp.bfloat16)
                cross[pl.ds(row, 16), im] = (jnp.concatenate(halves_im) * scale).astype(jnp.bfloat16)
            return 0

        lax.fori_loop(0, pairs, one_pair, 0)
        at += pairs
    rows = cross.shape[0]
    block = split.shape[0]
    part = 256

    def some_rows(i, _):
        at_rows = pl.ds(pl.multiple_of(i * part, part), part)
        evens, odds = [], []
        for k in range(cross.shape[1] // block):
            both = jnp.dot(cross[at_rows, pl.ds(k * block, block)], split[...], preferred_element_type=jnp.float32).astype(jnp.bfloat16)
            evens.append(both[:, : block // 2])
            odds.append(both[:, block // 2 :])
        lhs_even = jnp.concatenate(evens, axis=1)
        lhs_odd = jnp.concatenate(odds, axis=1)
        for n in range(freqs // 256):
            columns = pl.ds(n * 256, 256)
            e = jnp.dot(lhs_even, even[:, columns], preferred_element_type=jnp.float32)
            o = jnp.dot(lhs_odd, odd[:, columns], preferred_element_type=jnp.float32)
            out[at_rows, columns] = (e + o).astype(jnp.bfloat16)
            out[at_rows, pl.ds(freqs + n * 256, 256)] = (e - o).astype(jnp.bfloat16)
        return 0

    lax.fori_loop(0, rows // part, some_rows, 0)


def correlate(step, steps, place, pieces, receivers, split, even, odd, *result):
    windows, r, width = receivers.shape
    rows = sum(piece.shape[0] for piece in pieces) * r
    whole = pl.BlockSpec(memory_space=pltpu.VMEM)
    return pl.pallas_call(
        functools.partial(corr_kernel, len(pieces), windows),
        grid=(1,),
        out_shape=jax.ShapeDtypeStruct((steps * rows, width), jnp.bfloat16),
        in_specs=[pl.BlockSpec(memory_space=pltpu.SMEM)] + [whole] * (len(pieces) + 4) + [pl.BlockSpec(memory_space=pl.ANY)] * len(result),
        out_specs=pl.BlockSpec((rows, width), lambda i: (step, 0)),
        scratch_shapes=[
            pltpu.VMEM((windows, r, width), jnp.float32),
            pltpu.VMEM((rows, width), jnp.bfloat16),
        ],
        input_output_aliases={len(pieces) + 5: 0} if result else {},
        compiler_params=pltpu.CompilerParams(vmem_limit_bytes=40 * 1024 * 1024),
        cost_estimate=pl.CostEstimate(flops=6 * 10**9, bytes_accessed=10 * 2**20, transcendentals=0),
        name=f"correlate_{step}",
    )(place, *pieces, receivers, split, even, odd, *result)


def on_device(source_spectra, receiver_spectra, block_order, source_mask, receiver_mask):
    width = receiver_spectra.shape[2]
    freqs = width // 2
    own_windows = receiver_spectra.shape[1]
    r = receiver_spectra.shape[0]
    wins = lax.axis_size("win")
    chans = lax.axis_size("chan")
    windows = own_windows * wins
    steps = block_order.shape[0]
    me = lax.axis_index("chan")
    win = lax.axis_index("win")
    y, z, x = me // (NZ * NX), (me // NX) % NZ, me % NX

    owned = source_spectra[0] * source_mask[0][:, None, None].astype(jnp.bfloat16)
    rows = owned.reshape(wins, chans, own_windows, width).transpose(1, 0, 2, 3)
    spread = lax.all_to_all(rows.reshape(chans, wins * own_windows, width), "chan", 0, 0, tiled=True)

    def over_win(give):
        kept = [give(win)]
        for j in range(1, wins):
            kept.append(lax.ppermute(give(win ^ j), "win", [(w, w ^ j) for w in range(wins)]))
        return kept

    receivers = receiver_spectra * receiver_mask[:, None, None].astype(jnp.bfloat16)
    receivers = receivers.transpose(1, 0, 2)
    receivers = jnp.concatenate(over_win(lambda to: receivers), axis=0)

    chosen = jnp.stack([lax.dynamic_index_in_dim(spread, block_order[t], 0, keepdims=False) for t in range(steps)])
    chosen = chosen.reshape(steps, wins, own_windows, width)
    mine = jnp.concatenate(over_win(lambda to: lax.dynamic_index_in_dim(chosen, to, 1, keepdims=False)), axis=1)

    other = shift(mine, dx=1)
    pair = jnp.stack([mine, other], axis=1)
    first, second = pair[0], pair[1]
    y_off = (0, 1, 3, 2)
    z_off = (0, 1, 7, 2, 6, 3, 5, 4)
    first = jnp.concatenate([first] + [shift(first, dy=k) for k in y_off[1:]])
    second = jnp.concatenate([second] + [shift(second, dz=k) for k in z_off[1:]])
    second_pieces = [second] + [shift(second, dy=k) for k in y_off[1:]]
    first_pieces = [first]
    up = down = first
    for k in range(1, 5):
        up = shift(up, dz=1)
        first_pieces.append(up)
        if k < 4:
            down = shift(down, dz=-1)
            first_pieces.append(down)

    ys = jnp.mod(y - jnp.array(y_off, jnp.int32), NY)
    zs = jnp.mod(z - jnp.array(z_off, jnp.int32), NZ)
    place_first = jnp.append((ys[None, :] * NZ + zs[:, None]).reshape(-1), x)
    place_second = jnp.append((ys[:, None] * NZ + zs[None, :]).reshape(-1), x)

    split = split_matrix(256)
    even = half_table(freqs, 0)
    odd = half_table(freqs, 1)
    result = correlate(0, steps, place_first, first_pieces, receivers, split, even, odd)
    result = correlate(1, steps, place_second, second_pieces, receivers, split, even, odd, result)
    return result.reshape(steps, chans, r, width)


def solution(mesh):
    return jax.shard_map(
        on_device,
        mesh=mesh,
        in_specs=(
            P("chan", None, "win", None),
            P("chan", "win", None),
            P(),
            P("chan", None),
            P("chan"),
        ),
        out_specs=P(None, "win", "chan", None),
        check_vma=False,
    )
```

time: 978 us -> 169 us (0.17)
  the two profiles are of different devices: /device:TPU:10 before, /device:TPU:1 now
where the time goes in v1:
time: 169 us; the launch traced here: 168 us
  waiting for transfers between devices  57.4 us (34%)
  starting transfers between devices  56.5 us (33%)
  Pallas kernels  22.4 us (13%)
  other arithmetic  20.9 us (12%)
  local copies, waits for them, and re-layouts  7.06 us (4%)
  between operations  4.14 us (2%)
    ppermute x21, waiting for transfers between devices, shift(): return lax.ppermute(value, 'chan', chan_pairs(dy, dz, dx))  32.2 us
    ppermute x21, starting transfers between devices, shift(): return lax.ppermute(value, 'chan', chan_pairs(dy, dz, dx))  29.6 us
    pallas_call x2, Pallas kernels, correlate(): pl.pallas_call(functools.partial(corr_kernel, len(pieces), windows), grid...  22.4 us
    all_to_all x1, waiting for transfers between devices, on_device(): lax.all_to_all(rows.reshape(chans, wins * own_windows, width), 'chan', 0,...  21.3 us
    another operation x1, other arithmetic  17.7 us
    all_to_all x1, starting transfers between devices, on_device(): lax.all_to_all(rows.reshape(chans, wins * own_windows, width), 'chan', 0,...  14 us
    ppermute x6, starting transfers between devices, over_win(): lax.ppermute(give(win ^ j), 'win', [(w, w ^ j) for w in range(wins)])  12.9 us
    ppermute x6, waiting for transfers between devices, over_win(): lax.ppermute(give(win ^ j), 'win', [(w, w ^ j) for w in range(wins)])  4 us
  transfers between devices with their start and end apart: 28, of which 13 were waited for; matrix products, arithmetic and copies ran while one was open for 13% of the time, Pallas kernels for 7%

profile of v1, /device:TPU:1, one launch (start us, length us, event | category | flops | bytes accessed | tf_op | source)
XLA Modules:
  0.0 168.5 jit_solution(12473318247138143844)
XLA Ops:
  0.0 0.7 convert_reduce_fusion
  0.8 2.5 %copy.25 = bf16[1,256,2,2048]{3,1,2,0:T(8,128)(2,1)S(1)} copy(bf16[1,256,2,2048]{3,2,1,0:T(2,128)(2,1)} %param.7) | data formatting | bytes 4194304 | tf_op args[0]
  3.3 0.2 multiply_bitcast_fusion
  3.5 0.2 copy.26
  3.7 2.5 %copy.27 = bf16[64,8,2048]{2,1,0:T(8,128)(2,1)} copy(bf16[64,8,2048]{2,0,1:T(8,128)(2,1)S(1)} %bitcast.34) | data formatting | bytes 4194304 | tf_op jit(solution)/shard_map/reshape | solution.py:147
  6.2 14.0 %all-to-all-start = ((bf16[64,8,2048]{2,1,0:T(8,128)(2,1)}), bf16[64,8,2048]{2,1,0:T(8,128)(2,1)}, u32[]{:S(2)}, u32[]{:S(2)}) async-start(bf16[64,8,2048]{2,1,0:T(8,128)(2,1)} %copy.27), calls=%async_computation | async-start | bytes 4194304 | tf_op jit(solution)/shard_map/all_to_all | solution.py:147
  20.3 3.3 %collective-permute-start.16 = (bf16[2,8,2048]{2,1,0:T(8,128)(2,1)S(1)}, bf16[2,8,2048]{2,1,0:T(8,128)(2,1)S(1)}, u32[]{:S(2)}, u32[]{:S(2)}) collective-permute-start(bf16[2,8,2048]{2,1,0:T(8,128)(2,1)S(1)} %fusion.10), channel_id=1, source_target_pairs={{0,3},{1,2},{2,1},{3,0},{4,7},{5,6},{6,5},{7,4},{8,11},{9,10},{10,... | collective-permute-start | bytes 196616 | tf_op jit(solution)/shard_map/ppermute | solution.py:152
  23.7 0.5 collective-permute-start.15
  24.2 0.6 fusion.22
  28.9 17.7 %multiply_convert_fusion.1 = (bf16[512,1024]{1,0:T(8,128)(2,1)S(1)}, bf16[512,1024]{1,0:T(8,128)(2,1)S(1)}, bf16[512,1024]{1,0:T(8,128)(2,1)S(1)}, bf16[512,1024]{1,0:T(8,128)(2,1)S(1)}) fusion(f32[512]{0:T(512)S(1)} %get-tuple-element.23, s32[1024]{0:T(1024)S(1)} %iota_add_fusion, s32[512]{0:T(512)S(1)} %get-tuple-element.28, f32[512]{0:T(512)S(1)} %get-tuple-element.26, ...), kind=kLoop, calls=%fused_computation.19 | loop fusion | flops 18874368 | bytes 4210688 | tf_op jit(solution)/shard_map/convert
  46.8 1.5 pad_maximum_fusion.refs_10_.refs_6_
  48.4 21.3 %all-to-all-done = bf16[64,8,2048]{2,1,0:T(8,128)(2,1)} async-done(((bf16[64,8,2048]{2,1,0:T(8,128)(2,1)}), bf16[64,8,2048]{2,1,0:T(8,128)(2,1)}, u32[]{:S(2)}, u32[]{:S(2)}) %all-to-all-start) | async-done | bytes 2097184 | tf_op jit(solution)/shard_map/all_to_all | solution.py:147
  69.6 0.8 constant_dynamic-slice_fusion.5
  70.6 2.9 %collective-permute-start = (bf16[2,2,2048]{2,1,0:T(2,128)(2,1)S(1)}, bf16[2,2,2048]{2,1,0:T(2,128)(2,1)S(1)}, u32[]{:S(2)}, u32[]{:S(2)}) collective-permute-start(bf16[2,2,2048]{2,1,0:T(2,128)(2,1)S(1)} %bitcast.41), channel_id=1, source_target_pairs={{0,1},{1,0},{2,3},{3,2},{4,5},{5,4},{6,7},{7,6},{8,9},{9,8},{10,11... | collective-permute-start | bytes 49160 | tf_op jit(solution)/shard_map/ppermute | solution.py:152
  73.6 2.5 %collective-permute-start.1 = (bf16[2,2,2048]{2,1,0:T(2,128)(2,1)S(1)}, bf16[2,2,2048]{2,1,0:T(2,128)(2,1)S(1)}, u32[]{:S(2)}, u32[]{:S(2)}) collective-permute-start(bf16[2,2,2048]{2,1,0:T(2,128)(2,1)S(1)} %bitcast.40), channel_id=1, source_target_pairs={{0,2},{1,3},{2,0},{3,1},{4,6},{5,7},{6,4},{7,5},{8,10},{9,11},{10,... | collective-permute-start | bytes 49160 | tf_op jit(solution)/shard_map/ppermute | solution.py:152
  76.0 0.8 collective-permute-start.2
  77.0 0.7 collective-permute-done.1
  77.7 3.0 %collective-permute-done.2 = bf16[2,2,2048]{2,1,0:T(2,128)(2,1)S(1)} collective-permute-done((bf16[2,2,2048]{2,1,0:T(2,128)(2,1)S(1)}, bf16[2,2,2048]{2,1,0:T(2,128)(2,1)S(1)}, u32[]{:S(2)}, u32[]{:S(2)}) %collective-permute-start.2) | collective-permute-done | bytes 16416 | tf_op jit(solution)/shard_map/ppermute | solution.py:152
  81.0 3.0 %collective-permute-done.3 = bf16[2,8,2048]{2,1,0:T(8,128)(2,1)S(1)} collective-permute-done((bf16[2,8,2048]{2,1,0:T(8,128)(2,1)S(1)}, bf16[2,8,2048]{2,1,0:T(8,128)(2,1)S(1)}, u32[]{:S(2)}, u32[]{:S(2)}) %collective-permute-start.3) | collective-permute-done | bytes 65568 | tf_op jit(solution)/shard_map/ppermute | solution.py:25
  84.0 1.5 collective-permute-start.19
  85.5 1.4 collective-permute-start.18
  87.0 1.8 %collective-permute-done.19 = bf16[2,8,2048]{2,1,0:T(8,128)(2,1)S(1)} collective-permute-done((bf16[2,8,2048]{2,1,0:T(8,128)(2,1)S(1)}, bf16[2,8,2048]{2,1,0:T(8,128)(2,1)S(1)}, u32[]{:S(2)}, u32[]{:S(2)}) %collective-permute-start.19) | collective-permute-done | bytes 65568 | tf_op jit(solution)/shard_map/ppermute | solution.py:25
  88.7 2.9 %collective-permute-start.14 = (bf16[2,8,2048]{2,1,0:T(8,128)(2,1)S(1)}, bf16[2,8,2048]{2,1,0:T(8,128)(2,1)S(1)}, u32[]{:S(2)}, u32[]{:S(2)}) collective-permute-start(bf16[2,8,2048]{2,1,0:T(8,128)(2,1)S(1)} %fusion.10), channel_id=1, source_target_pairs={{0,1},{1,0},{2,3},{3,2},{4,5},{5,4},{6,7},{7,6},{8,9},{9,8},{10,11... | collective-permute-start | bytes 196616 | tf_op jit(solution)/shard_map/ppermute | solution.py:152
  91.6 0.3 collective-permute-start.4
  92.0 0.3 collective-permute-start.20
  92.2 0.3 collective-permute-done.14
  92.5 4.1 %collective-permute-start.10 = (bf16[2,8,2048]{2,1,0:T(8,128)(2,1)S(1)}, bf16[2,8,2048]{2,1,0:T(8,128)(2,1)S(1)}, u32[]{:S(2)}, u32[]{:S(2)}) collective-permute-start(bf16[2,8,2048]{2,1,0:T(8,128)(2,1)S(1)} %get-tuple-element.6), channel_id=1, source_target_pairs={{0,32},{4,36},{8,40},{12,44},{16,48},{20,52},{24,56},{28,60},{32,0... | collective-permute-start | bytes 196616 | tf_op jit(solution)/shard_map/ppermute | solution.py:25
  96.7 0.5 collective-permute-start.9
  97.1 2.4 %collective-permute-start.6 = (bf16[2,8,2048]{2,1,0:T(8,128)(2,1)S(1)}, bf16[2,8,2048]{2,1,0:T(8,128)(2,1)S(1)}, u32[]{:S(2)}, u32[]{:S(2)}) collective-permute-start(bf16[2,8,2048]{2,1,0:T(8,128)(2,1)S(1)} %get-tuple-element.6), channel_id=1, source_target_pairs={{0,16},{4,20},{8,24},{12,28},{16,32},{20,36},{24,40},{28,44},{32,4... | collective-permute-start | bytes 196616 | tf_op jit(solution)/shard_map/ppermute | solution.py:25
  99.5 2.5 %collective-permute-start.5 = (bf16[2,8,2048]{2,1,0:T(8,128)(2,1)S(1)}, bf16[2,8,2048]{2,1,0:T(8,128)(2,1)S(1)}, u32[]{:S(2)}, u32[]{:S(2)}) collective-permute-start(bf16[2,8,2048]{2,1,0:T(8,128)(2,1)S(1)} %get-tuple-element.6), channel_id=1, source_target_pairs={{0,56},{4,60},{8,0},{12,4},{16,8},{20,12},{24,16},{28,20},{32,24},... | collective-permute-start | bytes 196616 | tf_op jit(solution)/shard_map/ppermute | solution.py:25
  102.0 4.7 %collective-permute-done.5 = bf16[2,8,2048]{2,1,0:T(8,128)(2,1)S(1)} collective-permute-done((bf16[2,8,2048]{2,1,0:T(8,128)(2,1)S(1)}, bf16[2,8,2048]{2,1,0:T(8,128)(2,1)S(1)}, u32[]{:S(2)}, u32[]{:S(2)}) %collective-permute-start.5) | collective-permute-done | bytes 65568 | tf_op jit(solution)/shard_map/ppermute | solution.py:25
  106.7 2.2 %collective-permute-start.21 = (bf16[8,8,2048]{2,1,0:T(8,128)(2,1)S(1)}, bf16[8,8,2048]{2,1,0:T(8,128)(2,1)S(1)}, u32[]{:S(2)}, u32[]{:S(2)}) collective-permute-start(bf16[8,8,2048]{2,1,0:T(8,128)(2,1)S(1)} %pad_maximum_fusion.3.refs_0_), channel_id=1, source_target_pairs={{0,56},{4,60},{8,0},{12,4},{16,8},{20,12},{24,16},{28,20},{32,24},... | collective-permute-start | bytes 786440 | tf_op jit(solution)/shard_map/ppermute | solution.py:25
  108.9 1.3 collective-permute-start.7
  110.2 4.9 %collective-permute-done.7 = bf16[2,8,2048]{2,1,0:T(8,128)(2,1)S(1)} collective-permute-done((bf16[2,8,2048]{2,1,0:T(8,128)(2,1)S(1)}, bf16[2,8,2048]{2,1,0:T(8,128)(2,1)S(1)}, u32[]{:S(2)}, u32[]{:S(2)}) %collective-permute-start.7) | collective-permute-done | bytes 65568 | tf_op jit(solution)/shard_map/ppermute | solution.py:25
  115.0 2.7 %collective-permute-start.8 = (bf16[2,8,2048]{2,1,0:T(8,128)(2,1)S(1)}, bf16[2,8,2048]{2,1,0:T(8,128)(2,1)S(1)}, u32[]{:S(2)}, u32[]{:S(2)}) collective-permute-start(bf16[2,8,2048]{2,1,0:T(8,128)(2,1)S(1)} %get-tuple-element.6), channel_id=1, source_target_pairs={{0,24},{4,28},{8,32},{12,36},{16,40},{20,44},{24,48},{28,52},{32,5... | collective-permute-start | bytes 196616 | tf_op jit(solution)/shard_map/ppermute | solution.py:25
  117.7 4.3 %collective-permute-start.23 = (bf16[8,8,2048]{2,1,0:T(8,128)(2,1)S(1)}, bf16[8,8,2048]{2,1,0:T(8,128)(2,1)S(1)}, u32[]{:S(2)}, u32[]{:S(2)}) collective-permute-start(bf16[8,8,2048]{2,1,0:T(8,128)(2,1)S(1)} %collective-permute-done.21.refs_2_), channel_id=1, source_target_pairs={{0,56},{4,60},{8,0},{12,4},{16,8},{20,12},{24,16},{28,20},{32,24},... | collective-permute-start | bytes 786440 | tf_op jit(solution)/shard_map/ppermute | solution.py:25
  122.0 3.3 %collective-permute-done.23.refs_4_ = bf16[8,8,2048]{2,1,0:T(8,128)(2,1)S(1)} collective-permute-done((bf16[8,8,2048]{2,1,0:T(8,128)(2,1)S(1)}, bf16[8,8,2048]{2,1,0:T(8,128)(2,1)S(1)}, u32[]{:S(2)}, u32[]{:S(2)}) %collective-permute-start.23) | collective-permute-done | bytes 262176 | tf_op jit(solution)/shard_map/ppermute | solution.py:25
  125.3 3.1 %collective-permute-start.25 = (bf16[8,8,2048]{2,1,0:T(8,128)(2,1)S(1)}, bf16[8,8,2048]{2,1,0:T(8,128)(2,1)S(1)}, u32[]{:S(2)}, u32[]{:S(2)}) collective-permute-start(bf16[8,8,2048]{2,1,0:T(8,128)(2,1)S(1)} %collective-permute-done.23.refs_4_), channel_id=1, source_target_pairs={{0,56},{4,60},{8,0},{12,4},{16,8},{20,12},{24,16},{28,20},{32,24},... | collective-permute-start | bytes 786440 | tf_op jit(solution)/shard_map/ppermute | solution.py:25
  128.4 1.6 collective-permute-done.24.refs_5_
  130.0 0.6 collective-permute-start.26
  130.6 1.0 collective-permute-start.13
  131.6 1.1 collective-permute-start.12
  132.7 0.4 collective-permute-start.11
  133.1 3.3 %collective-permute-done.26.refs_7_ = bf16[8,8,2048]{2,1,0:T(8,128)(2,1)S(1)} collective-permute-done((bf16[8,8,2048]{2,1,0:T(8,128)(2,1)S(1)}, bf16[8,8,2048]{2,1,0:T(8,128)(2,1)S(1)}, u32[]{:S(2)}, u32[]{:S(2)}) %collective-permute-start.26) | collective-permute-done | bytes 262176 | tf_op jit(solution)/shard_map/ppermute | solution.py:25
  136.4 11.2 %correlate_0.1.refs_8_ = bf16[1024,2048]{1,0:T(8,128)(2,1)} custom-call(s32[33]{0:T(128)S(1)} %pad_add_fusion.1.place, bf16[8,8,2048]{2,1,0:T(8,128)(2,1)S(1)} %pad_maximum_fusion.3.refs_0_, bf16[8,8,2048]{2,1,0:T(8,128)(2,1)S(1)} %collective-permute-done.20.refs_1_, bf16[8,8,2048]{2,1,0:T(8,128)(2,1)S(1)} %collective-permute-done.21.refs_2_, ...), custom_call_target="tpu_custom_call" | custom-call | flops 6000000000 | bytes 10485760 | tf_op jit(solution)/shard_map/correlate_0/pallas_call | solution.py:115
  147.6 6.7 %collective-permute-done.12.refs_2_ = bf16[16,8,2048]{2,1,0:T(8,128)(2,1)S(1)} collective-permute-done((bf16[16,8,2048]{2,1,0:T(8,128)(2,1)S(1)}, bf16[16,8,2048]{2,1,0:T(8,128)(2,1)S(1)}, u32[]{:S(2)}, u32[]{:S(2)}) %collective-permute-start.12) | collective-permute-done | bytes 524320 | tf_op jit(solution)/shard_map/ppermute | solution.py:25
  154.3 2.9 %collective-permute-done.11.refs_1_ = bf16[16,8,2048]{2,1,0:T(8,128)(2,1)S(1)} collective-permute-done((bf16[16,8,2048]{2,1,0:T(8,128)(2,1)S(1)}, bf16[16,8,2048]{2,1,0:T(8,128)(2,1)S(1)}, u32[]{:S(2)}, u32[]{:S(2)}) %collective-permute-start.11) | collective-permute-done | bytes 524320 | tf_op jit(solution)/shard_map/ppermute | solution.py:25
  157.2 11.2 %correlate_1.1 = bf16[1024,2048]{1,0:T(8,128)(2,1)} custom-call(s32[33]{0:T(128)S(1)} %pad_add_fusion.place, bf16[16,8,2048]{2,1,0:T(8,128)(2,1)S(1)} %constant_dynamic-update-slice_fusion.refs_0_, bf16[16,8,2048]{2,1,0:T(8,128)(2,1)S(1)} %collective-permute-done.11.refs_1_, ...), custom_call_target="tpu_custom_call", output_to_operand_aliasing={{}: (9, {})} | custom-call | flops 6000000000 | bytes 10485760 | tf_op jit(solution)/shard_map/correlate_1/pallas_call | solution.py:115
  (68 shorter events, 1.5 us)
Async XLA Ops:
  6.2 14.0 %copy-start.3 = (s32[8]{0:T(128)S(1)}, s32[8]{0:T(128)}, u32[]{:S(2)}) copy-start(s32[8]{0:T(128)} %param.11) | copy-start | bytes 100
  6.2 14.0 %copy-start.1 = (bf16[8,2,2048]{2,1,0:T(2,128)(2,1)S(1)}, bf16[8,2,2048]{2,1,0:T(2,128)(2,1)}, u32[]{:S(2)}) copy-start(bf16[8,2,2048]{2,1,0:T(2,128)(2,1)} %param.8) | copy-start | bytes 196612
  6.2 18.0 %copy-start.2 = (s32[2]{0:T(128)S(1)}, s32[2]{0:T(128)}, u32[]{:S(2)}) copy-start(s32[2]{0:T(128)} %param.9) | copy-start | bytes 28
  6.2 21.1 %copy-start.5 = (s32[8]{0:T(128)S(1)}, s32[8]{0:T(128)}, u32[]{:S(2)}) copy-start(s32[8]{0:T(128)} %constant.148) | copy-start | bytes 100
  6.2 21.2 %copy-start.4 = (s32[4]{0:T(128)S(1)}, s32[4]{0:T(128)}, u32[]{:S(2)}) copy-start(s32[4]{0:T(128)} %constant.147) | copy-start | bytes 52
  6.2 63.4 %all-to-all-start = ((bf16[64,8,2048]{2,1,0:T(8,128)(2,1)}), bf16[64,8,2048]{2,1,0:T(8,128)(2,1)}, u32[]{:S(2)}, u32[]{:S(2)}) async-start(bf16[64,8,2048]{2,1,0:T(8,128)(2,1)} %copy.27), calls=%async_computation | async-start | bytes 4194304 | tf_op jit(solution)/shard_map/all_to_all | solution.py:147
  20.3 71.9 %collective-permute-start.16 = (bf16[2,8,2048]{2,1,0:T(8,128)(2,1)S(1)}, bf16[2,8,2048]{2,1,0:T(8,128)(2,1)S(1)}, u32[]{:S(2)}, u32[]{:S(2)}) collective-permute-start(bf16[2,8,2048]{2,1,0:T(8,128)(2,1)S(1)} %fusion.10), channel_id=1, source_target_pairs={{0,3},{1,2},{2,1},{3,0},{4,7},{5,6},{6,5},{7,4},{8,11},{9,10},{10,... | collective-permute-start | bytes 196616 | tf_op jit(solution)/shard_map/ppermute | solution.py:152
  23.7 68.6 %collective-permute-start.15 = (bf16[2,8,2048]{2,1,0:T(8,128)(2,1)S(1)}, bf16[2,8,2048]{2,1,0:T(8,128)(2,1)S(1)}, u32[]{:S(2)}, u32[]{:S(2)}) collective-permute-start(bf16[2,8,2048]{2,1,0:T(8,128)(2,1)S(1)} %fusion.10), channel_id=1, source_target_pairs={{0,2},{1,3},{2,0},{3,1},{4,6},{5,7},{6,4},{7,5},{8,10},{9,11},{10,... | collective-permute-start | bytes 196616 | tf_op jit(solution)/shard_map/ppermute | solution.py:152
  70.6 6.3 %collective-permute-start = (bf16[2,2,2048]{2,1,0:T(2,128)(2,1)S(1)}, bf16[2,2,2048]{2,1,0:T(2,128)(2,1)S(1)}, u32[]{:S(2)}, u32[]{:S(2)}) collective-permute-start(bf16[2,2,2048]{2,1,0:T(2,128)(2,1)S(1)} %bitcast.41), channel_id=1, source_target_pairs={{0,1},{1,0},{2,3},{3,2},{4,5},{5,4},{6,7},{7,6},{8,9},{9,8},{10,11... | collective-permute-start | bytes 49160 | tf_op jit(solution)/shard_map/ppermute | solution.py:152
  73.6 4.1 %collective-permute-start.1 = (bf16[2,2,2048]{2,1,0:T(2,128)(2,1)S(1)}, bf16[2,2,2048]{2,1,0:T(2,128)(2,1)S(1)}, u32[]{:S(2)}, u32[]{:S(2)}) collective-permute-start(bf16[2,2,2048]{2,1,0:T(2,128)(2,1)S(1)} %bitcast.40), channel_id=1, source_target_pairs={{0,2},{1,3},{2,0},{3,1},{4,6},{5,7},{6,4},{7,5},{8,10},{9,11},{10,... | collective-permute-start | bytes 49160 | tf_op jit(solution)/shard_map/ppermute | solution.py:152
  76.0 4.7 %collective-permute-start.2 = (bf16[2,2,2048]{2,1,0:T(2,128)(2,1)S(1)}, bf16[2,2,2048]{2,1,0:T(2,128)(2,1)S(1)}, u32[]{:S(2)}, u32[]{:S(2)}) collective-permute-start(bf16[2,2,2048]{2,1,0:T(2,128)(2,1)S(1)} %bitcast.39), channel_id=1, source_target_pairs={{0,3},{1,2},{2,1},{3,0},{4,7},{5,6},{6,5},{7,4},{8,11},{9,10},{10,... | collective-permute-start | bytes 49160 | tf_op jit(solution)/shard_map/ppermute | solution.py:152
  77.0 59.5 %copy-start = (bf16[1024,1024]{1,0:T(8,128)(2,1)S(1)}, bf16[1024,1024]{1,0:T(8,128)(2,1)}, u32[]{:S(2)}) copy-start(bf16[1024,1024]{1,0:T(8,128)(2,1)} %pad_maximum_fusion.refs_10_.refs_6_) | copy-start | bytes 6291460
  80.8 3.2 %collective-permute-start.3 = (bf16[2,8,2048]{2,1,0:T(8,128)(2,1)S(1)}, bf16[2,8,2048]{2,1,0:T(8,128)(2,1)S(1)}, u32[]{:S(2)}, u32[]{:S(2)}) collective-permute-start(bf16[2,8,2048]{2,1,0:T(8,128)(2,1)S(1)} %get-tuple-element.10), channel_id=1, source_target_pairs={{0,4},{4,0},{8,12},{12,8},{16,20},{20,16},{24,28},{28,24},{32,36},... | collective-permute-start | bytes 196616 | tf_op jit(solution)/shard_map/ppermute | solution.py:25
  84.0 4.7 %collective-permute-start.19 = (bf16[2,8,2048]{2,1,0:T(8,128)(2,1)S(1)}, bf16[2,8,2048]{2,1,0:T(8,128)(2,1)S(1)}, u32[]{:S(2)}, u32[]{:S(2)}) collective-permute-start(bf16[2,8,2048]{2,1,0:T(8,128)(2,1)S(1)} %fusion.9), channel_id=1, source_target_pairs={{0,128},{4,132},{8,136},{12,140},{16,144},{20,148},{24,152},{28,15... | collective-permute-start | bytes 196616 | tf_op jit(solution)/shard_map/ppermute | solution.py:25
  85.5 6.1 %collective-permute-start.18 = (bf16[2,8,2048]{2,1,0:T(8,128)(2,1)S(1)}, bf16[2,8,2048]{2,1,0:T(8,128)(2,1)S(1)}, u32[]{:S(2)}, u32[]{:S(2)}) collective-permute-start(bf16[2,8,2048]{2,1,0:T(8,128)(2,1)S(1)} %fusion.9), channel_id=1, source_target_pairs={{0,192},{4,196},{8,200},{12,204},{16,208},{20,212},{24,216},{28,22... | collective-permute-start | bytes 196616 | tf_op jit(solution)/shard_map/ppermute | solution.py:25
  86.9 5.0 %collective-permute-start.17 = (bf16[2,8,2048]{2,1,0:T(8,128)(2,1)S(1)}, bf16[2,8,2048]{2,1,0:T(8,128)(2,1)S(1)}, u32[]{:S(2)}, u32[]{:S(2)}) collective-permute-start(bf16[2,8,2048]{2,1,0:T(8,128)(2,1)S(1)} %fusion.9), channel_id=1, source_target_pairs={{0,64},{4,68},{8,72},{12,76},{16,80},{20,84},{24,88},{28,92},{32,9... | collective-permute-start | bytes 196616 | tf_op jit(solution)/shard_map/ppermute | solution.py:25
  88.7 3.8 %collective-permute-start.14 = (bf16[2,8,2048]{2,1,0:T(8,128)(2,1)S(1)}, bf16[2,8,2048]{2,1,0:T(8,128)(2,1)S(1)}, u32[]{:S(2)}, u32[]{:S(2)}) collective-permute-start(bf16[2,8,2048]{2,1,0:T(8,128)(2,1)S(1)} %fusion.10), channel_id=1, source_target_pairs={{0,1},{1,0},{2,3},{3,2},{4,5},{5,4},{6,7},{7,6},{8,9},{9,8},{10,11... | collective-permute-start | bytes 196616 | tf_op jit(solution)/shard_map/ppermute | solution.py:152
  91.6 7.9 %collective-permute-start.4 = (bf16[2,8,2048]{2,1,0:T(8,128)(2,1)S(1)}, bf16[2,8,2048]{2,1,0:T(8,128)(2,1)S(1)}, u32[]{:S(2)}, u32[]{:S(2)}) collective-permute-start(bf16[2,8,2048]{2,1,0:T(8,128)(2,1)S(1)} %get-tuple-element.6), channel_id=1, source_target_pairs={{0,8},{4,12},{8,16},{12,20},{16,24},{20,28},{24,32},{28,36},{32,40... | collective-permute-start | bytes 196616 | tf_op jit(solution)/shard_map/ppermute | solution.py:25
  92.0 16.9 %collective-permute-start.20 = (bf16[8,8,2048]{2,1,0:T(8,128)(2,1)S(1)}, bf16[8,8,2048]{2,1,0:T(8,128)(2,1)S(1)}, u32[]{:S(2)}, u32[]{:S(2)}) collective-permute-start(bf16[8,8,2048]{2,1,0:T(8,128)(2,1)S(1)} %pad_maximum_fusion.3.refs_0_), channel_id=1, source_target_pairs={{0,8},{4,12},{8,16},{12,20},{16,24},{20,28},{24,32},{28,36},{32,40... | collective-permute-start | bytes 786440 | tf_op jit(solution)/shard_map/ppermute | solution.py:25
  92.5 38.0 %collective-permute-start.10 = (bf16[2,8,2048]{2,1,0:T(8,128)(2,1)S(1)}, bf16[2,8,2048]{2,1,0:T(8,128)(2,1)S(1)}, u32[]{:S(2)}, u32[]{:S(2)}) collective-permute-start(bf16[2,8,2048]{2,1,0:T(8,128)(2,1)S(1)} %get-tuple-element.6), channel_id=1, source_target_pairs={{0,32},{4,36},{8,40},{12,44},{16,48},{20,52},{24,56},{28,60},{32,0... | collective-permute-start | bytes 196616 | tf_op jit(solution)/shard_map/ppermute | solution.py:25
  96.7 33.9 %collective-permute-start.9 = (bf16[2,8,2048]{2,1,0:T(8,128)(2,1)S(1)}, bf16[2,8,2048]{2,1,0:T(8,128)(2,1)S(1)}, u32[]{:S(2)}, u32[]{:S(2)}) collective-permute-start(bf16[2,8,2048]{2,1,0:T(8,128)(2,1)S(1)} %get-tuple-element.6), channel_id=1, source_target_pairs={{0,40},{4,44},{8,48},{12,52},{16,56},{20,60},{24,0},{28,4},{32,8},... | collective-permute-start | bytes 196616 | tf_op jit(solution)/shard_map/ppermute | solution.py:25
  97.1 11.8 %collective-permute-start.6 = (bf16[2,8,2048]{2,1,0:T(8,128)(2,1)S(1)}, bf16[2,8,2048]{2,1,0:T(8,128)(2,1)S(1)}, u32[]{:S(2)}, u32[]{:S(2)}) collective-permute-start(bf16[2,8,2048]{2,1,0:T(8,128)(2,1)S(1)} %get-tuple-element.6), channel_id=1, source_target_pairs={{0,16},{4,20},{8,24},{12,28},{16,32},{20,36},{24,40},{28,44},{32,4... | collective-permute-start | bytes 196616 | tf_op jit(solution)/shard_map/ppermute | solution.py:25
  99.5 7.2 %collective-permute-start.5 = (bf16[2,8,2048]{2,1,0:T(8,128)(2,1)S(1)}, bf16[2,8,2048]{2,1,0:T(8,128)(2,1)S(1)}, u32[]{:S(2)}, u32[]{:S(2)}) collective-permute-start(bf16[2,8,2048]{2,1,0:T(8,128)(2,1)S(1)} %get-tuple-element.6), channel_id=1, source_target_pairs={{0,56},{4,60},{8,0},{12,4},{16,8},{20,12},{24,16},{28,20},{32,24},... | collective-permute-start | bytes 196616 | tf_op jit(solution)/shard_map/ppermute | solution.py:25
  106.7 11.0 %collective-permute-start.21 = (bf16[8,8,2048]{2,1,0:T(8,128)(2,1)S(1)}, bf16[8,8,2048]{2,1,0:T(8,128)(2,1)S(1)}, u32[]{:S(2)}, u32[]{:S(2)}) collective-permute-start(bf16[8,8,2048]{2,1,0:T(8,128)(2,1)S(1)} %pad_maximum_fusion.3.refs_0_), channel_id=1, source_target_pairs={{0,56},{4,60},{8,0},{12,4},{16,8},{20,12},{24,16},{28,20},{32,24},... | collective-permute-start | bytes 786440 | tf_op jit(solution)/shard_map/ppermute | solution.py:25
  108.9 13.1 %collective-permute-start.22 = (bf16[8,8,2048]{2,1,0:T(8,128)(2,1)S(1)}, bf16[8,8,2048]{2,1,0:T(8,128)(2,1)S(1)}, u32[]{:S(2)}, u32[]{:S(2)}) collective-permute-start(bf16[8,8,2048]{2,1,0:T(8,128)(2,1)S(1)} %collective-permute-done.20.refs_1_), channel_id=1, source_target_pairs={{0,8},{4,12},{8,16},{12,20},{16,24},{20,28},{24,32},{28,36},{32,40... | collective-permute-start | bytes 786440 | tf_op jit(solution)/shard_map/ppermute | solution.py:25
  108.9 6.1 %collective-permute-start.7 = (bf16[2,8,2048]{2,1,0:T(8,128)(2,1)S(1)}, bf16[2,8,2048]{2,1,0:T(8,128)(2,1)S(1)}, u32[]{:S(2)}, u32[]{:S(2)}) collective-permute-start(bf16[2,8,2048]{2,1,0:T(8,128)(2,1)S(1)} %get-tuple-element.6), channel_id=1, source_target_pairs={{0,48},{4,52},{8,56},{12,60},{16,0},{20,4},{24,8},{28,12},{32,16},... | collective-permute-start | bytes 196616 | tf_op jit(solution)/shard_map/ppermute | solution.py:25
  115.0 6.9 %collective-permute-start.8 = (bf16[2,8,2048]{2,1,0:T(8,128)(2,1)S(1)}, bf16[2,8,2048]{2,1,0:T(8,128)(2,1)S(1)}, u32[]{:S(2)}, u32[]{:S(2)}) collective-permute-start(bf16[2,8,2048]{2,1,0:T(8,128)(2,1)S(1)} %get-tuple-element.6), channel_id=1, source_target_pairs={{0,24},{4,28},{8,32},{12,36},{16,40},{20,44},{24,48},{28,52},{32,5... | collective-permute-start | bytes 196616 | tf_op jit(solution)/shard_map/ppermute | solution.py:25
  117.7 7.6 %collective-permute-start.23 = (bf16[8,8,2048]{2,1,0:T(8,128)(2,1)S(1)}, bf16[8,8,2048]{2,1,0:T(8,128)(2,1)S(1)}, u32[]{:S(2)}, u32[]{:S(2)}) collective-permute-start(bf16[8,8,2048]{2,1,0:T(8,128)(2,1)S(1)} %collective-permute-done.21.refs_2_), channel_id=1, source_target_pairs={{0,56},{4,60},{8,0},{12,4},{16,8},{20,12},{24,16},{28,20},{32,24},... | collective-permute-start | bytes 786440 | tf_op jit(solution)/shard_map/ppermute | solution.py:25
  122.0 8.0 %collective-permute-start.24 = (bf16[8,8,2048]{2,1,0:T(8,128)(2,1)S(1)}, bf16[8,8,2048]{2,1,0:T(8,128)(2,1)S(1)}, u32[]{:S(2)}, u32[]{:S(2)}) collective-permute-start(bf16[8,8,2048]{2,1,0:T(8,128)(2,1)S(1)} %collective-permute-done.22.refs_3_), channel_id=1, source_target_pairs={{0,8},{4,12},{8,16},{12,20},{16,24},{20,28},{24,32},{28,36},{32,40... | collective-permute-start | bytes 786440 | tf_op jit(solution)/shard_map/ppermute | solution.py:25
  125.3 7.8 %collective-permute-start.25 = (bf16[8,8,2048]{2,1,0:T(8,128)(2,1)S(1)}, bf16[8,8,2048]{2,1,0:T(8,128)(2,1)S(1)}, u32[]{:S(2)}, u32[]{:S(2)}) collective-permute-start(bf16[8,8,2048]{2,1,0:T(8,128)(2,1)S(1)} %collective-permute-done.23.refs_4_), channel_id=1, source_target_pairs={{0,56},{4,60},{8,0},{12,4},{16,8},{20,12},{24,16},{28,20},{32,24},... | collective-permute-start | bytes 786440 | tf_op jit(solution)/shard_map/ppermute | solution.py:25
  130.0 6.4 %collective-permute-start.26 = (bf16[8,8,2048]{2,1,0:T(8,128)(2,1)S(1)}, bf16[8,8,2048]{2,1,0:T(8,128)(2,1)S(1)}, u32[]{:S(2)}, u32[]{:S(2)}) collective-permute-start(bf16[8,8,2048]{2,1,0:T(8,128)(2,1)S(1)} %collective-permute-done.24.refs_5_), channel_id=1, source_target_pairs={{0,8},{4,12},{8,16},{12,20},{16,24},{20,28},{24,32},{28,36},{32,40... | collective-permute-start | bytes 786440 | tf_op jit(solution)/shard_map/ppermute | solution.py:25
  130.6 17.0 %collective-permute-start.13 = (bf16[16,8,2048]{2,1,0:T(8,128)(2,1)S(1)}, bf16[16,8,2048]{2,1,0:T(8,128)(2,1)S(1)}, u32[]{:S(2)}, u32[]{:S(2)}) collective-permute-start(bf16[16,8,2048]{2,1,0:T(8,128)(2,1)S(1)} %constant_dynamic-update-slice_fusion.refs_0_), channel_id=1, source_target_pairs={{0,128},{4,132},{8,136},{12,140},{16,144},{20,148},{24,152},{28,15... | collective-permute-start | bytes 1572872 | tf_op jit(solution)/shard_map/ppermute | solution.py:25
  131.6 22.7 %collective-permute-start.12 = (bf16[16,8,2048]{2,1,0:T(8,128)(2,1)S(1)}, bf16[16,8,2048]{2,1,0:T(8,128)(2,1)S(1)}, u32[]{:S(2)}, u32[]{:S(2)}) collective-permute-start(bf16[16,8,2048]{2,1,0:T(8,128)(2,1)S(1)} %constant_dynamic-update-slice_fusion.refs_0_), channel_id=1, source_target_pairs={{0,192},{4,196},{8,200},{12,204},{16,208},{20,212},{24,216},{28,22... | collective-permute-start | bytes 1572872 | tf_op jit(solution)/shard_map/ppermute | solution.py:25
  132.7 24.5 %collective-permute-start.11 = (bf16[16,8,2048]{2,1,0:T(8,128)(2,1)S(1)}, bf16[16,8,2048]{2,1,0:T(8,128)(2,1)S(1)}, u32[]{:S(2)}, u32[]{:S(2)}) collective-permute-start(bf16[16,8,2048]{2,1,0:T(8,128)(2,1)S(1)} %constant_dynamic-update-slice_fusion.refs_0_), channel_id=1, source_target_pairs={{0,64},{4,68},{8,72},{12,76},{16,80},{20,84},{24,88},{28,92},{32,9... | collective-permute-start | bytes 1572872 | tf_op jit(solution)/shard_map/ppermute | solution.py:25

commit v2 on v0

v2 whole, which is shorter than its diff:
```python
import functools
import math

import jax
import jax.numpy as jnp
from jax import lax
from jax.experimental import pallas as pl
from jax.experimental.pallas import tpu as pltpu
from jax.sharding import PartitionSpec as P

NY, NZ, NX = 4, 8, 2
BF16 = jnp.bfloat16
F32 = jnp.float32


def chan_index(y, z, x):
    return ((y % NY) * NZ + z % NZ) * NX + x % NX


def shift(value, dy=0, dz=0, dx=0):
    pairs = []
    for y in range(NY):
        for z in range(NZ):
            for x in range(NX):
                pairs.append((chan_index(y, z, x), chan_index(y + dy, z + dz, x + dx)))
    return lax.ppermute(value, "chan", pairs)


def yx_groups():
    return [[chan_index(y, z, x) for y in range(NY) for x in range(NX)] for z in range(NZ)]


def z_groups():
    return [[chan_index(y, z, x) for z in range(NZ)] for y in range(NY) for x in range(NX)]


def yx_win_groups(wins):
    return [[chan * wins + w for chan in group for w in range(wins)] for group in yx_groups()]


def half_table(freqs, parity):
    nfft = 2 * freqs
    bins = 2 * jnp.arange(freqs // 2, dtype=jnp.int32)[:, None] + parity
    lags = jnp.arange(freqs, dtype=jnp.int32)[None, :] - freqs
    phase = jnp.mod(bins * lags, nfft).astype(F32) * (2.0 * math.pi / nfft)
    weight = jnp.where(bins == 0, 1.0, 2.0).astype(F32) / math.sqrt(nfft)
    table = jnp.concatenate([weight * jnp.cos(phase), -weight * jnp.sin(phase)], axis=0)
    return table.astype(BF16)


def split_matrix(width):
    row = jnp.arange(width, dtype=jnp.int32)[:, None]
    column = jnp.arange(width, dtype=jnp.int32)[None, :]
    half = width // 2
    source = jnp.where(column < half, 2 * column, 2 * (column - half) + 1)
    return (row == source).astype(BF16)


def add_cross(piece, receivers, wide, cross, first_pair):
    windows, r, width = receivers.shape
    freqs = width // 2
    lane = 128
    scale = 1.0 / windows

    def one_pair(i, _, step):
        row = pl.multiple_of((first_pair + step * (piece.shape[0] // 2) + i) * 2 * r, 2 * r)
        wide[...] = piece[pl.ds(2 * i, 2), step * windows : (step + 1) * windows].astype(F32)
        for tile in range(freqs // lane):
            re = pl.ds(tile * lane, lane)
            im = pl.ds(freqs + tile * lane, lane)
            real, imag = [None, None], [None, None]
            for w in range(windows):
                c, d = receivers[w, :, re], receivers[w, :, im]
                for member in range(2):
                    a = jnp.broadcast_to(wide[member, w : w + 1, re], c.shape)
                    b = jnp.broadcast_to(wide[member, w : w + 1, im], c.shape)
                    p, q = a * c + b * d, a * d - b * c
                    real[member] = p if w == 0 else real[member] + p
                    imag[member] = q if w == 0 else imag[member] + q
            cross[pl.ds(row, 2 * r), re] = (jnp.concatenate(real) * scale).astype(BF16)
            cross[pl.ds(row, 2 * r), im] = (jnp.concatenate(imag) * scale).astype(BF16)
        return 0

    for step in range(piece.shape[1] // windows):
        lax.fori_loop(0, piece.shape[0] // 2, functools.partial(one_pair, step=step), 0)


def lag_kernel(n_pieces, first_place, place, *refs):
    pieces = refs[:n_pieces]
    receivers, split, even_in, odd_in = refs[n_pieces : n_pieces + 4]
    out, wide, cross, result, even, odd, table_sem, sem = refs[-8:]
    tables = [
        pltpu.make_async_copy(even_in, even, table_sem.at[0]),
        pltpu.make_async_copy(odd_in, odd, table_sem.at[1]),
    ]
    for copy in tables:
        copy.start()
    freqs = even.shape[1]
    pair = 2 * receivers.shape[1]
    at = 0
    for piece in pieces:
        add_cross(piece, receivers, wide, cross, at)
        at += piece.shape[0] * piece.shape[1] // (2 * receivers.shape[0])
    for copy in tables:
        copy.wait()
    block = split.shape[0]
    total = at * pair
    chunk = 256 if total % 256 == 0 else 192 if total % 192 == 0 else total
    copies = []
    for first in range(0, total, chunk):
        rows = pl.ds(first, chunk)
        evens, odds = [], []
        for k in range(cross.shape[1] // block):
            both = jnp.dot(cross[rows, pl.ds(k * block, block)], split[...], preferred_element_type=F32).astype(BF16)
            evens.append(both[:, : block // 2])
            odds.append(both[:, block // 2 :])
        lhs_even = jnp.concatenate(evens, axis=1)
        lhs_odd = jnp.concatenate(odds, axis=1)
        for n in range(freqs // 256):
            columns = pl.ds(n * 256, 256)
            e = jnp.dot(lhs_even, even[:, columns], preferred_element_type=F32)
            o = jnp.dot(lhs_odd, odd[:, columns], preferred_element_type=F32)
            result[rows, columns] = (e + o).astype(BF16)
            result[rows, pl.ds(freqs + n * 256, 256)] = (e - o).astype(BF16)
        for i in range(first // pair, (first + chunk) // pair):
            row = pl.multiple_of(place[first_place + i] * pair, pair)
            copy = pltpu.make_async_copy(result.at[pl.ds(i * pair, pair)], out.at[pl.ds(row, pair)], sem.at[i])
            copy.start()
            copies.append(copy)
    for copy in copies:
        copy.wait()


def lags_of(name, place, first_place, pieces, receivers, split, even, odd, out_rows, *result):
    windows, r, width = receivers.shape
    rows = sum(piece.shape[0] * piece.shape[1] for piece in pieces) * r // windows
    whole = pl.BlockSpec(memory_space=pltpu.VMEM)
    anywhere = pl.BlockSpec(memory_space=pl.ANY)
    in_hbm = pl.BlockSpec(memory_space=pltpu.HBM)
    held = len(pieces)
    return pl.pallas_call(
        functools.partial(lag_kernel, len(pieces), first_place),
        out_shape=jax.ShapeDtypeStruct((out_rows, width), BF16),
        in_specs=[pl.BlockSpec(memory_space=pltpu.SMEM)] + [whole] * (held + 2) + [in_hbm] * 2 + [anywhere] * len(result),
        out_specs=anywhere,
        scratch_shapes=[
            pltpu.VMEM((2, windows, width), F32),
            pltpu.VMEM((rows, width), BF16),
            pltpu.VMEM((rows, width), BF16),
            pltpu.VMEM(even.shape, BF16),
            pltpu.VMEM(odd.shape, BF16),
            pltpu.SemaphoreType.DMA((2,)),
            pltpu.SemaphoreType.DMA((rows // (2 * r),)),
        ],
        input_output_aliases={held + 5: 0} if result else {},
        compiler_params=pltpu.CompilerParams(vmem_limit_bytes=16 * 1024 * 1024),
        cost_estimate=pl.CostEstimate(flops=rows * 12 * 10**6, bytes_accessed=rows * 2**14, transcendentals=0),
        name=name,
    )(place, *pieces, receivers, split, even, odd, *result)


def on_device(source_spectra, receiver_spectra, block_order, source_mask, receiver_mask):
    width = receiver_spectra.shape[2]
    freqs = width // 2
    r, own_windows = receiver_spectra.shape[:2]
    wins = lax.axis_size("win")
    chans = lax.axis_size("chan")
    windows = own_windows * wins
    steps = block_order.shape[0]
    me = lax.axis_index("chan")
    win = lax.axis_index("win")
    z = (me // NX) % NZ

    owned = source_spectra[0] * source_mask[0][:, None, None].astype(BF16)
    rows = owned.reshape(wins, NY, NZ, NX, own_windows, width).transpose(1, 3, 0, 2, 4, 5)
    rows = rows.reshape(NY * NX * wins, NZ * own_windows, width)
    rows, receiver_spectra = lax.optimization_barrier((rows, receiver_spectra))
    spread = lax.all_to_all(rows, ("chan", "win"), 0, 0, tiled=True, axis_index_groups=yx_win_groups(wins))

    def all_windows(give):
        kept = [give(win)]
        for j in range(1, wins):
            kept.append(lax.ppermute(give(jnp.mod(win + j, wins)), "win", [(w, (w + j) % wins) for w in range(wins)]))
        return jnp.concatenate([lax.select_n(jnp.mod(win - w, wins), *kept) for w in range(wins)], axis=0)

    split = split_matrix(256)
    even = half_table(freqs, 0)
    odd = half_table(freqs, 1)
    receivers = receiver_spectra * receiver_mask[:, None, None].astype(BF16)
    receivers = all_windows(lambda to: receivers.transpose(1, 0, 2)).astype(F32)

    ys = jnp.arange(NY, dtype=jnp.int32)
    zs = jnp.mod(z - jnp.array((0, 1, -1, 2, -2, 3, -3), jnp.int32), NZ)
    bases = (jnp.arange(steps, dtype=jnp.int32)[:, None] * (NY * NZ) + (ys * NZ)[None, :]).reshape(1, -1)
    last = (bases + jnp.mod(z + NZ // 2, NZ)).reshape(steps, 2, NY // 2).transpose(1, 0, 2)
    place = jnp.concatenate([(bases + zs[:, None]).reshape(-1), last.reshape(-1)])
    owner_y, owner_z, owner_x = block_order // (NZ * NX), (block_order // NX) % NZ, block_order % NX
    first_from = [(owner_y[t] * NX + owner_x[t]) * wins for t in range(steps)]
    owner_z = [owner_z[t] for t in range(steps)]
    shadow = (receivers, split, even, odd, place, first_from, owner_z)
    spread, shadow = lax.optimization_barrier((spread, shadow))
    receivers, split, even, odd, place, first_from, owner_z = shadow

    chosen = [lax.dynamic_slice_in_dim(spread, first_from[t], wins, 0) for t in range(steps)]
    chosen = jnp.stack([part.reshape(wins, NZ, own_windows, width) for part in chosen])
    chosen = chosen.transpose(2, 0, 1, 3, 4).reshape(NZ, steps * windows, width)
    chosen = lax.all_to_all(chosen, "chan", 0, 0, tiled=True, axis_index_groups=z_groups())
    chosen = [lax.dynamic_index_in_dim(chosen, owner_z[t], 0, keepdims=False) for t in range(steps)]
    chosen = jnp.concatenate([part[t * windows : (t + 1) * windows] for t, part in enumerate(chosen)])

    def gather_yx(value):
        copies = jnp.broadcast_to(value[None], (NY * NX,) + value.shape)
        return lax.all_to_all(copies, "chan", 0, 0, tiled=True, axis_index_groups=yx_groups())

    near = gather_yx(chosen)

    tables = (receivers, split, even, odd, steps * chans * r)
    up, down = shift(near, dz=1), shift(near, dz=-1)
    up2, down2 = shift(up, dz=1), shift(down, dz=-1)
    pairs = steps * NY
    half = near.shape[0] // 2
    out = lags_of("lags_a", place, 0, (near, up, down), *tables)
    up2, down2, out = lax.optimization_barrier((up2, down2, out))
    up3, down3 = shift(up2, dz=1), shift(down2, dz=-1)
    out = lags_of("lags_b", place, 3 * pairs, (up2, down2), *tables, out)
    up3, down3, out = lax.optimization_barrier((up3, down3, out))
    up4, down4 = shift(up3[:half], dz=1), shift(down3[half:], dz=-1)
    out = lags_of("lags_c", place, 5 * pairs, (up3, down3), *tables, out)
    up4, down4, out = lax.optimization_barrier((up4, down4, out))
    out = lags_of("lags_d", place, 7 * pairs, (up4, down4), *tables, out)
    return out.reshape(steps, chans, r, width)


def solution(mesh):
    return jax.shard_map(
        on_device,
        mesh=mesh,
        in_specs=(
            P("chan", None, "win", None),
            P("chan", "win", None),
            P(),
            P("chan", None),
            P("chan"),
        ),
        out_specs=P(None, "win", "chan", None),
        check_vma=False,
    )
```

time: 978 us -> 143 us (0.15)
  waiting for transfers between devices: 813 us -> 33.6 us
  other arithmetic: 66.1 us -> 25.3 us
  local copies, waits for them, and re-layouts: 49 us -> 8.61 us
  matrix products: 32.6 us -> 0 us
  starting transfers between devices: 0.27 us -> 30.3 us
  Pallas kernels: 0 us -> 23.5 us
  blocking collectives: 0 us -> 14.3 us
    psum x1 -> x0, waiting for transfers between devices: 600 us -> none  [broadcast(): return lax.psum(kept, axis)]
    reduce_scatter x2 -> x0, waiting for transfers between devices: 213 us -> none  [on_device(): lax.psum_scatter(partial_stack, 'win', scatter_dimension=0, tiled=True)]
    concatenate x2 -> x0, local copies, waits for them, and re-layouts: 37.2 us -> none  [cross_sum(): return jnp.concatenate([real, imag], axis=-1)]
    dot_general x10 -> x0, matrix products: 32.6 us -> none  [the longest x2 18.3 us: on_device(): jnp.dot(rows, table, preferred_element_type=jnp.float32)]
    pallas_call x0 -> x4, Pallas kernels: none -> 23.5 us  [lags_of(): pl.pallas_call(functools.partial(lag_kernel, len(pieces), first_place), o...]
    concatenate x2 -> x3, other arithmetic: 23.4 us -> 1.83 us  [the longest x1 1.75 us: half_table(): jnp.concatenate([weight * jnp.cos(phase), -weight * jnp.sin(phase)], axis=0)]
    another operation x2 -> x1, other arithmetic: 37.4 us -> 17.7 us
    ppermute x0 -> x11, waiting for transfers between devices: none -> 18.4 us  [the longest x8 18.4 us: shift(): return lax.ppermute(value, 'chan', pairs)]
  transfers between devices with their start and end apart: 3 -> 13, of which waited for: 3 -> 6; matrix products, arithmetic and copies ran while one was open for 8% -> 15% of each run, Pallas kernels for 0% -> 14%
where the time goes in v2:
time: 143 us; the launch traced here: 142 us
  waiting for transfers between devices  33.6 us (23%)
  starting transfers between devices  30.3 us (21%)
  other arithmetic  25.3 us (18%)
  Pallas kernels  23.5 us (16%)
  blocking collectives  14.3 us (10%)
  local copies, waits for them, and re-layouts  8.61 us (6%)
  between operations  6.96 us (5%)
    pallas_call x4, Pallas kernels, lags_of(): pl.pallas_call(functools.partial(lag_kernel, len(pieces), first_place), o...  23.5 us
    ppermute x8, waiting for transfers between devices, shift(): return lax.ppermute(value, 'chan', pairs)  18.4 us
    another operation x1, other arithmetic  17.7 us
    all_to_all x1, blocking collectives, gather_yx(): lax.all_to_all(copies, 'chan', 0, 0, tiled=True, axis_index_groups=yx_gro...  14.3 us
    all_to_all x1, waiting for transfers between devices, on_device(): lax.all_to_all(chosen, 'chan', 0, 0, tiled=True, axis_index_groups=z_grou...  13.8 us
    ppermute x8, starting transfers between devices, shift(): return lax.ppermute(value, 'chan', pairs)  10.6 us
    all_to_all x1, starting transfers between devices, on_device(): lax.all_to_all(chosen, 'chan', 0, 0, tiled=True, axis_index_groups=z_grou...  8.47 us
    all_to_all x1, starting transfers between devices, on_device(): lax.all_to_all(rows, ('chan', 'win'), 0, 0, tiled=True, axis_index_groups...  8.43 us
  transfers between devices with their start and end apart: 13, of which 6 were waited for; matrix products, arithmetic and copies ran while one was open for 15% of the time, Pallas kernels for 14%

profile of v2, /device:TPU:10, one launch (start us, length us, event | category | flops | bytes accessed | tf_op | source)
XLA Modules:
  0.0 142.5 jit_solution(7496557456181880929)
XLA Ops:
  0.0 0.7 convert_element_type.35
  0.7 0.7 convert_reduce_fusion
  1.4 0.2 convert_element_type.34
  1.5 0.2 copy.35
  1.7 3.5 %fusion.6 = bf16[4,2,4,8,2,2048]{5,4,3,2,1,0:T(2,128)(2,1)S(1)} fusion(bf16[4,4,8,2,2,2048]{5,4,3,2,1,0:T(2,128)(2,1)} %bitcast.21, bf16[4,4,8,2]{2,0,3,1:T(4,128)(2,1)S(1)} %copy.35), kind=kLoop, calls=%fused_computation.19 | loop fusion | flops 1048576 | bytes 4194816 | tf_op jit(solution)/shard_map/transpose | solution.py:175
  5.2 0.0 copy-start.1
  5.2 2.2 %reshape.142 = bf16[32,16,2048]{2,1,0:T(8,128)(2,1)} reshape(bf16[4,2,4,8,2,2048]{5,4,3,2,1,0:T(2,128)(2,1)S(1)} %fusion.6) | data formatting | bytes 4194304 | tf_op jit(solution)/shard_map/reshape | solution.py:176
  7.4 0.1 fusion.8
  7.5 2.2 %collective-permute-start.1 = (bf16[2,8,2048]{2,1,0:T(8,128)(2,1)S(1)}, bf16[2,8,2048]{2,1,0:T(8,128)(2,1)S(1)}, u32[]{:S(2)}, u32[]{:S(2)}) collective-permute-start(bf16[2,8,2048]{2,1,0:T(8,128)(2,1)S(1)} %fusion.8), channel_id=1, source_target_pairs={{0,2},{1,3},{2,0},{3,1},{4,6},{5,7},{6,4},{7,5},{8,10},{9,11},{10,... | collective-permute-start | bytes 196616 | tf_op jit(solution)/shard_map/ppermute | solution.py:183
  9.7 0.6 collective-permute-start.2
  10.3 8.4 %all-to-all-start = ((bf16[32,16,2048]{2,1,0:T(8,128)(2,1)}), bf16[32,16,2048]{2,1,0:T(8,128)(2,1)}, u32[]{:S(2)}, u32[]{:S(2)}) async-start(bf16[32,16,2048]{2,1,0:T(8,128)(2,1)} %reshape.142), calls=%async_computation | async-start | bytes 4194304 | tf_op jit(solution)/shard_map/all_to_all | solution.py:178
  18.9 0.1 broadcast_add_fusion.1
  19.0 0.1 add.198
  19.1 0.6 fusion.19
  19.7 0.1 add_add_fusion
  19.7 0.7 fusion.17
  20.4 0.1 broadcast_add_fusion
  20.5 0.1 add.212
  23.2 0.1 add.204
  23.2 17.7 %multiply_convert_fusion.1 = (bf16[512,1024]{1,0:T(8,128)(2,1)S(1)}, bf16[512,1024]{1,0:T(8,128)(2,1)S(1)}, bf16[512,1024]{1,0:T(8,128)(2,1)S(1)}, bf16[512,1024]{1,0:T(8,128)(2,1)S(1)}) fusion(f32[512]{0:T(512)S(1)} %select_multiply_fusion, s32[1024]{0:T(1024)S(1)} %iota_add_fusion, s32[512]{0:T(512)S(1)} %fusion.10, f32[512]{0:T(512)S(1)} %fusion.14, ...), kind=kLoop, calls=%fused_computation.21 | loop fusion | flops 18874368 | bytes 4210688 | tf_op jit(solution)/shard_map/convert
  40.9 1.8 %pad_maximum_fusion = (bf16[1024,1024]{1,0:T(8,128)(2,1)S(1)}, bf16[1024,1024]{1,0:T(8,128)(2,1)}) fusion(bf16[512,1024]{1,0:T(8,128)(2,1)S(1)} %get-tuple-element.59, bf16[512,1024]{1,0:T(8,128)(2,1)S(1)} %get-tuple-element.60, bf16[512,1024]{1,0:T(8,128)(2,1)S(1)} %get-tuple-element.56, bf16[512,1024]{1,0:T(8,128)(2,1)S(1)} %get-tuple-element.55), kind=kLoop, calls=%fused_computation.16 | loop fusion | flops 8388608 | bytes 8388608 | tf_op jit(solution)/shard_map/concatenate | solution.py:47
  42.7 0.1 pad_add_fusion.place
  42.8 0.1 select_select_fusion.3
  43.0 1.4 all-to-all-done
  44.3 1.1 constant_dynamic-slice_fusion.1
  45.4 0.2 copy.38
  45.6 0.2 copy.39
  45.8 0.4 maximum_bitcast_fusion
  46.2 0.3 copy.40
  46.5 1.1 copy.41
  47.6 8.5 %all-to-all-start.1 = ((bf16[8,16,2048]{2,1,0:T(8,128)(2,1)}), bf16[8,16,2048]{2,1,0:T(8,128)(2,1)S(1)}, u32[]{:S(2)}, u32[]{:S(2)}) async-start(bf16[8,16,2048]{2,1,0:T(8,128)(2,1)} %copy.41), calls=%async_computation.1 | async-start | bytes 1048576 | tf_op jit(solution)/shard_map/all_to_all | solution.py:207
  59.9 13.8 %all-to-all-done.1 = bf16[8,16,2048]{2,1,0:T(8,128)(2,1)S(1)} async-done(((bf16[8,16,2048]{2,1,0:T(8,128)(2,1)}), bf16[8,16,2048]{2,1,0:T(8,128)(2,1)S(1)}, u32[]{:S(2)}, u32[]{:S(2)}) %all-to-all-start.1) | async-done | bytes 524320 | tf_op jit(solution)/shard_map/all_to_all | solution.py:207
  73.8 14.3 %all_to_all.15.refs_0_ = bf16[8,16,2048]{2,1,0:T(8,128)(2,1)S(1)} all-to-all(bf16[8,16,2048]{2,1,0:T(8,128)(2,1)S(1)} %broadcast_in_dim.14), channel_id=1, replica_groups={{0,4,64,68,128,132,192,196},{8,12,72,76,136,140,200,204},{16,20,80,84,1..., dimensions={0} | all-to-all | bytes 1048576 | tf_op jit(solution)/shard_map/all_to_all | solution.py:213
  88.1 2.0 %collective-permute-start.3 = (bf16[8,16,2048]{2,1,0:T(8,128)(2,1)S(1)}, bf16[8,16,2048]{2,1,0:T(8,128)(2,1)S(1)}, u32[]{:S(2)}, u32[]{:S(2)}) collective-permute-start(bf16[8,16,2048]{2,1,0:T(8,128)(2,1)S(1)} %all_to_all.15.refs_0_), channel_id=1, source_target_pairs={{0,8},{4,12},{8,16},{12,20},{16,24},{20,28},{24,32},{28,36},{32,40... | collective-permute-start | bytes 1572872 | tf_op jit(solution)/shard_map/ppermute | solution.py:26
  90.1 11.2 %collective-permute-done.5.refs_2_ = bf16[8,16,2048]{2,1,0:T(8,128)(2,1)S(1)} collective-permute-done((bf16[8,16,2048]{2,1,0:T(8,128)(2,1)S(1)}, bf16[8,16,2048]{2,1,0:T(8,128)(2,1)S(1)}, u32[]{:S(2)}, u32[]{:S(2)}) %collective-permute-start.5) | collective-permute-done | bytes 524320 | tf_op jit(solution)/shard_map/ppermute | solution.py:26
  101.4 1.5 %collective-permute-start.6 = (bf16[8,16,2048]{2,1,0:T(8,128)(2,1)S(1)}, bf16[8,16,2048]{2,1,0:T(8,128)(2,1)S(1)}, u32[]{:S(2)}, u32[]{:S(2)}) collective-permute-start(bf16[8,16,2048]{2,1,0:T(8,128)(2,1)S(1)} %collective-permute-done.5.refs_2_), channel_id=1, source_target_pairs={{0,56},{4,60},{8,0},{12,4},{16,8},{20,12},{24,16},{28,20},{32,24},... | collective-permute-start | bytes 1572872 | tf_op jit(solution)/shard_map/ppermute | solution.py:26
  102.9 0.5 collective-permute-start.4
  103.4 1.6 %copy-done = bf16[1024,1024]{1,0:T(8,128)(2,1)S(1)} copy-done((bf16[1024,1024]{1,0:T(8,128)(2,1)S(1)}, bf16[1024,1024]{1,0:T(8,128)(2,1)}, u32[]{:S(2)}) %copy-start) | copy-done | bytes 2097176
  105.0 7.8 %lags_a.1.refs_6_ = bf16[1024,2048]{1,0:T(8,128)(2,1)} custom-call(s32[64]{0:T(128)S(1)} %pad_add_fusion.place, bf16[8,16,2048]{2,1,0:T(8,128)(2,1)S(1)} %all_to_all.15.refs_0_, bf16[8,16,2048]{2,1,0:T(8,128)(2,1)S(1)} %collective-permute-done.3.refs_1_, bf16[8,16,2048]{2,1,0:T(8,128)(2,1)S(1)} %collective-permute-done.5.refs_2_, ...), custom_call_target="tpu_custom_call" | custom-call | flops 4608000000 | bytes 6291456 | tf_op jit(solution)/shard_map/lags_a/pallas_call | solution.py:141
  112.8 0.9 collective-permute-done.6.refs_1_
  113.7 2.7 %collective-permute-done.4.refs_0_ = bf16[8,16,2048]{2,1,0:T(8,128)(2,1)S(1)} collective-permute-done((bf16[8,16,2048]{2,1,0:T(8,128)(2,1)S(1)}, bf16[8,16,2048]{2,1,0:T(8,128)(2,1)S(1)}, u32[]{:S(2)}, u32[]{:S(2)}) %collective-permute-start.4) | collective-permute-done | bytes 524320 | tf_op jit(solution)/shard_map/ppermute | solution.py:26
  116.5 3.2 %collective-permute-start.8 = (bf16[8,16,2048]{2,1,0:T(8,128)(2,1)S(1)}, bf16[8,16,2048]{2,1,0:T(8,128)(2,1)S(1)}, u32[]{:S(2)}, u32[]{:S(2)}) collective-permute-start(bf16[8,16,2048]{2,1,0:T(8,128)(2,1)S(1)} %collective-permute-done.6.refs_1_), channel_id=1, source_target_pairs={{0,56},{4,60},{8,0},{12,4},{16,8},{20,12},{24,16},{28,20},{32,24},... | collective-permute-start | bytes 1572872 | tf_op jit(solution)/shard_map/ppermute | solution.py:26
  119.7 5.9 %lags_b.1.refs_6_ = bf16[1024,2048]{1,0:T(8,128)(2,1)} custom-call(s32[64]{0:T(128)S(1)} %pad_add_fusion.place, bf16[8,16,2048]{2,1,0:T(8,128)(2,1)S(1)} %collective-permute-done.4.refs_0_, bf16[8,16,2048]{2,1,0:T(8,128)(2,1)S(1)} %collective-permute-done.6.refs_1_, ...), custom_call_target="tpu_custom_call", output_to_operand_aliasing={{}: (7, {})} | custom-call | flops 3072000000 | bytes 4194304 | tf_op jit(solution)/shard_map/lags_b/pallas_call | solution.py:141
  125.6 3.5 %collective-permute-done.7.refs_0_ = bf16[8,16,2048]{2,1,0:T(8,128)(2,1)S(1)} collective-permute-done((bf16[8,16,2048]{2,1,0:T(8,128)(2,1)S(1)}, bf16[8,16,2048]{2,1,0:T(8,128)(2,1)S(1)}, u32[]{:S(2)}, u32[]{:S(2)}) %collective-permute-start.7) | collective-permute-done | bytes 524320 | tf_op jit(solution)/shard_map/ppermute | solution.py:26
  129.2 0.1 collective-permute-start.9
  129.3 3.2 %collective-permute-start.10 = (bf16[4,16,2048]{2,1,0:T(8,128)(2,1)S(1)}, bf16[4,16,2048]{2,1,0:T(8,128)(2,1)S(1)}, u32[]{:S(2)}, u32[]{:S(2)}) collective-permute-start(bf16[4,16,2048]{2,1,0:T(8,128)(2,1)S(1)} %slice.47), channel_id=1, source_target_pairs={{0,56},{4,60},{8,0},{12,4},{16,8},{20,12},{24,16},{28,20},{32,24},... | collective-permute-start | bytes 786440 | tf_op jit(solution)/shard_map/ppermute | solution.py:26
  132.5 5.9 %lags_c.1.refs_6_ = bf16[1024,2048]{1,0:T(8,128)(2,1)} custom-call(s32[64]{0:T(128)S(1)} %pad_add_fusion.place, bf16[8,16,2048]{2,1,0:T(8,128)(2,1)S(1)} %collective-permute-done.7.refs_0_, bf16[8,16,2048]{2,1,0:T(8,128)(2,1)S(1)} %collective-permute-done.8.refs_1_, ...), custom_call_target="tpu_custom_call", output_to_operand_aliasing={{}: (7, {})} | custom-call | flops 3072000000 | bytes 4194304 | tf_op jit(solution)/shard_map/lags_c/pallas_call | solution.py:141
  138.5 3.8 %lags_d.1 = bf16[1024,2048]{1,0:T(8,128)(2,1)} custom-call(s32[64]{0:T(128)S(1)} %pad_add_fusion.place, bf16[4,16,2048]{2,1,0:T(8,128)(2,1)S(1)} %collective-permute-done.9.refs_0_, bf16[4,16,2048]{2,1,0:T(8,128)(2,1)S(1)} %collective-permute-done.10.refs_1_, f32[8,8,2048]{2,1,0:T(8,128)S(1)} %maximum_convert_fusion.refs_3_.refs_2_, ...), custom_call_target="tpu_custom_call", output_to_operand_aliasing={{}: (7, {})} | custom-call | flops 1536000000 | bytes 2097152 | tf_op jit(solution)/shard_map/lags_d/pallas_call | solution.py:141
  (36 shorter events, 0.3 us)
Async XLA Ops:
  5.2 2.2 %copy-start.1 = (bf16[8,2,2048]{2,1,0:T(2,128)(2,1)S(1)}, bf16[8,2,2048]{2,1,0:T(2,128)(2,1)}, u32[]{:S(2)}) copy-start(bf16[8,2,2048]{2,1,0:T(2,128)(2,1)} %param.7) | copy-start | bytes 196612
  7.5 11.4 %copy-start.3 = (s32[7]{0:T(128)S(1)}, s32[7]{0:T(128)}, u32[]{:S(2)}) copy-start(s32[7]{0:T(128)} %constant.178) | copy-start | bytes 88
  7.5 11.6 %copy-start.2 = (s32[2]{0:T(128)S(1)}, s32[2]{0:T(128)}, u32[]{:S(2)}) copy-start(s32[2]{0:T(128)} %param.8) | copy-start | bytes 28
  7.5 35.3 %collective-permute-start.1 = (bf16[2,8,2048]{2,1,0:T(8,128)(2,1)S(1)}, bf16[2,8,2048]{2,1,0:T(8,128)(2,1)S(1)}, u32[]{:S(2)}, u32[]{:S(2)}) collective-permute-start(bf16[2,8,2048]{2,1,0:T(8,128)(2,1)S(1)} %fusion.8), channel_id=1, source_target_pairs={{0,2},{1,3},{2,0},{3,1},{4,6},{5,7},{6,4},{7,5},{8,10},{9,11},{10,... | collective-permute-start | bytes 196616 | tf_op jit(solution)/shard_map/ppermute | solution.py:183
  9.7 33.1 %collective-permute-start.2 = (bf16[2,8,2048]{2,1,0:T(8,128)(2,1)S(1)}, bf16[2,8,2048]{2,1,0:T(8,128)(2,1)S(1)}, u32[]{:S(2)}, u32[]{:S(2)}) collective-permute-start(bf16[2,8,2048]{2,1,0:T(8,128)(2,1)S(1)} %fusion.8), channel_id=1, source_target_pairs={{0,3},{1,0},{2,1},{3,2},{4,7},{5,4},{6,5},{7,6},{8,11},{9,8},{10,9... | collective-permute-start | bytes 196616 | tf_op jit(solution)/shard_map/ppermute | solution.py:183
  10.3 32.5 %collective-permute-start = (bf16[2,8,2048]{2,1,0:T(8,128)(2,1)S(1)}, bf16[2,8,2048]{2,1,0:T(8,128)(2,1)S(1)}, u32[]{:S(2)}, u32[]{:S(2)}) collective-permute-start(bf16[2,8,2048]{2,1,0:T(8,128)(2,1)S(1)} %fusion.8), channel_id=1, source_target_pairs={{0,1},{1,2},{2,3},{3,0},{4,5},{5,6},{6,7},{7,4},{8,9},{9,10},{10,1... | collective-permute-start | bytes 196616 | tf_op jit(solution)/shard_map/ppermute | solution.py:183
  10.3 34.0 %all-to-all-start = ((bf16[32,16,2048]{2,1,0:T(8,128)(2,1)}), bf16[32,16,2048]{2,1,0:T(8,128)(2,1)}, u32[]{:S(2)}, u32[]{:S(2)}) async-start(bf16[32,16,2048]{2,1,0:T(8,128)(2,1)} %reshape.142), calls=%async_computation | async-start | bytes 4194304 | tf_op jit(solution)/shard_map/all_to_all | solution.py:178
  47.6 26.2 %all-to-all-start.1 = ((bf16[8,16,2048]{2,1,0:T(8,128)(2,1)}), bf16[8,16,2048]{2,1,0:T(8,128)(2,1)S(1)}, u32[]{:S(2)}, u32[]{:S(2)}) async-start(bf16[8,16,2048]{2,1,0:T(8,128)(2,1)} %copy.41), calls=%async_computation.1 | async-start | bytes 1048576 | tf_op jit(solution)/shard_map/all_to_all | solution.py:207
  88.1 13.3 %collective-permute-start.5 = (bf16[8,16,2048]{2,1,0:T(8,128)(2,1)S(1)}, bf16[8,16,2048]{2,1,0:T(8,128)(2,1)S(1)}, u32[]{:S(2)}, u32[]{:S(2)}) collective-permute-start(bf16[8,16,2048]{2,1,0:T(8,128)(2,1)S(1)} %all_to_all.15.refs_0_), channel_id=1, source_target_pairs={{0,56},{4,60},{8,0},{12,4},{16,8},{20,12},{24,16},{28,20},{32,24},... | collective-permute-start | bytes 1572872 | tf_op jit(solution)/shard_map/ppermute | solution.py:26
  88.1 14.8 %collective-permute-start.3 = (bf16[8,16,2048]{2,1,0:T(8,128)(2,1)S(1)}, bf16[8,16,2048]{2,1,0:T(8,128)(2,1)S(1)}, u32[]{:S(2)}, u32[]{:S(2)}) collective-permute-start(bf16[8,16,2048]{2,1,0:T(8,128)(2,1)S(1)} %all_to_all.15.refs_0_), channel_id=1, source_target_pairs={{0,8},{4,12},{8,16},{12,20},{16,24},{20,28},{24,32},{28,36},{32,40... | collective-permute-start | bytes 1572872 | tf_op jit(solution)/shard_map/ppermute | solution.py:26
  101.4 12.4 %collective-permute-start.6 = (bf16[8,16,2048]{2,1,0:T(8,128)(2,1)S(1)}, bf16[8,16,2048]{2,1,0:T(8,128)(2,1)S(1)}, u32[]{:S(2)}, u32[]{:S(2)}) collective-permute-start(bf16[8,16,2048]{2,1,0:T(8,128)(2,1)S(1)} %collective-permute-done.5.refs_2_), channel_id=1, source_target_pairs={{0,56},{4,60},{8,0},{12,4},{16,8},{20,12},{24,16},{28,20},{32,24},... | collective-permute-start | bytes 1572872 | tf_op jit(solution)/shard_map/ppermute | solution.py:26
  102.9 13.6 %collective-permute-start.4 = (bf16[8,16,2048]{2,1,0:T(8,128)(2,1)S(1)}, bf16[8,16,2048]{2,1,0:T(8,128)(2,1)S(1)}, u32[]{:S(2)}, u32[]{:S(2)}) collective-permute-start(bf16[8,16,2048]{2,1,0:T(8,128)(2,1)S(1)} %collective-permute-done.3.refs_1_), channel_id=1, source_target_pairs={{0,8},{4,12},{8,16},{12,20},{16,24},{20,28},{24,32},{28,36},{32,40... | collective-permute-start | bytes 1572872 | tf_op jit(solution)/shard_map/ppermute | solution.py:26
  103.4 1.6 %copy-start = (bf16[1024,1024]{1,0:T(8,128)(2,1)S(1)}, bf16[1024,1024]{1,0:T(8,128)(2,1)}, u32[]{:S(2)}) copy-start(bf16[1024,1024]{1,0:T(8,128)(2,1)} %get-tuple-element.37.refs_6_.refs_5_) | copy-start | bytes 6291460
  116.5 12.7 %collective-permute-start.7 = (bf16[8,16,2048]{2,1,0:T(8,128)(2,1)S(1)}, bf16[8,16,2048]{2,1,0:T(8,128)(2,1)S(1)}, u32[]{:S(2)}, u32[]{:S(2)}) collective-permute-start(bf16[8,16,2048]{2,1,0:T(8,128)(2,1)S(1)} %collective-permute-done.4.refs_0_), channel_id=1, source_target_pairs={{0,8},{4,12},{8,16},{12,20},{16,24},{20,28},{24,32},{28,36},{32,40... | collective-permute-start | bytes 1572872 | tf_op jit(solution)/shard_map/ppermute | solution.py:26
  116.5 12.7 %collective-permute-start.8 = (bf16[8,16,2048]{2,1,0:T(8,128)(2,1)S(1)}, bf16[8,16,2048]{2,1,0:T(8,128)(2,1)S(1)}, u32[]{:S(2)}, u32[]{:S(2)}) collective-permute-start(bf16[8,16,2048]{2,1,0:T(8,128)(2,1)S(1)} %collective-permute-done.6.refs_1_), channel_id=1, source_target_pairs={{0,56},{4,60},{8,0},{12,4},{16,8},{20,12},{24,16},{28,20},{32,24},... | collective-permute-start | bytes 1572872 | tf_op jit(solution)/shard_map/ppermute | solution.py:26
  129.2 9.3 %collective-permute-start.9 = (bf16[4,16,2048]{2,1,0:T(8,128)(2,1)S(1)}, bf16[4,16,2048]{2,1,0:T(8,128)(2,1)S(1)}, u32[]{:S(2)}, u32[]{:S(2)}) collective-permute-start(bf16[4,16,2048]{2,1,0:T(8,128)(2,1)S(1)} %slice.46), channel_id=1, source_target_pairs={{0,8},{4,12},{8,16},{12,20},{16,24},{20,28},{24,32},{28,36},{32,40... | collective-permute-start | bytes 786440 | tf_op jit(solution)/shard_map/ppermute | solution.py:26
  129.3 9.2 %collective-permute-start.10 = (bf16[4,16,2048]{2,1,0:T(8,128)(2,1)S(1)}, bf16[4,16,2048]{2,1,0:T(8,128)(2,1)S(1)}, u32[]{:S(2)}, u32[]{:S(2)}) collective-permute-start(bf16[4,16,2048]{2,1,0:T(8,128)(2,1)S(1)} %slice.47), channel_id=1, source_target_pairs={{0,56},{4,60},{8,0},{12,4},{16,8},{20,12},{24,16},{28,20},{32,24},... | collective-permute-start | bytes 786440 | tf_op jit(solution)/shard_map/ppermute | solution.py:26

commit v3 on v2

--- a/solution.py
+++ b/solution.py
@@ -85,27 +85,86 @@
         lax.fori_loop(0, piece.shape[0] // 2, functools.partial(one_pair, step=step), 0)
 
 
-def lag_kernel(n_pieces, first_place, place, *refs):
-    pieces = refs[:n_pieces]
-    receivers, split, even_in, odd_in = refs[n_pieces : n_pieces + 4]
-    out, wide, cross, result, even, odd, table_sem, sem = refs[-8:]
-    tables = [
-        pltpu.make_async_copy(even_in, even, table_sem.at[0]),
-        pltpu.make_async_copy(odd_in, odd, table_sem.at[1]),
-    ]
-    for copy in tables:
+def fetch(refs, buffers, sems):
+    copies = [pltpu.make_async_copy(ref, buffer, sems.at[i]) for i, (ref, buffer) in enumerate(zip(refs, buffers))]
+    for copy in copies:
         copy.start()
-    freqs = even.shape[1]
-    pair = 2 * receivers.shape[1]
+    return copies
+
+
+def in_hbm(array):
+    return pltpu.with_memory_space_constraint(array, pltpu.HBM)
+
+
+def buffers_of(arrays):
+    return [pltpu.VMEM(array.shape, array.dtype) for array in arrays] + [pltpu.SemaphoreType.DMA((len(arrays),))]
+
+
+def cross_kernel(*refs):
+    n = (len(refs) - 7) // 2
+    sources, out = refs[: n + 1], refs[n + 1]
+    buffers, (sems, cross, wide, sem) = refs[n + 2 : 2 * n + 3], refs[2 * n + 3 :]
+    copies = fetch(sources, buffers, sems)
+    copies[0].wait()
+    receivers, pieces = buffers[0], buffers[1:]
     at = 0
-    for piece in pieces:
+    for piece, copy in zip(pieces, copies[1:]):
+        copy.wait()
         add_cross(piece, receivers, wide, cross, at)
         at += piece.shape[0] * piece.shape[1] // (2 * receivers.shape[0])
-    for copy in tables:
+    copy = pltpu.make_async_copy(cross, out, sem)
+    copy.start()
+    copy.wait()
+
+
+def cross_rows(pieces, receivers):
+    return sum(piece.shape[0] * piece.shape[1] for piece in pieces) * receivers.shape[1] // receivers.shape[0]
+
+
+def cross_of(name, pieces, receivers):
+    windows, r, width = receivers.shape
+    rows = cross_rows(pieces, receivers)
+    anywhere = pl.BlockSpec(memory_space=pl.ANY)
+    inputs = (in_hbm(receivers), *pieces)
+    return pl.pallas_call(
+        cross_kernel,
+        out_shape=pltpu.HBM((rows, width), BF16),
+        in_specs=[anywhere] * len(inputs),
+        out_specs=anywhere,
+        scratch_shapes=buffers_of(inputs)
+        + [pltpu.VMEM((rows, width), BF16), pltpu.VMEM((2, windows, width), F32), pltpu.SemaphoreType.DMA],
+        compiler_params=pltpu.CompilerParams(vmem_limit_bytes=8 * 1024 * 1024),
+        cost_estimate=pl.CostEstimate(flops=rows * 10**6, bytes_accessed=rows * 2**10, transcendentals=0),
+        name=name,
+    )(*inputs)
+
+
+def lag_kernel(n_done, n_pieces, first_place, aliased, place, *refs):
+    n = n_done + n_pieces + 4
+    sources, refs = refs[:n], refs[n + aliased :]
+    out, buffers, (sems, wide, cross, result, sem) = refs[0], refs[1 : n + 1], refs[n + 1 :]
+    receivers, pieces, split = buffers[0], buffers[1 : 1 + n_pieces], buffers[1 + n_pieces + n_done]
+    even, odd = buffers[-2:]
+    spans = []
+    at = 0
+    pair = 2 * receivers.shape[1]
+    for part in buffers[1 + n_pieces : 1 + n_pieces + n_done]:
+        spans.append(cross.at[pl.ds(at * pair, part.shape[0])])
+        at += part.shape[0] // pair
+    targets = list(buffers)
+    targets[1 + n_pieces : 1 + n_pieces + n_done] = spans
+    copies = fetch(sources, targets, sems)
+    copies[0].wait()
+    for piece, copy in zip(pieces, copies[1:]):
         copy.wait()
+        add_cross(piece, receivers, wide, cross, at)
+        at += piece.shape[0] * piece.shape[1] // (2 * receivers.shape[0])
+    for copy in copies[1 + n_pieces :]:
+        copy.wait()
+    freqs = even.shape[1]
     block = split.shape[0]
     total = at * pair
-    chunk = 256 if total % 256 == 0 else 192 if total % 192 == 0 else total
+    chunk = 192 if total % 192 == 0 else 256
     copies = []
     for first in range(0, total, chunk):
         rows = pl.ds(first, chunk)
@@ -131,32 +190,28 @@
         copy.wait()
 
 
-def lags_of(name, place, first_place, pieces, receivers, split, even, odd, out_rows, *result):
+def lags_of(name, place, first_place, done, pieces, receivers, split, even, odd, out_rows, *result):
     windows, r, width = receivers.shape
-    rows = sum(piece.shape[0] * piece.shape[1] for piece in pieces) * r // windows
-    whole = pl.BlockSpec(memory_space=pltpu.VMEM)
+    rows = cross_rows(pieces, receivers) + sum(part.shape[0] for part in done)
     anywhere = pl.BlockSpec(memory_space=pl.ANY)
-    in_hbm = pl.BlockSpec(memory_space=pltpu.HBM)
-    held = len(pieces)
+    inputs = (in_hbm(receivers), *pieces, *map(in_hbm, (*done, split, even, odd)))
     return pl.pallas_call(
-        functools.partial(lag_kernel, len(pieces), first_place),
-        out_shape=jax.ShapeDtypeStruct((out_rows, width), BF16),
-        in_specs=[pl.BlockSpec(memory_space=pltpu.SMEM)] + [whole] * (held + 2) + [in_hbm] * 2 + [anywhere] * len(result),
+        functools.partial(lag_kernel, len(done), len(pieces), first_place, len(result)),
+        out_shape=pltpu.HBM((out_rows, width), BF16),
+        in_specs=[pl.BlockSpec(memory_space=pltpu.SMEM)] + [anywhere] * (len(inputs) + len(result)),
         out_specs=anywhere,
-        scratch_shapes=[
+        scratch_shapes=buffers_of(inputs)
+        + [
             pltpu.VMEM((2, windows, width), F32),
             pltpu.VMEM((rows, width), BF16),
             pltpu.VMEM((rows, width), BF16),
-            pltpu.VMEM(even.shape, BF16),
-            pltpu.VMEM(odd.shape, BF16),
-            pltpu.SemaphoreType.DMA((2,)),
             pltpu.SemaphoreType.DMA((rows // (2 * r),)),
         ],
-        input_output_aliases={held + 5: 0} if result else {},
-        compiler_params=pltpu.CompilerParams(vmem_limit_bytes=16 * 1024 * 1024),
-        cost_estimate=pl.CostEstimate(flops=rows * 12 * 10**6, bytes_accessed=rows * 2**14, transcendentals=0),
+        input_output_aliases={len(inputs) + 1: 0} if result else {},
+        compiler_params=pltpu.CompilerParams(vmem_limit_bytes=24 * 1024 * 1024),
+        cost_estimate=pl.CostEstimate(flops=rows * 12 * 10**6, bytes_accessed=rows * 2**10, transcendentals=0),
         name=name,
-    )(place, *pieces, receivers, split, even, odd, *result)
+    )(place, *inputs, *result)
 
 
 def on_device(source_spectra, receiver_spectra, block_order, source_mask, receiver_mask):
@@ -174,7 +229,6 @@
     owned = source_spectra[0] * source_mask[0][:, None, None].astype(BF16)
     rows = owned.reshape(wins, NY, NZ, NX, own_windows, width).transpose(1, 3, 0, 2, 4, 5)
     rows = rows.reshape(NY * NX * wins, NZ * own_windows, width)
-    rows, receiver_spectra = lax.optimization_barrier((rows, receiver_spectra))
     spread = lax.all_to_all(rows, ("chan", "win"), 0, 0, tiled=True, axis_index_groups=yx_win_groups(wins))
 
     def all_windows(give):
@@ -186,20 +240,16 @@
     split = split_matrix(256)
     even = half_table(freqs, 0)
     odd = half_table(freqs, 1)
-    receivers = receiver_spectra * receiver_mask[:, None, None].astype(BF16)
-    receivers = all_windows(lambda to: receivers.transpose(1, 0, 2)).astype(F32)
-
     ys = jnp.arange(NY, dtype=jnp.int32)
-    zs = jnp.mod(z - jnp.array((0, 1, -1, 2, -2, 3, -3), jnp.int32), NZ)
+    zs = jnp.mod(z - jnp.array((0, 1, -1, 4, 2, -2, 3, -3), jnp.int32), NZ)
     bases = (jnp.arange(steps, dtype=jnp.int32)[:, None] * (NY * NZ) + (ys * NZ)[None, :]).reshape(1, -1)
-    last = (bases + jnp.mod(z + NZ // 2, NZ)).reshape(steps, 2, NY // 2).transpose(1, 0, 2)
-    place = jnp.concatenate([(bases + zs[:, None]).reshape(-1), last.reshape(-1)])
+    place = (bases + zs[:, None]).reshape(-1)
     owner_y, owner_z, owner_x = block_order // (NZ * NX), (block_order // NX) % NZ, block_order % NX
     first_from = [(owner_y[t] * NX + owner_x[t]) * wins for t in range(steps)]
     owner_z = [owner_z[t] for t in range(steps)]
-    shadow = (receivers, split, even, odd, place, first_from, owner_z)
+    shadow = (split, even, odd, place, first_from, owner_z)
     spread, shadow = lax.optimization_barrier((spread, shadow))
-    receivers, split, even, odd, place, first_from, owner_z = shadow
+    split, even, odd, place, first_from, owner_z = shadow
 
     chosen = [lax.dynamic_slice_in_dim(spread, first_from[t], wins, 0) for t in range(steps)]
     chosen = jnp.stack([part.reshape(wins, NZ, own_windows, width) for part in chosen])
@@ -212,22 +262,28 @@
         copies = jnp.broadcast_to(value[None], (NY * NX,) + value.shape)
         return lax.all_to_all(copies, "chan", 0, 0, tiled=True, axis_index_groups=yx_groups())
 
+    receivers = receiver_spectra * receiver_mask[:, None, None].astype(BF16)
+    receivers = all_windows(lambda to: receivers.transpose(1, 0, 2)).astype(F32)
+
+    chosen, receivers = lax.optimization_barrier((chosen, receivers))
+
     near = gather_yx(chosen)
-
+    opposite = shift(chosen, dz=4)
+    near, opposite = lax.optimization_barrier((near, opposite))
     tables = (receivers, split, even, odd, steps * chans * r)
+    pairs = steps * NY
     up, down = shift(near, dz=1), shift(near, dz=-1)
+    cross_near = cross_of("cross_near", (near,), receivers)
+    opposite, cross_near = lax.optimization_barrier((opposite, cross_near))
+    far = gather_yx(opposite)
+    up, down, cross_near = lax.optimization_barrier((up, down, cross_near))
     up2, down2 = shift(up, dz=1), shift(down, dz=-1)
-    pairs = steps * NY
-    half = near.shape[0] // 2
-    out = lags_of("lags_a", place, 0, (near, up, down), *tables)
+    out = lags_of("lags_1", place, 0, (cross_near,), (up, down, far), *tables)
     up2, down2, out = lax.optimization_barrier((up2, down2, out))
     up3, down3 = shift(up2, dz=1), shift(down2, dz=-1)
-    out = lags_of("lags_b", place, 3 * pairs, (up2, down2), *tables, out)
+    out = lags_of("lags_2", place, 4 * pairs, (), (up2, down2), *tables, out)
     up3, down3, out = lax.optimization_barrier((up3, down3, out))
-    up4, down4 = shift(up3[:half], dz=1), shift(down3[half:], dz=-1)
-    out = lags_of("lags_c", place, 5 * pairs, (up3, down3), *tables, out)
-    up4, down4, out = lax.optimization_barrier((up4, down4, out))
-    out = lags_of("lags_d", place, 7 * pairs, (up4, down4), *tables, out)
+    out = lags_of("lags_3", place, 6 * pairs, (), (up3, down3), *tables, out)
     return out.reshape(steps, chans, r, width)
 
 

time: 143 us -> 135 us (0.944)
  blocking collectives: 14.3 us -> 0 us
  starting transfers between devices: 30.3 us -> 40.3 us
  waiting for transfers between devices: 33.6 us -> 26.4 us
  Pallas kernels: 23.5 us -> 26 us
    all_to_all x1 -> x0, blocking collectives: 14.3 us -> none  [gather_yx(): lax.all_to_all(copies, 'chan', 0, 0, tiled=True, axis_index_groups=yx_gro...]
    all_to_all x0 -> x2, starting transfers between devices: none -> 12.4 us  [gather_yx(): lax.all_to_all(copies, 'chan', 0, 0, tiled=True, axis_index_groups=yx_gro...]
    all_to_all x1, waiting for transfers between devices: 13.8 us -> 5.24 us  [on_device(): lax.all_to_all(chosen, 'chan', 0, 0, tiled=True, axis_index_groups=z_grou...]
    ppermute x3, waiting for transfers between devices: 0.01 us -> 5.22 us  [all_windows(): lax.ppermute(give(jnp.mod(win + j, wins)), 'win', [(w, (w + j) % wins) fo...]
    ppermute x8 -> x7, waiting for transfers between devices: 18.4 us -> 15 us  [shift(): return lax.ppermute(value, 'chan', pairs)]
    pallas_call x4, Pallas kernels: 23.5 us -> 26 us  [the longest x3 22.9 us: lags_of(): pl.pallas_call(functools.partial(lag_kernel, len(done), len(pieces), firs...]
    broadcast_in_dim x1 -> x2, local copies, waits for them, and re-layouts: 0.04 us -> 1.69 us  [gather_yx(): copies = jnp.broadcast_to(value[None], (NY * NX,) + value.shape)]
    ppermute x8 -> x7, starting transfers between devices: 10.6 us -> 9.02 us  [shift(): return lax.ppermute(value, 'chan', pairs)]
  transfers between devices with their start and end apart: 13 -> 14, of which waited for: 6 -> 10; matrix products, arithmetic and copies ran while one was open for 15% -> 18% of each run, Pallas kernels for 14% -> 14%
where the time goes in v3:
time: 135 us; the launch traced here: 134 us
  starting transfers between devices  40.3 us (30%)
  other arithmetic  26.7 us (20%)
  waiting for transfers between devices  26.4 us (20%)
  Pallas kernels  26 us (19%)
  local copies, waits for them, and re-layouts  8.48 us (6%)
  between operations  6.42 us (5%)
    pallas_call x3, Pallas kernels, lags_of(): pl.pallas_call(functools.partial(lag_kernel, len(done), len(pieces), firs...  22.9 us
    another operation x1, other arithmetic  17.7 us
    ppermute x7, waiting for transfers between devices, shift(): return lax.ppermute(value, 'chan', pairs)  15 us
    all_to_all x2, starting transfers between devices, gather_yx(): lax.all_to_all(copies, 'chan', 0, 0, tiled=True, axis_index_groups=yx_gro...  12.4 us
    ppermute x7, starting transfers between devices, shift(): return lax.ppermute(value, 'chan', pairs)  9.02 us
    all_to_all x1, starting transfers between devices, on_device(): lax.all_to_all(chosen, 'chan', 0, 0, tiled=True, axis_index_groups=z_grou...  8.47 us
    all_to_all x1, starting transfers between devices, on_device(): lax.all_to_all(rows, ('chan', 'win'), 0, 0, tiled=True, axis_index_groups...  7.7 us
    all_to_all x1, waiting for transfers between devices, on_device(): lax.all_to_all(chosen, 'chan', 0, 0, tiled=True, axis_index_groups=z_grou...  5.24 us
  transfers between devices with their start and end apart: 14, of which 10 were waited for; matrix products, arithmetic and copies ran while one was open for 18% of the time, Pallas kernels for 14%

profile of v3, /device:TPU:10, one launch (start us, length us, event | category | flops | bytes accessed | tf_op | source)
XLA Modules:
  0.0 134.2 jit_solution(9060531759241621186)
XLA Ops:
  0.0 0.7 convert_reduce_fusion
  0.7 0.2 convert_element_type.34
  0.9 0.2 copy.34
  1.0 3.5 %fusion.6 = bf16[4,2,4,8,2,2048]{5,4,3,2,1,0:T(2,128)(2,1)S(1)} fusion(bf16[4,4,8,2,2,2048]{5,4,3,2,1,0:T(2,128)(2,1)} %bitcast.21, bf16[4,4,8,2]{2,0,3,1:T(4,128)(2,1)S(1)} %copy.34), kind=kLoop, calls=%fused_computation.19 | loop fusion | flops 1048576 | bytes 4194816 | tf_op jit(solution)/shard_map/transpose | solution.py:230
  4.5 2.2 %reshape.118 = bf16[32,16,2048]{2,1,0:T(8,128)(2,1)} reshape(bf16[4,2,4,8,2,2048]{5,4,3,2,1,0:T(2,128)(2,1)S(1)} %fusion.6) | data formatting | bytes 4194304 | tf_op jit(solution)/shard_map/reshape | solution.py:231
  6.7 7.7 %all-to-all-start = ((bf16[32,16,2048]{2,1,0:T(8,128)(2,1)}), bf16[32,16,2048]{2,1,0:T(8,128)(2,1)}, u32[]{:S(2)}, u32[]{:S(2)}) async-start(bf16[32,16,2048]{2,1,0:T(8,128)(2,1)} %reshape.118), calls=%async_computation | async-start | bytes 4194304 | tf_op jit(solution)/shard_map/all_to_all | solution.py:232
  14.6 0.1 add.161
  14.7 0.6 fusion.17
  15.4 0.6 fusion.19
  18.5 0.1 add.167.place
  18.7 17.7 %multiply_convert_fusion.1 = (bf16[512,1024]{1,0:T(8,128)(2,1)S(1)}, bf16[512,1024]{1,0:T(8,128)(2,1)S(1)}, bf16[512,1024]{1,0:T(8,128)(2,1)S(1)}, bf16[512,1024]{1,0:T(8,128)(2,1)S(1)}) fusion(f32[512]{0:T(512)S(1)} %select_multiply_fusion, s32[1024]{0:T(1024)S(1)} %iota_add_fusion, s32[512]{0:T(512)S(1)} %fusion.10, f32[512]{0:T(512)S(1)} %fusion.14, ...), kind=kLoop, calls=%fused_computation.21 | loop fusion | flops 18874368 | bytes 4210688 | tf_op jit(solution)/shard_map/convert
  36.4 2.5 %pad_maximum_fusion = (bf16[1024,1024]{1,0:T(8,128)(2,1)}, bf16[1024,1024]{1,0:T(8,128)(2,1)}) fusion(bf16[512,1024]{1,0:T(8,128)(2,1)S(1)} %get-tuple-element.65, bf16[512,1024]{1,0:T(8,128)(2,1)S(1)} %get-tuple-element.66, bf16[512,1024]{1,0:T(8,128)(2,1)S(1)} %get-tuple-element.62, bf16[512,1024]{1,0:T(8,128)(2,1)S(1)} %get-tuple-element.61), kind=kLoop, calls=%fused_computation.16 | loop fusion | flops 8388608 | bytes 8388608 | tf_op jit(solution)/shard_map/concatenate | solution.py:47
  38.8 0.7 fusion.7.refs_5_.refs_3_
  39.5 0.6 all-to-all-done
  40.1 1.1 constant_dynamic-slice_fusion.1
  41.1 0.2 copy.36
  41.3 0.2 copy.37
  41.6 0.4 maximum_bitcast_fusion
  41.9 0.3 copy.38
  42.2 1.1 copy.39
  43.3 8.5 %all-to-all-start.1 = ((bf16[8,16,2048]{2,1,0:T(8,128)(2,1)}), bf16[8,16,2048]{2,1,0:T(8,128)(2,1)S(1)}, u32[]{:S(2)}, u32[]{:S(2)}) async-start(bf16[8,16,2048]{2,1,0:T(8,128)(2,1)} %copy.39), calls=%async_computation.1 | async-start | bytes 1048576 | tf_op jit(solution)/shard_map/all_to_all | solution.py:257
  51.8 0.1 fusion.8
  51.9 1.6 %collective-permute-start.1 = (bf16[2,8,2048]{2,1,0:T(8,128)(2,1)S(1)}, bf16[2,8,2048]{2,1,0:T(8,128)(2,1)S(1)}, u32[]{:S(2)}, u32[]{:S(2)}) collective-permute-start(bf16[2,8,2048]{2,1,0:T(8,128)(2,1)S(1)} %fusion.8), channel_id=1, source_target_pairs={{0,2},{1,3},{2,0},{3,1},{4,6},{5,7},{6,4},{7,5},{8,10},{9,11},{10,... | collective-permute-start | bytes 196616 | tf_op jit(solution)/shard_map/ppermute | solution.py:237
  53.4 1.1 collective-permute-start.2
  54.6 3.1 %collective-permute-done.1 = bf16[2,8,2048]{2,1,0:T(8,128)(2,1)S(1)} collective-permute-done((bf16[2,8,2048]{2,1,0:T(8,128)(2,1)S(1)}, bf16[2,8,2048]{2,1,0:T(8,128)(2,1)S(1)}, u32[]{:S(2)}, u32[]{:S(2)}) %collective-permute-start.1) | collective-permute-done | bytes 65568 | tf_op jit(solution)/shard_map/ppermute | solution.py:237
  57.7 2.1 %collective-permute-done = bf16[2,8,2048]{2,1,0:T(8,128)(2,1)S(1)} collective-permute-done((bf16[2,8,2048]{2,1,0:T(8,128)(2,1)S(1)}, bf16[2,8,2048]{2,1,0:T(8,128)(2,1)S(1)}, u32[]{:S(2)}, u32[]{:S(2)}) %collective-permute-start) | collective-permute-done | bytes 65568 | tf_op jit(solution)/shard_map/ppermute | solution.py:237
  59.8 0.1 select_select_fusion.3
  59.9 0.9 maximum_convert_fusion.refs_0_
  64.3 5.2 %all-to-all-done.1 = bf16[8,16,2048]{2,1,0:T(8,128)(2,1)S(1)} async-done(((bf16[8,16,2048]{2,1,0:T(8,128)(2,1)}), bf16[8,16,2048]{2,1,0:T(8,128)(2,1)S(1)}, u32[]{:S(2)}, u32[]{:S(2)}) %all-to-all-start.1) | async-done | bytes 524320 | tf_op jit(solution)/shard_map/all_to_all | solution.py:257
  69.5 0.8 broadcast_in_dim.16
  70.4 6.7 %all-to-all-start.2 = ((bf16[8,16,2048]{2,1,0:T(8,128)(2,1)}), bf16[8,16,2048]{2,1,0:T(8,128)(2,1)S(1)}, u32[]{:S(2)}, u32[]{:S(2)}) async-start(bf16[8,16,2048]{2,1,0:T(8,128)(2,1)} %broadcast_in_dim.16), calls=%async_computation.2 | async-start | bytes 1048576 | tf_op jit(solution)/shard_map/all_to_all | solution.py:263
  77.1 0.5 collective-permute-start.3
  77.6 8.3 %collective-permute-done.3 = bf16[16,2048]{1,0:T(8,128)(2,1)S(1)} collective-permute-done((bf16[16,2048]{1,0:T(8,128)(2,1)S(1)}, bf16[16,2048]{1,0:T(8,128)(2,1)S(1)}, u32[]{:S(2)}, u32[]{:S(2)}) %collective-permute-start.3) | collective-permute-done | bytes 65568 | tf_op jit(solution)/shard_map/ppermute | solution.py:26
  85.9 2.0 %collective-permute-start.4 = (bf16[8,16,2048]{2,1,0:T(8,128)(2,1)S(1)}, bf16[8,16,2048]{2,1,0:T(8,128)(2,1)S(1)}, u32[]{:S(2)}, u32[]{:S(2)}) collective-permute-start(bf16[8,16,2048]{2,1,0:T(8,128)(2,1)S(1)} %all-to-all-done.2.refs_1_), channel_id=1, source_target_pairs={{0,8},{4,12},{8,16},{12,20},{16,24},{20,28},{24,32},{28,36},{32,40... | collective-permute-start | bytes 1572872 | tf_op jit(solution)/shard_map/ppermute | solution.py:26
  88.0 3.1 %cross_near.1.refs_4_ = bf16[128,2048]{1,0:T(8,128)(2,1)} custom-call(f32[8,8,2048]{2,1,0:T(8,128)} %maximum_convert_fusion.refs_0_, bf16[8,16,2048]{2,1,0:T(8,128)(2,1)S(1)} %all-to-all-done.2.refs_1_), custom_call_target="tpu_custom_call" | custom-call | flops 128000000 | bytes 131072 | tf_op jit(solution)/shard_map/cross_near/pallas_call | solution.py:129
  91.1 0.8 broadcast_in_dim.17
  91.9 5.7 %all-to-all-start.3 = ((bf16[8,16,2048]{2,1,0:T(8,128)(2,1)}), bf16[8,16,2048]{2,1,0:T(8,128)(2,1)S(1)}, u32[]{:S(2)}, u32[]{:S(2)}) async-start(bf16[8,16,2048]{2,1,0:T(8,128)(2,1)} %broadcast_in_dim.17), calls=%async_computation.3 | async-start | bytes 1048576 | tf_op jit(solution)/shard_map/all_to_all | solution.py:263
  97.6 1.8 %collective-permute-done.5.refs_2_ = bf16[8,16,2048]{2,1,0:T(8,128)(2,1)S(1)} collective-permute-done((bf16[8,16,2048]{2,1,0:T(8,128)(2,1)S(1)}, bf16[8,16,2048]{2,1,0:T(8,128)(2,1)S(1)}, u32[]{:S(2)}, u32[]{:S(2)}) %collective-permute-start.5) | collective-permute-done | bytes 524320 | tf_op jit(solution)/shard_map/ppermute | solution.py:26
  99.4 1.2 collective-permute-done.4.refs_1_
  100.6 0.5 collective-permute-start.6
  101.2 2.7 %collective-permute-start.7 = (bf16[8,16,2048]{2,1,0:T(8,128)(2,1)S(1)}, bf16[8,16,2048]{2,1,0:T(8,128)(2,1)S(1)}, u32[]{:S(2)}, u32[]{:S(2)}) collective-permute-start(bf16[8,16,2048]{2,1,0:T(8,128)(2,1)S(1)} %collective-permute-done.5.refs_2_), channel_id=1, source_target_pairs={{0,56},{4,60},{8,0},{12,4},{16,8},{20,12},{24,16},{28,20},{32,24},... | collective-permute-start | bytes 1572872 | tf_op jit(solution)/shard_map/ppermute | solution.py:26
  103.9 0.4 all-to-all-done.3.refs_3_
  104.3 9.5 %lags_1.1.refs_6_ = bf16[1024,2048]{1,0:T(8,128)(2,1)} custom-call(s32[64]{0:T(128)S(1)} %add.167.place, f32[8,8,2048]{2,1,0:T(8,128)} %maximum_convert_fusion.refs_0_, bf16[8,16,2048]{2,1,0:T(8,128)(2,1)S(1)} %collective-permute-done.4.refs_1_, bf16[8,16,2048]{2,1,0:T(8,128)(2,1)S(1)} %collective-permute-done.5.refs_2_, ...), custom_call_target="tpu_custom_call" | custom-call | flops 6144000000 | bytes 524288 | tf_op jit(solution)/shard_map/lags_1/pallas_call | solution.py:198
  113.7 0.7 collective-permute-done.6.refs_1_
  114.5 3.2 %collective-permute-start.9 = (bf16[8,16,2048]{2,1,0:T(8,128)(2,1)S(1)}, bf16[8,16,2048]{2,1,0:T(8,128)(2,1)S(1)}, u32[]{:S(2)}, u32[]{:S(2)}) collective-permute-start(bf16[8,16,2048]{2,1,0:T(8,128)(2,1)S(1)} %collective-permute-done.7.refs_2_), channel_id=1, source_target_pairs={{0,56},{4,60},{8,0},{12,4},{16,8},{20,12},{24,16},{28,20},{32,24},... | collective-permute-start | bytes 1572872 | tf_op jit(solution)/shard_map/ppermute | solution.py:26
  117.7 6.7 %lags_2.1.refs_6_ = bf16[1024,2048]{1,0:T(8,128)(2,1)} custom-call(s32[64]{0:T(128)S(1)} %add.167.place, f32[8,8,2048]{2,1,0:T(8,128)} %maximum_convert_fusion.refs_0_, bf16[8,16,2048]{2,1,0:T(8,128)(2,1)S(1)} %collective-permute-done.6.refs_1_, bf16[8,16,2048]{2,1,0:T(8,128)(2,1)S(1)} %collective-permute-done.7.refs_2_, ...), custom_call_target="tpu_custom_call", output_to_operand_aliasing={{}: (7, {})} | custom-call | flops 3072000000 | bytes 262144 | tf_op jit(solution)/shard_map/lags_2/pallas_call | solution.py:198
  124.4 2.9 %collective-permute-done.8.refs_1_ = bf16[8,16,2048]{2,1,0:T(8,128)(2,1)S(1)} collective-permute-done((bf16[8,16,2048]{2,1,0:T(8,128)(2,1)S(1)}, bf16[8,16,2048]{2,1,0:T(8,128)(2,1)S(1)}, u32[]{:S(2)}, u32[]{:S(2)}) %collective-permute-start.8) | collective-permute-done | bytes 524320 | tf_op jit(solution)/shard_map/ppermute | solution.py:26
  127.3 6.7 %lags_3.1 = bf16[1024,2048]{1,0:T(8,128)(2,1)} custom-call(s32[64]{0:T(128)S(1)} %add.167.place, f32[8,8,2048]{2,1,0:T(8,128)} %maximum_convert_fusion.refs_0_, bf16[8,16,2048]{2,1,0:T(8,128)(2,1)S(1)} %collective-permute-done.8.refs_1_, bf16[8,16,2048]{2,1,0:T(8,128)(2,1)S(1)} %collective-permute-done.9.refs_2_, ...), custom_call_target="tpu_custom_call", output_to_operand_aliasing={{}: (7, {})} | custom-call | flops 3072000000 | bytes 262144 | tf_op jit(solution)/shard_map/lags_3/pallas_call | solution.py:198
  (32 shorter events, 0.3 us)
Async XLA Ops:
  6.7 7.9 %copy-start.1 = (s32[2]{0:T(128)S(1)}, s32[2]{0:T(128)}, u32[]{:S(2)}) copy-start(s32[2]{0:T(128)} %param.8) | copy-start | bytes 28
  6.7 7.9 %copy-start.3 = (s32[8]{0:T(128)S(1)}, s32[8]{0:T(128)}, u32[]{:S(2)}) copy-start(s32[8]{0:T(128)} %constant.173) | copy-start | bytes 100
  6.7 9.3 %copy-start.2 = (s32[8]{0:T(128)S(1)}, s32[8]{0:T(128)}, u32[]{:S(2)}) copy-start(s32[8]{0:T(128)} %param.10) | copy-start | bytes 100
  6.7 33.3 %all-to-all-start = ((bf16[32,16,2048]{2,1,0:T(8,128)(2,1)}), bf16[32,16,2048]{2,1,0:T(8,128)(2,1)}, u32[]{:S(2)}, u32[]{:S(2)}) async-start(bf16[32,16,2048]{2,1,0:T(8,128)(2,1)} %reshape.118), calls=%async_computation | async-start | bytes 4194304 | tf_op jit(solution)/shard_map/all_to_all | solution.py:232
  41.6 10.2 %copy-start = (bf16[8,2,2048]{2,1,0:T(2,128)(2,1)S(1)}, bf16[8,2,2048]{2,1,0:T(2,128)(2,1)}, u32[]{:S(2)}) copy-start(bf16[8,2,2048]{2,1,0:T(2,128)(2,1)} %param.7) | copy-start | bytes 196612
  43.3 26.2 %all-to-all-start.1 = ((bf16[8,16,2048]{2,1,0:T(8,128)(2,1)}), bf16[8,16,2048]{2,1,0:T(8,128)(2,1)S(1)}, u32[]{:S(2)}, u32[]{:S(2)}) async-start(bf16[8,16,2048]{2,1,0:T(8,128)(2,1)} %copy.39), calls=%async_computation.1 | async-start | bytes 1048576 | tf_op jit(solution)/shard_map/all_to_all | solution.py:257
  51.9 5.8 %collective-permute-start.1 = (bf16[2,8,2048]{2,1,0:T(8,128)(2,1)S(1)}, bf16[2,8,2048]{2,1,0:T(8,128)(2,1)S(1)}, u32[]{:S(2)}, u32[]{:S(2)}) collective-permute-start(bf16[2,8,2048]{2,1,0:T(8,128)(2,1)S(1)} %fusion.8), channel_id=1, source_target_pairs={{0,2},{1,3},{2,0},{3,1},{4,6},{5,7},{6,4},{7,5},{8,10},{9,11},{10,... | collective-permute-start | bytes 196616 | tf_op jit(solution)/shard_map/ppermute | solution.py:237
  53.4 4.3 %collective-permute-start.2 = (bf16[2,8,2048]{2,1,0:T(8,128)(2,1)S(1)}, bf16[2,8,2048]{2,1,0:T(8,128)(2,1)S(1)}, u32[]{:S(2)}, u32[]{:S(2)}) collective-permute-start(bf16[2,8,2048]{2,1,0:T(8,128)(2,1)S(1)} %fusion.8), channel_id=1, source_target_pairs={{0,3},{1,0},{2,1},{3,2},{4,7},{5,4},{6,5},{7,6},{8,11},{9,8},{10,9... | collective-permute-start | bytes 196616 | tf_op jit(solution)/shard_map/ppermute | solution.py:237
  54.6 5.2 %collective-permute-start = (bf16[2,8,2048]{2,1,0:T(8,128)(2,1)S(1)}, bf16[2,8,2048]{2,1,0:T(8,128)(2,1)S(1)}, u32[]{:S(2)}, u32[]{:S(2)}) collective-permute-start(bf16[2,8,2048]{2,1,0:T(8,128)(2,1)S(1)} %fusion.8), channel_id=1, source_target_pairs={{0,1},{1,2},{2,3},{3,0},{4,5},{5,6},{6,7},{7,4},{8,9},{9,10},{10,1... | collective-permute-start | bytes 196616 | tf_op jit(solution)/shard_map/ppermute | solution.py:237
  70.4 15.6 %all-to-all-start.2 = ((bf16[8,16,2048]{2,1,0:T(8,128)(2,1)}), bf16[8,16,2048]{2,1,0:T(8,128)(2,1)S(1)}, u32[]{:S(2)}, u32[]{:S(2)}) async-start(bf16[8,16,2048]{2,1,0:T(8,128)(2,1)} %broadcast_in_dim.16), calls=%async_computation.2 | async-start | bytes 1048576 | tf_op jit(solution)/shard_map/all_to_all | solution.py:263
  77.1 8.9 %collective-permute-start.3 = (bf16[16,2048]{1,0:T(8,128)(2,1)S(1)}, bf16[16,2048]{1,0:T(8,128)(2,1)S(1)}, u32[]{:S(2)}, u32[]{:S(2)}) collective-permute-start(bf16[16,2048]{1,0:T(8,128)(2,1)S(1)} %pad_maximum_fusion.2), channel_id=1, source_target_pairs={{0,32},{4,36},{8,40},{12,44},{16,48},{20,52},{24,56},{28,60},{32,0... | collective-permute-start | bytes 196616 | tf_op jit(solution)/shard_map/ppermute | solution.py:26
  85.9 13.5 %collective-permute-start.5 = (bf16[8,16,2048]{2,1,0:T(8,128)(2,1)S(1)}, bf16[8,16,2048]{2,1,0:T(8,128)(2,1)S(1)}, u32[]{:S(2)}, u32[]{:S(2)}) collective-permute-start(bf16[8,16,2048]{2,1,0:T(8,128)(2,1)S(1)} %all-to-all-done.2.refs_1_), channel_id=1, source_target_pairs={{0,56},{4,60},{8,0},{12,4},{16,8},{20,12},{24,16},{28,20},{32,24},... | collective-permute-start | bytes 1572872 | tf_op jit(solution)/shard_map/ppermute | solution.py:26
  85.9 14.7 %collective-permute-start.4 = (bf16[8,16,2048]{2,1,0:T(8,128)(2,1)S(1)}, bf16[8,16,2048]{2,1,0:T(8,128)(2,1)S(1)}, u32[]{:S(2)}, u32[]{:S(2)}) collective-permute-start(bf16[8,16,2048]{2,1,0:T(8,128)(2,1)S(1)} %all-to-all-done.2.refs_1_), channel_id=1, source_target_pairs={{0,8},{4,12},{8,16},{12,20},{16,24},{20,28},{24,32},{28,36},{32,40... | collective-permute-start | bytes 1572872 | tf_op jit(solution)/shard_map/ppermute | solution.py:26
  91.9 12.3 %all-to-all-start.3 = ((bf16[8,16,2048]{2,1,0:T(8,128)(2,1)}), bf16[8,16,2048]{2,1,0:T(8,128)(2,1)S(1)}, u32[]{:S(2)}, u32[]{:S(2)}) async-start(bf16[8,16,2048]{2,1,0:T(8,128)(2,1)} %broadcast_in_dim.17), calls=%async_computation.3 | async-start | bytes 1048576 | tf_op jit(solution)/shard_map/all_to_all | solution.py:263
  100.6 13.8 %collective-permute-start.6 = (bf16[8,16,2048]{2,1,0:T(8,128)(2,1)S(1)}, bf16[8,16,2048]{2,1,0:T(8,128)(2,1)S(1)}, u32[]{:S(2)}, u32[]{:S(2)}) collective-permute-start(bf16[8,16,2048]{2,1,0:T(8,128)(2,1)S(1)} %collective-permute-done.4.refs_1_), channel_id=1, source_target_pairs={{0,8},{4,12},{8,16},{12,20},{16,24},{20,28},{24,32},{28,36},{32,40... | collective-permute-start | bytes 1572872 | tf_op jit(solution)/shard_map/ppermute | solution.py:26
  101.2 13.3 %collective-permute-start.7 = (bf16[8,16,2048]{2,1,0:T(8,128)(2,1)S(1)}, bf16[8,16,2048]{2,1,0:T(8,128)(2,1)S(1)}, u32[]{:S(2)}, u32[]{:S(2)}) collective-permute-start(bf16[8,16,2048]{2,1,0:T(8,128)(2,1)S(1)} %collective-permute-done.5.refs_2_), channel_id=1, source_target_pairs={{0,56},{4,60},{8,0},{12,4},{16,8},{20,12},{24,16},{28,20},{32,24},... | collective-permute-start | bytes 1572872 | tf_op jit(solution)/shard_map/ppermute | solution.py:26
  114.5 12.9 %collective-permute-start.8 = (bf16[8,16,2048]{2,1,0:T(8,128)(2,1)S(1)}, bf16[8,16,2048]{2,1,0:T(8,128)(2,1)S(1)}, u32[]{:S(2)}, u32[]{:S(2)}) collective-permute-start(bf16[8,16,2048]{2,1,0:T(8,128)(2,1)S(1)} %collective-permute-done.6.refs_1_), channel_id=1, source_target_pairs={{0,8},{4,12},{8,16},{12,20},{16,24},{20,28},{24,32},{28,36},{32,40... | collective-permute-start | bytes 1572872 | tf_op jit(solution)/shard_map/ppermute | solution.py:26
  114.5 12.9 %collective-permute-start.9 = (bf16[8,16,2048]{2,1,0:T(8,128)(2,1)S(1)}, bf16[8,16,2048]{2,1,0:T(8,128)(2,1)S(1)}, u32[]{:S(2)}, u32[]{:S(2)}) collective-permute-start(bf16[8,16,2048]{2,1,0:T(8,128)(2,1)S(1)} %collective-permute-done.7.refs_2_), channel_id=1, source_target_pairs={{0,56},{4,60},{8,0},{12,4},{16,8},{20,12},{24,16},{28,20},{32,24},... | collective-permute-start | bytes 1572872 | tf_op jit(solution)/shard_map/ppermute | solution.py:26

commit v4 on v3

--- a/solution.py
+++ b/solution.py
@@ -269,19 +269,21 @@
 
     near = gather_yx(chosen)
     opposite = shift(chosen, dz=4)
-    near, opposite = lax.optimization_barrier((near, opposite))
     tables = (receivers, split, even, odd, steps * chans * r)
     pairs = steps * NY
+    near, opposite = lax.optimization_barrier((near, opposite))
     up, down = shift(near, dz=1), shift(near, dz=-1)
-    cross_near = cross_of("cross_near", (near,), receivers)
+    ready = near
+    cross_near = cross_of("cross_near", (ready,), receivers)
     opposite, cross_near = lax.optimization_barrier((opposite, cross_near))
     far = gather_yx(opposite)
     up, down, cross_near = lax.optimization_barrier((up, down, cross_near))
     up2, down2 = shift(up, dz=1), shift(down, dz=-1)
-    out = lags_of("lags_1", place, 0, (cross_near,), (up, down, far), *tables)
+    far, cross_near = lax.optimization_barrier((far, cross_near))
+    out = lags_of("lags_1", place, 0, (cross_near,), (up, down), *tables)
     up2, down2, out = lax.optimization_barrier((up2, down2, out))
     up3, down3 = shift(up2, dz=1), shift(down2, dz=-1)
-    out = lags_of("lags_2", place, 4 * pairs, (), (up2, down2), *tables, out)
+    out = lags_of("lags_2", place, 3 * pairs, (), (far, up2, down2), *tables, out)
     up3, down3, out = lax.optimization_barrier((up3, down3, out))
     out = lags_of("lags_3", place, 6 * pairs, (), (up3, down3), *tables, out)
     return out.reshape(steps, chans, r, width)

time: 135 us -> 134 us (level)
  no operation moved by 1% of the time
where the time goes in v4:
time: 134 us; the launch traced here: 133 us
  starting transfers between devices  40.3 us (30%)
  other arithmetic  26.6 us (20%)
  waiting for transfers between devices  26 us (19%)
  Pallas kernels  25.9 us (19%)
  local copies, waits for them, and re-layouts  7.5 us (6%)
  between operations  6.82 us (5%)
    pallas_call x3, Pallas kernels, lags_of(): pl.pallas_call(functools.partial(lag_kernel, len(done), len(pieces), firs...  22.8 us
    another operation x1, other arithmetic  17.7 us
    ppermute x7, waiting for transfers between devices, shift(): return lax.ppermute(value, 'chan', pairs)  15 us
    all_to_all x2, starting transfers between devices, gather_yx(): lax.all_to_all(copies, 'chan', 0, 0, tiled=True, axis_index_groups=yx_gro...  12.4 us
    ppermute x7, starting transfers between devices, shift(): return lax.ppermute(value, 'chan', pairs)  9.14 us
    all_to_all x1, starting transfers between devices, on_device(): lax.all_to_all(chosen, 'chan', 0, 0, tiled=True, axis_index_groups=z_grou...  8.47 us
    all_to_all x1, starting transfers between devices, on_device(): lax.all_to_all(rows, ('chan', 'win'), 0, 0, tiled=True, axis_index_groups...  7.64 us
    ppermute x3, waiting for transfers between devices, all_windows(): lax.ppermute(give(jnp.mod(win + j, wins)), 'win', [(w, (w + j) % wins) fo...  5.25 us
  transfers between devices with their start and end apart: 14, of which 10 were waited for; matrix products, arithmetic and copies ran while one was open for 18% of the time, Pallas kernels for 14%

profile of v4, /device:TPU:10, one launch (start us, length us, event | category | flops | bytes accessed | tf_op | source)
XLA Modules:
  0.0 133.1 jit_solution(2920254104769761868)
XLA Ops:
  0.0 0.7 convert_reduce_fusion
  0.7 0.2 convert_element_type.34
  0.9 0.2 copy.34
  1.0 3.5 %fusion.6 = bf16[4,2,4,8,2,2048]{5,4,3,2,1,0:T(2,128)(2,1)S(1)} fusion(bf16[4,4,8,2,2,2048]{5,4,3,2,1,0:T(2,128)(2,1)} %bitcast.21, bf16[4,4,8,2]{2,0,3,1:T(4,128)(2,1)S(1)} %copy.34), kind=kLoop, calls=%fused_computation.19 | loop fusion | flops 1048576 | bytes 4194816 | tf_op jit(solution)/shard_map/transpose | solution.py:230
  4.5 2.2 %reshape.118 = bf16[32,16,2048]{2,1,0:T(8,128)(2,1)} reshape(bf16[4,2,4,8,2,2048]{5,4,3,2,1,0:T(2,128)(2,1)S(1)} %fusion.6) | data formatting | bytes 4194304 | tf_op jit(solution)/shard_map/reshape | solution.py:231
  6.7 7.6 %all-to-all-start = ((bf16[32,16,2048]{2,1,0:T(8,128)(2,1)}), bf16[32,16,2048]{2,1,0:T(8,128)(2,1)S(1)}, u32[]{:S(2)}, u32[]{:S(2)}) async-start(bf16[32,16,2048]{2,1,0:T(8,128)(2,1)} %reshape.118), calls=%async_computation | async-start | bytes 4194304 | tf_op jit(solution)/shard_map/all_to_all | solution.py:232
  14.4 0.1 broadcast_add_fusion.1
  14.5 0.1 add.161
  14.7 0.7 fusion.17
  15.4 0.6 fusion.19
  18.6 0.1 add.167.place
  18.8 17.7 %multiply_convert_fusion.1 = (bf16[512,1024]{1,0:T(8,128)(2,1)S(1)}, bf16[512,1024]{1,0:T(8,128)(2,1)S(1)}, bf16[512,1024]{1,0:T(8,128)(2,1)S(1)}, bf16[512,1024]{1,0:T(8,128)(2,1)S(1)}) fusion(f32[512]{0:T(512)S(1)} %select_multiply_fusion, s32[1024]{0:T(1024)S(1)} %iota_add_fusion, s32[512]{0:T(512)S(1)} %fusion.10, f32[512]{0:T(512)S(1)} %fusion.14, ...), kind=kLoop, calls=%fused_computation.21 | loop fusion | flops 18874368 | bytes 4210688 | tf_op jit(solution)/shard_map/convert
  36.5 2.4 %pad_maximum_fusion = (bf16[1024,1024]{1,0:T(8,128)(2,1)}, bf16[1024,1024]{1,0:T(8,128)(2,1)}) fusion(bf16[512,1024]{1,0:T(8,128)(2,1)S(1)} %get-tuple-element.69, bf16[512,1024]{1,0:T(8,128)(2,1)S(1)} %get-tuple-element.70, bf16[512,1024]{1,0:T(8,128)(2,1)S(1)} %get-tuple-element.66, bf16[512,1024]{1,0:T(8,128)(2,1)S(1)} %get-tuple-element.65), kind=kLoop, calls=%fused_computation.16 | loop fusion | flops 8388608 | bytes 8388608 | tf_op jit(solution)/shard_map/concatenate | solution.py:47
  38.9 0.7 fusion.7.refs_4_.refs_3_
  39.5 0.4 all-to-all-done
  40.0 0.2 copy.36
  40.2 0.2 copy.37
  40.4 0.4 maximum_bitcast_fusion
  40.8 0.3 copy.38
  41.1 1.1 copy.39
  42.2 8.5 %all-to-all-start.1 = ((bf16[8,16,2048]{2,1,0:T(8,128)(2,1)}), bf16[8,16,2048]{2,1,0:T(8,128)(2,1)S(1)}, u32[]{:S(2)}, u32[]{:S(2)}) async-start(bf16[8,16,2048]{2,1,0:T(8,128)(2,1)} %copy.39), calls=%async_computation.1 | async-start | bytes 1048576 | tf_op jit(solution)/shard_map/all_to_all | solution.py:257
  50.7 0.1 fusion.8
  50.8 1.7 %collective-permute-start.1 = (bf16[2,8,2048]{2,1,0:T(8,128)(2,1)S(1)}, bf16[2,8,2048]{2,1,0:T(8,128)(2,1)S(1)}, u32[]{:S(2)}, u32[]{:S(2)}) collective-permute-start(bf16[2,8,2048]{2,1,0:T(8,128)(2,1)S(1)} %fusion.8), channel_id=1, source_target_pairs={{0,2},{1,3},{2,0},{3,1},{4,6},{5,7},{6,4},{7,5},{8,10},{9,11},{10,... | collective-permute-start | bytes 196616 | tf_op jit(solution)/shard_map/ppermute | solution.py:237
  52.5 1.0 collective-permute-start.2
  53.4 3.1 %collective-permute-done.1 = bf16[2,8,2048]{2,1,0:T(8,128)(2,1)S(1)} collective-permute-done((bf16[2,8,2048]{2,1,0:T(8,128)(2,1)S(1)}, bf16[2,8,2048]{2,1,0:T(8,128)(2,1)S(1)}, u32[]{:S(2)}, u32[]{:S(2)}) %collective-permute-start.1) | collective-permute-done | bytes 65568 | tf_op jit(solution)/shard_map/ppermute | solution.py:237
  56.6 2.1 %collective-permute-done = bf16[2,8,2048]{2,1,0:T(8,128)(2,1)S(1)} collective-permute-done((bf16[2,8,2048]{2,1,0:T(8,128)(2,1)S(1)}, bf16[2,8,2048]{2,1,0:T(8,128)(2,1)S(1)}, u32[]{:S(2)}, u32[]{:S(2)}) %collective-permute-start) | collective-permute-done | bytes 65568 | tf_op jit(solution)/shard_map/ppermute | solution.py:237
  58.7 0.1 select_select_fusion.3
  58.8 0.8 maximum_convert_fusion.refs_0_
  63.5 4.9 %all-to-all-done.1 = bf16[8,16,2048]{2,1,0:T(8,128)(2,1)S(1)} async-done(((bf16[8,16,2048]{2,1,0:T(8,128)(2,1)}), bf16[8,16,2048]{2,1,0:T(8,128)(2,1)S(1)}, u32[]{:S(2)}, u32[]{:S(2)}) %all-to-all-start.1) | async-done | bytes 524320 | tf_op jit(solution)/shard_map/all_to_all | solution.py:257
  68.4 0.8 broadcast_in_dim.16
  69.2 6.7 %all-to-all-start.2 = ((bf16[8,16,2048]{2,1,0:T(8,128)(2,1)}), bf16[8,16,2048]{2,1,0:T(8,128)(2,1)S(1)}, u32[]{:S(2)}, u32[]{:S(2)}) async-start(bf16[8,16,2048]{2,1,0:T(8,128)(2,1)} %broadcast_in_dim.16), calls=%async_computation.2 | async-start | bytes 1048576 | tf_op jit(solution)/shard_map/all_to_all | solution.py:263
  75.9 0.6 collective-permute-start.3
  76.6 8.2 %collective-permute-done.3 = bf16[16,2048]{1,0:T(8,128)(2,1)S(1)} collective-permute-done((bf16[16,2048]{1,0:T(8,128)(2,1)S(1)}, bf16[16,2048]{1,0:T(8,128)(2,1)S(1)}, u32[]{:S(2)}, u32[]{:S(2)}) %collective-permute-start.3) | collective-permute-done | bytes 65568 | tf_op jit(solution)/shard_map/ppermute | solution.py:26
  84.8 2.0 %collective-permute-start.4 = (bf16[8,16,2048]{2,1,0:T(8,128)(2,1)S(1)}, bf16[8,16,2048]{2,1,0:T(8,128)(2,1)S(1)}, u32[]{:S(2)}, u32[]{:S(2)}) collective-permute-start(bf16[8,16,2048]{2,1,0:T(8,128)(2,1)S(1)} %all-to-all-done.2.refs_1_), channel_id=1, source_target_pairs={{0,8},{4,12},{8,16},{12,20},{16,24},{20,28},{24,32},{28,36},{32,40... | collective-permute-start | bytes 1572872 | tf_op jit(solution)/shard_map/ppermute | solution.py:26
  86.8 3.1 %cross_near.1.refs_3_ = bf16[128,2048]{1,0:T(8,128)(2,1)} custom-call(f32[8,8,2048]{2,1,0:T(8,128)} %maximum_convert_fusion.refs_0_, bf16[8,16,2048]{2,1,0:T(8,128)(2,1)S(1)} %all-to-all-done.2.refs_1_), custom_call_target="tpu_custom_call" | custom-call | flops 128000000 | bytes 131072 | tf_op jit(solution)/shard_map/cross_near/pallas_call | solution.py:129
  89.9 0.8 broadcast_in_dim.17
  90.8 5.7 %all-to-all-start.3 = ((bf16[8,16,2048]{2,1,0:T(8,128)(2,1)}), bf16[8,16,2048]{2,1,0:T(8,128)(2,1)S(1)}, u32[]{:S(2)}, u32[]{:S(2)}) async-start(bf16[8,16,2048]{2,1,0:T(8,128)(2,1)} %broadcast_in_dim.17), calls=%async_computation.3 | async-start | bytes 1048576 | tf_op jit(solution)/shard_map/all_to_all | solution.py:263
  96.5 1.8 %collective-permute-done.5.refs_2_ = bf16[8,16,2048]{2,1,0:T(8,128)(2,1)S(1)} collective-permute-done((bf16[8,16,2048]{2,1,0:T(8,128)(2,1)S(1)}, bf16[8,16,2048]{2,1,0:T(8,128)(2,1)S(1)}, u32[]{:S(2)}, u32[]{:S(2)}) %collective-permute-start.5) | collective-permute-done | bytes 524320 | tf_op jit(solution)/shard_map/ppermute | solution.py:26
  98.3 1.2 collective-permute-done.4.refs_1_
  99.5 0.5 collective-permute-start.6
  100.0 2.7 %collective-permute-start.7 = (bf16[8,16,2048]{2,1,0:T(8,128)(2,1)S(1)}, bf16[8,16,2048]{2,1,0:T(8,128)(2,1)S(1)}, u32[]{:S(2)}, u32[]{:S(2)}) collective-permute-start(bf16[8,16,2048]{2,1,0:T(8,128)(2,1)S(1)} %collective-permute-done.5.refs_2_), channel_id=1, source_target_pairs={{0,56},{4,60},{8,0},{12,4},{16,8},{20,12},{24,16},{28,20},{32,24},... | collective-permute-start | bytes 1572872 | tf_op jit(solution)/shard_map/ppermute | solution.py:26
  102.8 0.4 all-to-all-done.3.refs_1_
  103.1 7.4 %lags_1.1.refs_7_ = bf16[1024,2048]{1,0:T(8,128)(2,1)} custom-call(s32[64]{0:T(128)S(1)} %add.167.place, f32[8,8,2048]{2,1,0:T(8,128)} %maximum_convert_fusion.refs_0_, bf16[8,16,2048]{2,1,0:T(8,128)(2,1)S(1)} %collective-permute-done.4.refs_1_, bf16[8,16,2048]{2,1,0:T(8,128)(2,1)S(1)} %collective-permute-done.5.refs_2_, ...), custom_call_target="tpu_custom_call" | custom-call | flops 4608000000 | bytes 393216 | tf_op jit(solution)/shard_map/lags_1/pallas_call | solution.py:198
  110.6 2.8 %collective-permute-done.6.refs_2_ = bf16[8,16,2048]{2,1,0:T(8,128)(2,1)S(1)} collective-permute-done((bf16[8,16,2048]{2,1,0:T(8,128)(2,1)S(1)}, bf16[8,16,2048]{2,1,0:T(8,128)(2,1)S(1)}, u32[]{:S(2)}, u32[]{:S(2)}) %collective-permute-start.6) | collective-permute-done | bytes 524320 | tf_op jit(solution)/shard_map/ppermute | solution.py:26
  113.3 3.2 %collective-permute-start.9 = (bf16[8,16,2048]{2,1,0:T(8,128)(2,1)S(1)}, bf16[8,16,2048]{2,1,0:T(8,128)(2,1)S(1)}, u32[]{:S(2)}, u32[]{:S(2)}) collective-permute-start(bf16[8,16,2048]{2,1,0:T(8,128)(2,1)S(1)} %collective-permute-done.7.refs_3_), channel_id=1, source_target_pairs={{0,56},{4,60},{8,0},{12,4},{16,8},{20,12},{24,16},{28,20},{32,24},... | collective-permute-start | bytes 1572872 | tf_op jit(solution)/shard_map/ppermute | solution.py:26
  116.6 8.7 %lags_2.1.refs_6_ = bf16[1024,2048]{1,0:T(8,128)(2,1)} custom-call(s32[64]{0:T(128)S(1)} %add.167.place, f32[8,8,2048]{2,1,0:T(8,128)} %maximum_convert_fusion.refs_0_, bf16[8,16,2048]{2,1,0:T(8,128)(2,1)S(1)} %all-to-all-done.3.refs_1_, bf16[8,16,2048]{2,1,0:T(8,128)(2,1)S(1)} %collective-permute-done.6.refs_2_, ...), custom_call_target="tpu_custom_call", output_to_operand_aliasing={{}: (8, {})} | custom-call | flops 4608000000 | bytes 393216 | tf_op jit(solution)/shard_map/lags_2/pallas_call | solution.py:198
  125.2 1.0 collective-permute-done.8.refs_1_
  126.2 6.7 %lags_3.1 = bf16[1024,2048]{1,0:T(8,128)(2,1)} custom-call(s32[64]{0:T(128)S(1)} %add.167.place, f32[8,8,2048]{2,1,0:T(8,128)} %maximum_convert_fusion.refs_0_, bf16[8,16,2048]{2,1,0:T(8,128)(2,1)S(1)} %collective-permute-done.8.refs_1_, bf16[8,16,2048]{2,1,0:T(8,128)(2,1)S(1)} %collective-permute-done.9.refs_2_, ...), custom_call_target="tpu_custom_call", output_to_operand_aliasing={{}: (7, {})} | custom-call | flops 3072000000 | bytes 262144 | tf_op jit(solution)/shard_map/lags_3/pallas_call | solution.py:198
  (32 shorter events, 0.2 us)
Async XLA Ops:
  6.7 7.9 %copy-start.1 = (s32[2]{0:T(128)S(1)}, s32[2]{0:T(128)}, u32[]{:S(2)}) copy-start(s32[2]{0:T(128)} %param.8) | copy-start | bytes 28
  6.7 7.9 %copy-start.3 = (s32[8]{0:T(128)S(1)}, s32[8]{0:T(128)}, u32[]{:S(2)}) copy-start(s32[8]{0:T(128)} %constant.173) | copy-start | bytes 100
  6.7 9.2 %copy-start.2 = (s32[8]{0:T(128)S(1)}, s32[8]{0:T(128)}, u32[]{:S(2)}) copy-start(s32[8]{0:T(128)} %param.10) | copy-start | bytes 100
  6.7 33.2 %all-to-all-start = ((bf16[32,16,2048]{2,1,0:T(8,128)(2,1)}), bf16[32,16,2048]{2,1,0:T(8,128)(2,1)S(1)}, u32[]{:S(2)}, u32[]{:S(2)}) async-start(bf16[32,16,2048]{2,1,0:T(8,128)(2,1)} %reshape.118), calls=%async_computation | async-start | bytes 4194304 | tf_op jit(solution)/shard_map/all_to_all | solution.py:232
  40.4 10.2 %copy-start = (bf16[8,2,2048]{2,1,0:T(2,128)(2,1)S(1)}, bf16[8,2,2048]{2,1,0:T(2,128)(2,1)}, u32[]{:S(2)}) copy-start(bf16[8,2,2048]{2,1,0:T(2,128)(2,1)} %param.7) | copy-start | bytes 196612
  42.2 26.2 %all-to-all-start.1 = ((bf16[8,16,2048]{2,1,0:T(8,128)(2,1)}), bf16[8,16,2048]{2,1,0:T(8,128)(2,1)S(1)}, u32[]{:S(2)}, u32[]{:S(2)}) async-start(bf16[8,16,2048]{2,1,0:T(8,128)(2,1)} %copy.39), calls=%async_computation.1 | async-start | bytes 1048576 | tf_op jit(solution)/shard_map/all_to_all | solution.py:257
  50.8 5.8 %collective-permute-start.1 = (bf16[2,8,2048]{2,1,0:T(8,128)(2,1)S(1)}, bf16[2,8,2048]{2,1,0:T(8,128)(2,1)S(1)}, u32[]{:S(2)}, u32[]{:S(2)}) collective-permute-start(bf16[2,8,2048]{2,1,0:T(8,128)(2,1)S(1)} %fusion.8), channel_id=1, source_target_pairs={{0,2},{1,3},{2,0},{3,1},{4,6},{5,7},{6,4},{7,5},{8,10},{9,11},{10,... | collective-permute-start | bytes 196616 | tf_op jit(solution)/shard_map/ppermute | solution.py:237
  52.5 4.1 %collective-permute-start.2 = (bf16[2,8,2048]{2,1,0:T(8,128)(2,1)S(1)}, bf16[2,8,2048]{2,1,0:T(8,128)(2,1)S(1)}, u32[]{:S(2)}, u32[]{:S(2)}) collective-permute-start(bf16[2,8,2048]{2,1,0:T(8,128)(2,1)S(1)} %fusion.8), channel_id=1, source_target_pairs={{0,3},{1,0},{2,1},{3,2},{4,7},{5,4},{6,5},{7,6},{8,11},{9,8},{10,9... | collective-permute-start | bytes 196616 | tf_op jit(solution)/shard_map/ppermute | solution.py:237
  53.4 5.3 %collective-permute-start = (bf16[2,8,2048]{2,1,0:T(8,128)(2,1)S(1)}, bf16[2,8,2048]{2,1,0:T(8,128)(2,1)S(1)}, u32[]{:S(2)}, u32[]{:S(2)}) collective-permute-start(bf16[2,8,2048]{2,1,0:T(8,128)(2,1)S(1)} %fusion.8), channel_id=1, source_target_pairs={{0,1},{1,2},{2,3},{3,0},{4,5},{5,6},{6,7},{7,4},{8,9},{9,10},{10,1... | collective-permute-start | bytes 196616 | tf_op jit(solution)/shard_map/ppermute | solution.py:237
  69.2 15.6 %all-to-all-start.2 = ((bf16[8,16,2048]{2,1,0:T(8,128)(2,1)}), bf16[8,16,2048]{2,1,0:T(8,128)(2,1)S(1)}, u32[]{:S(2)}, u32[]{:S(2)}) async-start(bf16[8,16,2048]{2,1,0:T(8,128)(2,1)} %broadcast_in_dim.16), calls=%async_computation.2 | async-start | bytes 1048576 | tf_op jit(solution)/shard_map/all_to_all | solution.py:263
  75.9 8.9 %collective-permute-start.3 = (bf16[16,2048]{1,0:T(8,128)(2,1)S(1)}, bf16[16,2048]{1,0:T(8,128)(2,1)S(1)}, u32[]{:S(2)}, u32[]{:S(2)}) collective-permute-start(bf16[16,2048]{1,0:T(8,128)(2,1)S(1)} %pad_maximum_fusion.2), channel_id=1, source_target_pairs={{0,32},{4,36},{8,40},{12,44},{16,48},{20,52},{24,56},{28,60},{32,0... | collective-permute-start | bytes 196616 | tf_op jit(solution)/shard_map/ppermute | solution.py:26
  84.8 13.5 %collective-permute-start.5 = (bf16[8,16,2048]{2,1,0:T(8,128)(2,1)S(1)}, bf16[8,16,2048]{2,1,0:T(8,128)(2,1)S(1)}, u32[]{:S(2)}, u32[]{:S(2)}) collective-permute-start(bf16[8,16,2048]{2,1,0:T(8,128)(2,1)S(1)} %all-to-all-done.2.refs_1_), channel_id=1, source_target_pairs={{0,56},{4,60},{8,0},{12,4},{16,8},{20,12},{24,16},{28,20},{32,24},... | collective-permute-start | bytes 1572872 | tf_op jit(solution)/shard_map/ppermute | solution.py:26
  84.8 14.7 %collective-permute-start.4 = (bf16[8,16,2048]{2,1,0:T(8,128)(2,1)S(1)}, bf16[8,16,2048]{2,1,0:T(8,128)(2,1)S(1)}, u32[]{:S(2)}, u32[]{:S(2)}) collective-permute-start(bf16[8,16,2048]{2,1,0:T(8,128)(2,1)S(1)} %all-to-all-done.2.refs_1_), channel_id=1, source_target_pairs={{0,8},{4,12},{8,16},{12,20},{16,24},{20,28},{24,32},{28,36},{32,40... | collective-permute-start | bytes 1572872 | tf_op jit(solution)/shard_map/ppermute | solution.py:26
  90.8 12.3 %all-to-all-start.3 = ((bf16[8,16,2048]{2,1,0:T(8,128)(2,1)}), bf16[8,16,2048]{2,1,0:T(8,128)(2,1)S(1)}, u32[]{:S(2)}, u32[]{:S(2)}) async-start(bf16[8,16,2048]{2,1,0:T(8,128)(2,1)} %broadcast_in_dim.17), calls=%async_computation.3 | async-start | bytes 1048576 | tf_op jit(solution)/shard_map/all_to_all | solution.py:263
  99.5 13.8 %collective-permute-start.6 = (bf16[8,16,2048]{2,1,0:T(8,128)(2,1)S(1)}, bf16[8,16,2048]{2,1,0:T(8,128)(2,1)S(1)}, u32[]{:S(2)}, u32[]{:S(2)}) collective-permute-start(bf16[8,16,2048]{2,1,0:T(8,128)(2,1)S(1)} %collective-permute-done.4.refs_1_), channel_id=1, source_target_pairs={{0,8},{4,12},{8,16},{12,20},{16,24},{20,28},{24,32},{28,36},{32,40... | collective-permute-start | bytes 1572872 | tf_op jit(solution)/shard_map/ppermute | solution.py:26
  100.0 13.3 %collective-permute-start.7 = (bf16[8,16,2048]{2,1,0:T(8,128)(2,1)S(1)}, bf16[8,16,2048]{2,1,0:T(8,128)(2,1)S(1)}, u32[]{:S(2)}, u32[]{:S(2)}) collective-permute-start(bf16[8,16,2048]{2,1,0:T(8,128)(2,1)S(1)} %collective-permute-done.5.refs_2_), channel_id=1, source_target_pairs={{0,56},{4,60},{8,0},{12,4},{16,8},{20,12},{24,16},{28,20},{32,24},... | collective-permute-start | bytes 1572872 | tf_op jit(solution)/shard_map/ppermute | solution.py:26
  113.3 12.9 %collective-permute-start.8 = (bf16[8,16,2048]{2,1,0:T(8,128)(2,1)S(1)}, bf16[8,16,2048]{2,1,0:T(8,128)(2,1)S(1)}, u32[]{:S(2)}, u32[]{:S(2)}) collective-permute-start(bf16[8,16,2048]{2,1,0:T(8,128)(2,1)S(1)} %collective-permute-done.6.refs_2_), channel_id=1, source_target_pairs={{0,8},{4,12},{8,16},{12,20},{16,24},{20,28},{24,32},{28,36},{32,40... | collective-permute-start | bytes 1572872 | tf_op jit(solution)/shard_map/ppermute | solution.py:26
  113.3 12.9 %collective-permute-start.9 = (bf16[8,16,2048]{2,1,0:T(8,128)(2,1)S(1)}, bf16[8,16,2048]{2,1,0:T(8,128)(2,1)S(1)}, u32[]{:S(2)}, u32[]{:S(2)}) collective-permute-start(bf16[8,16,2048]{2,1,0:T(8,128)(2,1)S(1)} %collective-permute-done.7.refs_3_), channel_id=1, source_target_pairs={{0,56},{4,60},{8,0},{12,4},{16,8},{20,12},{24,16},{28,20},{32,24},... | collective-permute-start | bytes 1572872 | tf_op jit(solution)/shard_map/ppermute | solution.py:26

commit v5 on v4

--- a/solution.py
+++ b/solution.py
@@ -153,10 +153,15 @@
         at += part.shape[0] // pair
     targets = list(buffers)
     targets[1 + n_pieces : 1 + n_pieces + n_done] = spans
-    copies = fetch(sources, targets, sems)
+    copies = [pltpu.make_async_copy(ref, target, sems.at[i]) for i, (ref, target) in enumerate(zip(sources, targets))]
+    for copy in copies[: 1 + n_pieces]:
+        copy.start()
     copies[0].wait()
-    for piece, copy in zip(pieces, copies[1:]):
+    for number, (piece, copy) in enumerate(zip(pieces, copies[1:])):
         copy.wait()
+        if number == 0:
+            for later in copies[1 + n_pieces :]:
+                later.start()
         add_cross(piece, receivers, wide, cross, at)
         at += piece.shape[0] * piece.shape[1] // (2 * receivers.shape[0])
     for copy in copies[1 + n_pieces :]:

time: 134 us -> 134 us (level)
  no operation moved by 1% of the time
where the time goes in v5:
time: 134 us; the launch traced here: 133 us
  starting transfers between devices  40.3 us (30%)
  other arithmetic  26.6 us (20%)
  waiting for transfers between devices  26 us (19%)
  Pallas kernels  25.9 us (19%)
  local copies, waits for them, and re-layouts  7.5 us (6%)
  between operations  6.82 us (5%)
    pallas_call x3, Pallas kernels, lags_of(): pl.pallas_call(functools.partial(lag_kernel, len(done), len(pieces), firs...  22.8 us
    another operation x1, other arithmetic  17.7 us
    ppermute x7, waiting for transfers between devices, shift(): return lax.ppermute(value, 'chan', pairs)  15 us
    all_to_all x2, starting transfers between devices, gather_yx(): lax.all_to_all(copies, 'chan', 0, 0, tiled=True, axis_index_groups=yx_gro...  12.4 us
    ppermute x7, starting transfers between devices, shift(): return lax.ppermute(value, 'chan', pairs)  9.14 us
    all_to_all x1, starting transfers between devices, on_device(): lax.all_to_all(chosen, 'chan', 0, 0, tiled=True, axis_index_groups=z_grou...  8.47 us
    all_to_all x1, starting transfers between devices, on_device(): lax.all_to_all(rows, ('chan', 'win'), 0, 0, tiled=True, axis_index_groups...  7.64 us
    ppermute x3, waiting for transfers between devices, all_windows(): lax.ppermute(give(jnp.mod(win + j, wins)), 'win', [(w, (w + j) % wins) fo...  5.25 us
  transfers between devices with their start and end apart: 14, of which 10 were waited for; matrix products, arithmetic and copies ran while one was open for 18% of the time, Pallas kernels for 14%

profile of v5, /device:TPU:10, one launch (start us, length us, event | category | flops | bytes accessed | tf_op | source)
XLA Modules:
  0.0 133.1 jit_solution(12472462986848400492)
XLA Ops:
  0.0 0.7 convert_reduce_fusion
  0.7 0.2 convert_element_type.34
  0.9 0.2 copy.34
  1.0 3.5 %fusion.6 = bf16[4,2,4,8,2,2048]{5,4,3,2,1,0:T(2,128)(2,1)S(1)} fusion(bf16[4,4,8,2,2,2048]{5,4,3,2,1,0:T(2,128)(2,1)} %bitcast.21, bf16[4,4,8,2]{2,0,3,1:T(4,128)(2,1)S(1)} %copy.34), kind=kLoop, calls=%fused_computation.19 | loop fusion | flops 1048576 | bytes 4194816 | tf_op jit(solution)/shard_map/transpose | solution.py:235
  4.5 2.2 %reshape.118 = bf16[32,16,2048]{2,1,0:T(8,128)(2,1)} reshape(bf16[4,2,4,8,2,2048]{5,4,3,2,1,0:T(2,128)(2,1)S(1)} %fusion.6) | data formatting | bytes 4194304 | tf_op jit(solution)/shard_map/reshape | solution.py:236
  6.7 7.6 %all-to-all-start = ((bf16[32,16,2048]{2,1,0:T(8,128)(2,1)}), bf16[32,16,2048]{2,1,0:T(8,128)(2,1)S(1)}, u32[]{:S(2)}, u32[]{:S(2)}) async-start(bf16[32,16,2048]{2,1,0:T(8,128)(2,1)} %reshape.118), calls=%async_computation | async-start | bytes 4194304 | tf_op jit(solution)/shard_map/all_to_all | solution.py:237
  14.4 0.1 broadcast_add_fusion.1
  14.5 0.1 add.161
  14.7 0.7 fusion.17
  15.4 0.6 fusion.19
  18.6 0.1 add.167.place
  18.8 17.7 %multiply_convert_fusion.1 = (bf16[512,1024]{1,0:T(8,128)(2,1)S(1)}, bf16[512,1024]{1,0:T(8,128)(2,1)S(1)}, bf16[512,1024]{1,0:T(8,128)(2,1)S(1)}, bf16[512,1024]{1,0:T(8,128)(2,1)S(1)}) fusion(f32[512]{0:T(512)S(1)} %select_multiply_fusion, s32[1024]{0:T(1024)S(1)} %iota_add_fusion, s32[512]{0:T(512)S(1)} %fusion.10, f32[512]{0:T(512)S(1)} %fusion.14, ...), kind=kLoop, calls=%fused_computation.21 | loop fusion | flops 18874368 | bytes 4210688 | tf_op jit(solution)/shard_map/convert
  36.5 2.4 %pad_maximum_fusion = (bf16[1024,1024]{1,0:T(8,128)(2,1)}, bf16[1024,1024]{1,0:T(8,128)(2,1)}) fusion(bf16[512,1024]{1,0:T(8,128)(2,1)S(1)} %get-tuple-element.69, bf16[512,1024]{1,0:T(8,128)(2,1)S(1)} %get-tuple-element.70, bf16[512,1024]{1,0:T(8,128)(2,1)S(1)} %get-tuple-element.66, bf16[512,1024]{1,0:T(8,128)(2,1)S(1)} %get-tuple-element.65), kind=kLoop, calls=%fused_computation.16 | loop fusion | flops 8388608 | bytes 8388608 | tf_op jit(solution)/shard_map/concatenate | solution.py:47
  38.9 0.7 fusion.7.refs_4_.refs_3_
  39.5 0.4 all-to-all-done
  40.0 0.2 copy.36
  40.2 0.2 copy.37
  40.4 0.4 maximum_bitcast_fusion
  40.8 0.3 copy.38
  41.1 1.1 copy.39
  42.2 8.5 %all-to-all-start.1 = ((bf16[8,16,2048]{2,1,0:T(8,128)(2,1)}), bf16[8,16,2048]{2,1,0:T(8,128)(2,1)S(1)}, u32[]{:S(2)}, u32[]{:S(2)}) async-start(bf16[8,16,2048]{2,1,0:T(8,128)(2,1)} %copy.39), calls=%async_computation.1 | async-start | bytes 1048576 | tf_op jit(solution)/shard_map/all_to_all | solution.py:262
  50.7 0.1 fusion.8
  50.8 1.7 %collective-permute-start.1 = (bf16[2,8,2048]{2,1,0:T(8,128)(2,1)S(1)}, bf16[2,8,2048]{2,1,0:T(8,128)(2,1)S(1)}, u32[]{:S(2)}, u32[]{:S(2)}) collective-permute-start(bf16[2,8,2048]{2,1,0:T(8,128)(2,1)S(1)} %fusion.8), channel_id=1, source_target_pairs={{0,2},{1,3},{2,0},{3,1},{4,6},{5,7},{6,4},{7,5},{8,10},{9,11},{10,... | collective-permute-start | bytes 196616 | tf_op jit(solution)/shard_map/ppermute | solution.py:242
  52.5 1.0 collective-permute-start.2
  53.4 3.1 %collective-permute-done.1 = bf16[2,8,2048]{2,1,0:T(8,128)(2,1)S(1)} collective-permute-done((bf16[2,8,2048]{2,1,0:T(8,128)(2,1)S(1)}, bf16[2,8,2048]{2,1,0:T(8,128)(2,1)S(1)}, u32[]{:S(2)}, u32[]{:S(2)}) %collective-permute-start.1) | collective-permute-done | bytes 65568 | tf_op jit(solution)/shard_map/ppermute | solution.py:242
  56.6 2.1 %collective-permute-done = bf16[2,8,2048]{2,1,0:T(8,128)(2,1)S(1)} collective-permute-done((bf16[2,8,2048]{2,1,0:T(8,128)(2,1)S(1)}, bf16[2,8,2048]{2,1,0:T(8,128)(2,1)S(1)}, u32[]{:S(2)}, u32[]{:S(2)}) %collective-permute-start) | collective-permute-done | bytes 65568 | tf_op jit(solution)/shard_map/ppermute | solution.py:242
  58.7 0.1 select_select_fusion.3
  58.8 0.8 maximum_convert_fusion.refs_0_
  63.5 4.9 %all-to-all-done.1 = bf16[8,16,2048]{2,1,0:T(8,128)(2,1)S(1)} async-done(((bf16[8,16,2048]{2,1,0:T(8,128)(2,1)}), bf16[8,16,2048]{2,1,0:T(8,128)(2,1)S(1)}, u32[]{:S(2)}, u32[]{:S(2)}) %all-to-all-start.1) | async-done | bytes 524320 | tf_op jit(solution)/shard_map/all_to_all | solution.py:262
  68.4 0.8 broadcast_in_dim.16
  69.2 6.7 %all-to-all-start.2 = ((bf16[8,16,2048]{2,1,0:T(8,128)(2,1)}), bf16[8,16,2048]{2,1,0:T(8,128)(2,1)S(1)}, u32[]{:S(2)}, u32[]{:S(2)}) async-start(bf16[8,16,2048]{2,1,0:T(8,128)(2,1)} %broadcast_in_dim.16), calls=%async_computation.2 | async-start | bytes 1048576 | tf_op jit(solution)/shard_map/all_to_all | solution.py:268
  75.9 0.6 collective-permute-start.3
  76.6 8.2 %collective-permute-done.3 = bf16[16,2048]{1,0:T(8,128)(2,1)S(1)} collective-permute-done((bf16[16,2048]{1,0:T(8,128)(2,1)S(1)}, bf16[16,2048]{1,0:T(8,128)(2,1)S(1)}, u32[]{:S(2)}, u32[]{:S(2)}) %collective-permute-start.3) | collective-permute-done | bytes 65568 | tf_op jit(solution)/shard_map/ppermute | solution.py:26
  84.8 2.0 %collective-permute-start.4 = (bf16[8,16,2048]{2,1,0:T(8,128)(2,1)S(1)}, bf16[8,16,2048]{2,1,0:T(8,128)(2,1)S(1)}, u32[]{:S(2)}, u32[]{:S(2)}) collective-permute-start(bf16[8,16,2048]{2,1,0:T(8,128)(2,1)S(1)} %all-to-all-done.2.refs_1_), channel_id=1, source_target_pairs={{0,8},{4,12},{8,16},{12,20},{16,24},{20,28},{24,32},{28,36},{32,40... | collective-permute-start | bytes 1572872 | tf_op jit(solution)/shard_map/ppermute | solution.py:26
  86.8 3.1 %cross_near.1.refs_3_ = bf16[128,2048]{1,0:T(8,128)(2,1)} custom-call(f32[8,8,2048]{2,1,0:T(8,128)} %maximum_convert_fusion.refs_0_, bf16[8,16,2048]{2,1,0:T(8,128)(2,1)S(1)} %all-to-all-done.2.refs_1_), custom_call_target="tpu_custom_call" | custom-call | flops 128000000 | bytes 131072 | tf_op jit(solution)/shard_map/cross_near/pallas_call | solution.py:129
  89.9 0.8 broadcast_in_dim.17
  90.8 5.7 %all-to-all-start.3 = ((bf16[8,16,2048]{2,1,0:T(8,128)(2,1)}), bf16[8,16,2048]{2,1,0:T(8,128)(2,1)S(1)}, u32[]{:S(2)}, u32[]{:S(2)}) async-start(bf16[8,16,2048]{2,1,0:T(8,128)(2,1)} %broadcast_in_dim.17), calls=%async_computation.3 | async-start | bytes 1048576 | tf_op jit(solution)/shard_map/all_to_all | solution.py:268
  96.5 1.8 %collective-permute-done.5.refs_2_ = bf16[8,16,2048]{2,1,0:T(8,128)(2,1)S(1)} collective-permute-done((bf16[8,16,2048]{2,1,0:T(8,128)(2,1)S(1)}, bf16[8,16,2048]{2,1,0:T(8,128)(2,1)S(1)}, u32[]{:S(2)}, u32[]{:S(2)}) %collective-permute-start.5) | collective-permute-done | bytes 524320 | tf_op jit(solution)/shard_map/ppermute | solution.py:26
  98.3 1.2 collective-permute-done.4.refs_1_
  99.5 0.5 collective-permute-start.6
  100.0 2.7 %collective-permute-start.7 = (bf16[8,16,2048]{2,1,0:T(8,128)(2,1)S(1)}, bf16[8,16,2048]{2,1,0:T(8,128)(2,1)S(1)}, u32[]{:S(2)}, u32[]{:S(2)}) collective-permute-start(bf16[8,16,2048]{2,1,0:T(8,128)(2,1)S(1)} %collective-permute-done.5.refs_2_), channel_id=1, source_target_pairs={{0,56},{4,60},{8,0},{12,4},{16,8},{20,12},{24,16},{28,20},{32,24},... | collective-permute-start | bytes 1572872 | tf_op jit(solution)/shard_map/ppermute | solution.py:26
  102.8 0.4 all-to-all-done.3.refs_1_
  103.1 7.4 %lags_1.1.refs_7_ = bf16[1024,2048]{1,0:T(8,128)(2,1)} custom-call(s32[64]{0:T(128)S(1)} %add.167.place, f32[8,8,2048]{2,1,0:T(8,128)} %maximum_convert_fusion.refs_0_, bf16[8,16,2048]{2,1,0:T(8,128)(2,1)S(1)} %collective-permute-done.4.refs_1_, bf16[8,16,2048]{2,1,0:T(8,128)(2,1)S(1)} %collective-permute-done.5.refs_2_, ...), custom_call_target="tpu_custom_call" | custom-call | flops 4608000000 | bytes 393216 | tf_op jit(solution)/shard_map/lags_1/pallas_call | solution.py:203
  110.5 2.8 %collective-permute-done.6.refs_2_ = bf16[8,16,2048]{2,1,0:T(8,128)(2,1)S(1)} collective-permute-done((bf16[8,16,2048]{2,1,0:T(8,128)(2,1)S(1)}, bf16[8,16,2048]{2,1,0:T(8,128)(2,1)S(1)}, u32[]{:S(2)}, u32[]{:S(2)}) %collective-permute-start.6) | collective-permute-done | bytes 524320 | tf_op jit(solution)/shard_map/ppermute | solution.py:26
  113.3 3.2 %collective-permute-start.9 = (bf16[8,16,2048]{2,1,0:T(8,128)(2,1)S(1)}, bf16[8,16,2048]{2,1,0:T(8,128)(2,1)S(1)}, u32[]{:S(2)}, u32[]{:S(2)}) collective-permute-start(bf16[8,16,2048]{2,1,0:T(8,128)(2,1)S(1)} %collective-permute-done.7.refs_3_), channel_id=1, source_target_pairs={{0,56},{4,60},{8,0},{12,4},{16,8},{20,12},{24,16},{28,20},{32,24},... | collective-permute-start | bytes 1572872 | tf_op jit(solution)/shard_map/ppermute | solution.py:26
  116.6 8.7 %lags_2.1.refs_6_ = bf16[1024,2048]{1,0:T(8,128)(2,1)} custom-call(s32[64]{0:T(128)S(1)} %add.167.place, f32[8,8,2048]{2,1,0:T(8,128)} %maximum_convert_fusion.refs_0_, bf16[8,16,2048]{2,1,0:T(8,128)(2,1)S(1)} %all-to-all-done.3.refs_1_, bf16[8,16,2048]{2,1,0:T(8,128)(2,1)S(1)} %collective-permute-done.6.refs_2_, ...), custom_call_target="tpu_custom_call", output_to_operand_aliasing={{}: (8, {})} | custom-call | flops 4608000000 | bytes 393216 | tf_op jit(solution)/shard_map/lags_2/pallas_call | solution.py:203
  125.2 1.0 collective-permute-done.8.refs_1_
  126.2 6.7 %lags_3.1 = bf16[1024,2048]{1,0:T(8,128)(2,1)} custom-call(s32[64]{0:T(128)S(1)} %add.167.place, f32[8,8,2048]{2,1,0:T(8,128)} %maximum_convert_fusion.refs_0_, bf16[8,16,2048]{2,1,0:T(8,128)(2,1)S(1)} %collective-permute-done.8.refs_1_, bf16[8,16,2048]{2,1,0:T(8,128)(2,1)S(1)} %collective-permute-done.9.refs_2_, ...), custom_call_target="tpu_custom_call", output_to_operand_aliasing={{}: (7, {})} | custom-call | flops 3072000000 | bytes 262144 | tf_op jit(solution)/shard_map/lags_3/pallas_call | solution.py:203
  (32 shorter events, 0.2 us)
Async XLA Ops:
  6.7 7.9 %copy-start.1 = (s32[2]{0:T(128)S(1)}, s32[2]{0:T(128)}, u32[]{:S(2)}) copy-start(s32[2]{0:T(128)} %param.8) | copy-start | bytes 28
  6.7 7.9 %copy-start.3 = (s32[8]{0:T(128)S(1)}, s32[8]{0:T(128)}, u32[]{:S(2)}) copy-start(s32[8]{0:T(128)} %constant.173) | copy-start | bytes 100
  6.7 9.2 %copy-start.2 = (s32[8]{0:T(128)S(1)}, s32[8]{0:T(128)}, u32[]{:S(2)}) copy-start(s32[8]{0:T(128)} %param.10) | copy-start | bytes 100
  6.7 33.2 %all-to-all-start = ((bf16[32,16,2048]{2,1,0:T(8,128)(2,1)}), bf16[32,16,2048]{2,1,0:T(8,128)(2,1)S(1)}, u32[]{:S(2)}, u32[]{:S(2)}) async-start(bf16[32,16,2048]{2,1,0:T(8,128)(2,1)} %reshape.118), calls=%async_computation | async-start | bytes 4194304 | tf_op jit(solution)/shard_map/all_to_all | solution.py:237
  40.4 10.2 %copy-start = (bf16[8,2,2048]{2,1,0:T(2,128)(2,1)S(1)}, bf16[8,2,2048]{2,1,0:T(2,128)(2,1)}, u32[]{:S(2)}) copy-start(bf16[8,2,2048]{2,1,0:T(2,128)(2,1)} %param.7) | copy-start | bytes 196612
  42.2 26.2 %all-to-all-start.1 = ((bf16[8,16,2048]{2,1,0:T(8,128)(2,1)}), bf16[8,16,2048]{2,1,0:T(8,128)(2,1)S(1)}, u32[]{:S(2)}, u32[]{:S(2)}) async-start(bf16[8,16,2048]{2,1,0:T(8,128)(2,1)} %copy.39), calls=%async_computation.1 | async-start | bytes 1048576 | tf_op jit(solution)/shard_map/all_to_all | solution.py:262
  50.8 5.8 %collective-permute-start.1 = (bf16[2,8,2048]{2,1,0:T(8,128)(2,1)S(1)}, bf16[2,8,2048]{2,1,0:T(8,128)(2,1)S(1)}, u32[]{:S(2)}, u32[]{:S(2)}) collective-permute-start(bf16[2,8,2048]{2,1,0:T(8,128)(2,1)S(1)} %fusion.8), channel_id=1, source_target_pairs={{0,2},{1,3},{2,0},{3,1},{4,6},{5,7},{6,4},{7,5},{8,10},{9,11},{10,... | collective-permute-start | bytes 196616 | tf_op jit(solution)/shard_map/ppermute | solution.py:242
  52.5 4.1 %collective-permute-start.2 = (bf16[2,8,2048]{2,1,0:T(8,128)(2,1)S(1)}, bf16[2,8,2048]{2,1,0:T(8,128)(2,1)S(1)}, u32[]{:S(2)}, u32[]{:S(2)}) collective-permute-start(bf16[2,8,2048]{2,1,0:T(8,128)(2,1)S(1)} %fusion.8), channel_id=1, source_target_pairs={{0,3},{1,0},{2,1},{3,2},{4,7},{5,4},{6,5},{7,6},{8,11},{9,8},{10,9... | collective-permute-start | bytes 196616 | tf_op jit(solution)/shard_map/ppermute | solution.py:242
  53.4 5.3 %collective-permute-start = (bf16[2,8,2048]{2,1,0:T(8,128)(2,1)S(1)}, bf16[2,8,2048]{2,1,0:T(8,128)(2,1)S(1)}, u32[]{:S(2)}, u32[]{:S(2)}) collective-permute-start(bf16[2,8,2048]{2,1,0:T(8,128)(2,1)S(1)} %fusion.8), channel_id=1, source_target_pairs={{0,1},{1,2},{2,3},{3,0},{4,5},{5,6},{6,7},{7,4},{8,9},{9,10},{10,1... | collective-permute-start | bytes 196616 | tf_op jit(solution)/shard_map/ppermute | solution.py:242
  69.2 15.6 %all-to-all-start.2 = ((bf16[8,16,2048]{2,1,0:T(8,128)(2,1)}), bf16[8,16,2048]{2,1,0:T(8,128)(2,1)S(1)}, u32[]{:S(2)}, u32[]{:S(2)}) async-start(bf16[8,16,2048]{2,1,0:T(8,128)(2,1)} %broadcast_in_dim.16), calls=%async_computation.2 | async-start | bytes 1048576 | tf_op jit(solution)/shard_map/all_to_all | solution.py:268
  75.9 8.9 %collective-permute-start.3 = (bf16[16,2048]{1,0:T(8,128)(2,1)S(1)}, bf16[16,2048]{1,0:T(8,128)(2,1)S(1)}, u32[]{:S(2)}, u32[]{:S(2)}) collective-permute-start(bf16[16,2048]{1,0:T(8,128)(2,1)S(1)} %pad_maximum_fusion.2), channel_id=1, source_target_pairs={{0,32},{4,36},{8,40},{12,44},{16,48},{20,52},{24,56},{28,60},{32,0... | collective-permute-start | bytes 196616 | tf_op jit(solution)/shard_map/ppermute | solution.py:26
  84.8 13.5 %collective-permute-start.5 = (bf16[8,16,2048]{2,1,0:T(8,128)(2,1)S(1)}, bf16[8,16,2048]{2,1,0:T(8,128)(2,1)S(1)}, u32[]{:S(2)}, u32[]{:S(2)}) collective-permute-start(bf16[8,16,2048]{2,1,0:T(8,128)(2,1)S(1)} %all-to-all-done.2.refs_1_), channel_id=1, source_target_pairs={{0,56},{4,60},{8,0},{12,4},{16,8},{20,12},{24,16},{28,20},{32,24},... | collective-permute-start | bytes 1572872 | tf_op jit(solution)/shard_map/ppermute | solution.py:26
  84.8 14.7 %collective-permute-start.4 = (bf16[8,16,2048]{2,1,0:T(8,128)(2,1)S(1)}, bf16[8,16,2048]{2,1,0:T(8,128)(2,1)S(1)}, u32[]{:S(2)}, u32[]{:S(2)}) collective-permute-start(bf16[8,16,2048]{2,1,0:T(8,128)(2,1)S(1)} %all-to-all-done.2.refs_1_), channel_id=1, source_target_pairs={{0,8},{4,12},{8,16},{12,20},{16,24},{20,28},{24,32},{28,36},{32,40... | collective-permute-start | bytes 1572872 | tf_op jit(solution)/shard_map/ppermute | solution.py:26
  90.8 12.3 %all-to-all-start.3 = ((bf16[8,16,2048]{2,1,0:T(8,128)(2,1)}), bf16[8,16,2048]{2,1,0:T(8,128)(2,1)S(1)}, u32[]{:S(2)}, u32[]{:S(2)}) async-start(bf16[8,16,2048]{2,1,0:T(8,128)(2,1)} %broadcast_in_dim.17), calls=%async_computation.3 | async-start | bytes 1048576 | tf_op jit(solution)/shard_map/all_to_all | solution.py:268
  99.5 13.8 %collective-permute-start.6 = (bf16[8,16,2048]{2,1,0:T(8,128)(2,1)S(1)}, bf16[8,16,2048]{2,1,0:T(8,128)(2,1)S(1)}, u32[]{:S(2)}, u32[]{:S(2)}) collective-permute-start(bf16[8,16,2048]{2,1,0:T(8,128)(2,1)S(1)} %collective-permute-done.4.refs_1_), channel_id=1, source_target_pairs={{0,8},{4,12},{8,16},{12,20},{16,24},{20,28},{24,32},{28,36},{32,40... | collective-permute-start | bytes 1572872 | tf_op jit(solution)/shard_map/ppermute | solution.py:26
  100.0 13.3 %collective-permute-start.7 = (bf16[8,16,2048]{2,1,0:T(8,128)(2,1)S(1)}, bf16[8,16,2048]{2,1,0:T(8,128)(2,1)S(1)}, u32[]{:S(2)}, u32[]{:S(2)}) collective-permute-start(bf16[8,16,2048]{2,1,0:T(8,128)(2,1)S(1)} %collective-permute-done.5.refs_2_), channel_id=1, source_target_pairs={{0,56},{4,60},{8,0},{12,4},{16,8},{20,12},{24,16},{28,20},{32,24},... | collective-permute-start | bytes 1572872 | tf_op jit(solution)/shard_map/ppermute | solution.py:26
  113.3 12.9 %collective-permute-start.8 = (bf16[8,16,2048]{2,1,0:T(8,128)(2,1)S(1)}, bf16[8,16,2048]{2,1,0:T(8,128)(2,1)S(1)}, u32[]{:S(2)}, u32[]{:S(2)}) collective-permute-start(bf16[8,16,2048]{2,1,0:T(8,128)(2,1)S(1)} %collective-permute-done.6.refs_2_), channel_id=1, source_target_pairs={{0,8},{4,12},{8,16},{12,20},{16,24},{20,28},{24,32},{28,36},{32,40... | collective-permute-start | bytes 1572872 | tf_op jit(solution)/shard_map/ppermute | solution.py:26
  113.3 12.9 %collective-permute-start.9 = (bf16[8,16,2048]{2,1,0:T(8,128)(2,1)S(1)}, bf16[8,16,2048]{2,1,0:T(8,128)(2,1)S(1)}, u32[]{:S(2)}, u32[]{:S(2)}) collective-permute-start(bf16[8,16,2048]{2,1,0:T(8,128)(2,1)S(1)} %collective-permute-done.7.refs_3_), channel_id=1, source_target_pairs={{0,56},{4,60},{8,0},{12,4},{16,8},{20,12},{24,16},{28,20},{32,24},... | collective-permute-start | bytes 1572872 | tf_op jit(solution)/shard_map/ppermute | solution.py:26

commit v6 on v4

--- a/solution.py
+++ b/solution.py
@@ -62,27 +62,32 @@
     lane = 128
     scale = 1.0 / windows
 
-    def one_pair(i, _, step):
-        row = pl.multiple_of((first_pair + step * (piece.shape[0] // 2) + i) * 2 * r, 2 * r)
-        wide[...] = piece[pl.ds(2 * i, 2), step * windows : (step + 1) * windows].astype(F32)
+    members = wide.shape[0]
+
+    def one_group(i, _, step):
+        pairs = members // 2
+        row = pl.multiple_of((first_pair + step * (piece.shape[0] // 2) + i * pairs) * 2 * r, 2 * r)
+        wide[...] = piece[pl.ds(members * i, members), step * windows : (step + 1) * windows].astype(F32)
         for tile in range(freqs // lane):
             re = pl.ds(tile * lane, lane)
             im = pl.ds(freqs + tile * lane, lane)
-            real, imag = [None, None], [None, None]
+            real, imag = [None] * members, [None] * members
             for w in range(windows):
                 c, d = receivers[w, :, re], receivers[w, :, im]
-                for member in range(2):
+                for member in range(members):
                     a = jnp.broadcast_to(wide[member, w : w + 1, re], c.shape)
                     b = jnp.broadcast_to(wide[member, w : w + 1, im], c.shape)
                     p, q = a * c + b * d, a * d - b * c
                     real[member] = p if w == 0 else real[member] + p
                     imag[member] = q if w == 0 else imag[member] + q
-            cross[pl.ds(row, 2 * r), re] = (jnp.concatenate(real) * scale).astype(BF16)
-            cross[pl.ds(row, 2 * r), im] = (jnp.concatenate(imag) * scale).astype(BF16)
+            for n in range(pairs):
+                rows = pl.ds(pl.multiple_of(row + n * 2 * r, 2 * r), 2 * r)
+                cross[rows, re] = (jnp.concatenate(real[2 * n : 2 * n + 2]) * scale).astype(BF16)
+                cross[rows, im] = (jnp.concatenate(imag[2 * n : 2 * n + 2]) * scale).astype(BF16)
         return 0
 
     for step in range(piece.shape[1] // windows):
-        lax.fori_loop(0, piece.shape[0] // 2, functools.partial(one_pair, step=step), 0)
+        lax.fori_loop(0, piece.shape[0] // members, functools.partial(one_group, step=step), 0)
 
 
 def fetch(refs, buffers, sems):
@@ -132,7 +137,7 @@
         in_specs=[anywhere] * len(inputs),
         out_specs=anywhere,
         scratch_shapes=buffers_of(inputs)
-        + [pltpu.VMEM((rows, width), BF16), pltpu.VMEM((2, windows, width), F32), pltpu.SemaphoreType.DMA],
+        + [pltpu.VMEM((rows, width), BF16), pltpu.VMEM((4, windows, width), F32), pltpu.SemaphoreType.DMA],
         compiler_params=pltpu.CompilerParams(vmem_limit_bytes=8 * 1024 * 1024),
         cost_estimate=pl.CostEstimate(flops=rows * 10**6, bytes_accessed=rows * 2**10, transcendentals=0),
         name=name,
@@ -164,7 +169,7 @@
     freqs = even.shape[1]
     block = split.shape[0]
     total = at * pair
-    chunk = 192 if total % 192 == 0 else 256
+    chunk = 192 if total % 192 == 0 else 128
     copies = []
     for first in range(0, total, chunk):
         rows = pl.ds(first, chunk)
@@ -202,7 +207,7 @@
         out_specs=anywhere,
         scratch_shapes=buffers_of(inputs)
         + [
-            pltpu.VMEM((2, windows, width), F32),
+            pltpu.VMEM((4, windows, width), F32),
             pltpu.VMEM((rows, width), BF16),
             pltpu.VMEM((rows, width), BF16),
             pltpu.SemaphoreType.DMA((rows // (2 * r),)),

time: 134 us -> 134 us (level)
  no operation moved by 1% of the time
where the time goes in v6:
time: 134 us; the launch traced here: 133 us
  starting transfers between devices  40.3 us (30%)
  other arithmetic  26.6 us (20%)
  waiting for transfers between devices  26.2 us (20%)
  Pallas kernels  25.6 us (19%)
  local copies, waits for them, and re-layouts  7.5 us (6%)
  between operations  6.84 us (5%)
    pallas_call x3, Pallas kernels, lags_of(): pl.pallas_call(functools.partial(lag_kernel, len(done), len(pieces), firs...  22.5 us
    another operation x1, other arithmetic  17.7 us
    ppermute x7, waiting for transfers between devices, shift(): return lax.ppermute(value, 'chan', pairs)  15.2 us
    all_to_all x2, starting transfers between devices, gather_yx(): lax.all_to_all(copies, 'chan', 0, 0, tiled=True, axis_index_groups=yx_gro...  12.4 us
    ppermute x7, starting transfers between devices, shift(): return lax.ppermute(value, 'chan', pairs)  9.14 us
    all_to_all x1, starting transfers between devices, on_device(): lax.all_to_all(chosen, 'chan', 0, 0, tiled=True, axis_index_groups=z_grou...  8.47 us
    all_to_all x1, starting transfers between devices, on_device(): lax.all_to_all(rows, ('chan', 'win'), 0, 0, tiled=True, axis_index_groups...  7.64 us
    ppermute x3, waiting for transfers between devices, all_windows(): lax.ppermute(give(jnp.mod(win + j, wins)), 'win', [(w, (w + j) % wins) fo...  5.25 us
  transfers between devices with their start and end apart: 14, of which 10 were waited for; matrix products, arithmetic and copies ran while one was open for 18% of the time, Pallas kernels for 14%

profile of v6, /device:TPU:10, one launch (start us, length us, event | category | flops | bytes accessed | tf_op | source)
XLA Modules:
  0.0 133.0 jit_solution(38647272270483788)
XLA Ops:
  0.0 0.7 convert_reduce_fusion
  0.7 0.2 convert_element_type.34
  0.9 0.2 copy.34
  1.0 3.5 %fusion.6 = bf16[4,2,4,8,2,2048]{5,4,3,2,1,0:T(2,128)(2,1)S(1)} fusion(bf16[4,4,8,2,2,2048]{5,4,3,2,1,0:T(2,128)(2,1)} %bitcast.21, bf16[4,4,8,2]{2,0,3,1:T(4,128)(2,1)S(1)} %copy.34), kind=kLoop, calls=%fused_computation.19 | loop fusion | flops 1048576 | bytes 4194816 | tf_op jit(solution)/shard_map/transpose | solution.py:235
  4.5 2.2 %reshape.118 = bf16[32,16,2048]{2,1,0:T(8,128)(2,1)} reshape(bf16[4,2,4,8,2,2048]{5,4,3,2,1,0:T(2,128)(2,1)S(1)} %fusion.6) | data formatting | bytes 4194304 | tf_op jit(solution)/shard_map/reshape | solution.py:236
  6.7 7.6 %all-to-all-start = ((bf16[32,16,2048]{2,1,0:T(8,128)(2,1)}), bf16[32,16,2048]{2,1,0:T(8,128)(2,1)S(1)}, u32[]{:S(2)}, u32[]{:S(2)}) async-start(bf16[32,16,2048]{2,1,0:T(8,128)(2,1)} %reshape.118), calls=%async_computation | async-start | bytes 4194304 | tf_op jit(solution)/shard_map/all_to_all | solution.py:237
  14.4 0.1 broadcast_add_fusion.1
  14.5 0.1 add.161
  14.7 0.7 fusion.17
  15.4 0.6 fusion.19
  18.6 0.1 add.167.place
  18.8 17.7 %multiply_convert_fusion.1 = (bf16[512,1024]{1,0:T(8,128)(2,1)S(1)}, bf16[512,1024]{1,0:T(8,128)(2,1)S(1)}, bf16[512,1024]{1,0:T(8,128)(2,1)S(1)}, bf16[512,1024]{1,0:T(8,128)(2,1)S(1)}) fusion(f32[512]{0:T(512)S(1)} %select_multiply_fusion, s32[1024]{0:T(1024)S(1)} %iota_add_fusion, s32[512]{0:T(512)S(1)} %fusion.10, f32[512]{0:T(512)S(1)} %fusion.14, ...), kind=kLoop, calls=%fused_computation.21 | loop fusion | flops 18874368 | bytes 4210688 | tf_op jit(solution)/shard_map/convert
  36.5 2.4 %pad_maximum_fusion = (bf16[1024,1024]{1,0:T(8,128)(2,1)}, bf16[1024,1024]{1,0:T(8,128)(2,1)}) fusion(bf16[512,1024]{1,0:T(8,128)(2,1)S(1)} %get-tuple-element.69, bf16[512,1024]{1,0:T(8,128)(2,1)S(1)} %get-tuple-element.70, bf16[512,1024]{1,0:T(8,128)(2,1)S(1)} %get-tuple-element.66, bf16[512,1024]{1,0:T(8,128)(2,1)S(1)} %get-tuple-element.65), kind=kLoop, calls=%fused_computation.16 | loop fusion | flops 8388608 | bytes 8388608 | tf_op jit(solution)/shard_map/concatenate | solution.py:47
  38.9 0.7 fusion.7.refs_4_.refs_3_
  39.5 0.4 all-to-all-done
  40.0 0.2 copy.36
  40.2 0.2 copy.37
  40.4 0.4 maximum_bitcast_fusion
  40.8 0.3 copy.38
  41.1 1.1 copy.39
  42.2 8.5 %all-to-all-start.1 = ((bf16[8,16,2048]{2,1,0:T(8,128)(2,1)}), bf16[8,16,2048]{2,1,0:T(8,128)(2,1)S(1)}, u32[]{:S(2)}, u32[]{:S(2)}) async-start(bf16[8,16,2048]{2,1,0:T(8,128)(2,1)} %copy.39), calls=%async_computation.1 | async-start | bytes 1048576 | tf_op jit(solution)/shard_map/all_to_all | solution.py:262
  50.7 0.1 fusion.8
  50.8 1.7 %collective-permute-start.1 = (bf16[2,8,2048]{2,1,0:T(8,128)(2,1)S(1)}, bf16[2,8,2048]{2,1,0:T(8,128)(2,1)S(1)}, u32[]{:S(2)}, u32[]{:S(2)}) collective-permute-start(bf16[2,8,2048]{2,1,0:T(8,128)(2,1)S(1)} %fusion.8), channel_id=1, source_target_pairs={{0,2},{1,3},{2,0},{3,1},{4,6},{5,7},{6,4},{7,5},{8,10},{9,11},{10,... | collective-permute-start | bytes 196616 | tf_op jit(solution)/shard_map/ppermute | solution.py:242
  52.5 1.0 collective-permute-start.2
  53.4 3.1 %collective-permute-done.1 = bf16[2,8,2048]{2,1,0:T(8,128)(2,1)S(1)} collective-permute-done((bf16[2,8,2048]{2,1,0:T(8,128)(2,1)S(1)}, bf16[2,8,2048]{2,1,0:T(8,128)(2,1)S(1)}, u32[]{:S(2)}, u32[]{:S(2)}) %collective-permute-start.1) | collective-permute-done | bytes 65568 | tf_op jit(solution)/shard_map/ppermute | solution.py:242
  56.6 2.1 %collective-permute-done = bf16[2,8,2048]{2,1,0:T(8,128)(2,1)S(1)} collective-permute-done((bf16[2,8,2048]{2,1,0:T(8,128)(2,1)S(1)}, bf16[2,8,2048]{2,1,0:T(8,128)(2,1)S(1)}, u32[]{:S(2)}, u32[]{:S(2)}) %collective-permute-start) | collective-permute-done | bytes 65568 | tf_op jit(solution)/shard_map/ppermute | solution.py:242
  58.7 0.1 select_select_fusion.3
  58.8 0.8 maximum_convert_fusion.refs_0_
  63.5 4.9 %all-to-all-done.1 = bf16[8,16,2048]{2,1,0:T(8,128)(2,1)S(1)} async-done(((bf16[8,16,2048]{2,1,0:T(8,128)(2,1)}), bf16[8,16,2048]{2,1,0:T(8,128)(2,1)S(1)}, u32[]{:S(2)}, u32[]{:S(2)}) %all-to-all-start.1) | async-done | bytes 524320 | tf_op jit(solution)/shard_map/all_to_all | solution.py:262
  68.4 0.8 broadcast_in_dim.16
  69.2 6.7 %all-to-all-start.2 = ((bf16[8,16,2048]{2,1,0:T(8,128)(2,1)}), bf16[8,16,2048]{2,1,0:T(8,128)(2,1)S(1)}, u32[]{:S(2)}, u32[]{:S(2)}) async-start(bf16[8,16,2048]{2,1,0:T(8,128)(2,1)} %broadcast_in_dim.16), calls=%async_computation.2 | async-start | bytes 1048576 | tf_op jit(solution)/shard_map/all_to_all | solution.py:268
  75.9 0.6 collective-permute-start.3
  76.6 8.2 %collective-permute-done.3 = bf16[16,2048]{1,0:T(8,128)(2,1)S(1)} collective-permute-done((bf16[16,2048]{1,0:T(8,128)(2,1)S(1)}, bf16[16,2048]{1,0:T(8,128)(2,1)S(1)}, u32[]{:S(2)}, u32[]{:S(2)}) %collective-permute-start.3) | collective-permute-done | bytes 65568 | tf_op jit(solution)/shard_map/ppermute | solution.py:26
  84.8 2.0 %collective-permute-start.4 = (bf16[8,16,2048]{2,1,0:T(8,128)(2,1)S(1)}, bf16[8,16,2048]{2,1,0:T(8,128)(2,1)S(1)}, u32[]{:S(2)}, u32[]{:S(2)}) collective-permute-start(bf16[8,16,2048]{2,1,0:T(8,128)(2,1)S(1)} %all-to-all-done.2.refs_1_), channel_id=1, source_target_pairs={{0,8},{4,12},{8,16},{12,20},{16,24},{20,28},{24,32},{28,36},{32,40... | collective-permute-start | bytes 1572872 | tf_op jit(solution)/shard_map/ppermute | solution.py:26
  86.8 3.1 %cross_near.1.refs_3_ = bf16[128,2048]{1,0:T(8,128)(2,1)} custom-call(f32[8,8,2048]{2,1,0:T(8,128)} %maximum_convert_fusion.refs_0_, bf16[8,16,2048]{2,1,0:T(8,128)(2,1)S(1)} %all-to-all-done.2.refs_1_), custom_call_target="tpu_custom_call" | custom-call | flops 128000000 | bytes 131072 | tf_op jit(solution)/shard_map/cross_near/pallas_call | solution.py:134
  89.9 0.8 broadcast_in_dim.17
  90.8 5.7 %all-to-all-start.3 = ((bf16[8,16,2048]{2,1,0:T(8,128)(2,1)}), bf16[8,16,2048]{2,1,0:T(8,128)(2,1)S(1)}, u32[]{:S(2)}, u32[]{:S(2)}) async-start(bf16[8,16,2048]{2,1,0:T(8,128)(2,1)} %broadcast_in_dim.17), calls=%async_computation.3 | async-start | bytes 1048576 | tf_op jit(solution)/shard_map/all_to_all | solution.py:268
  96.5 1.8 %collective-permute-done.5.refs_2_ = bf16[8,16,2048]{2,1,0:T(8,128)(2,1)S(1)} collective-permute-done((bf16[8,16,2048]{2,1,0:T(8,128)(2,1)S(1)}, bf16[8,16,2048]{2,1,0:T(8,128)(2,1)S(1)}, u32[]{:S(2)}, u32[]{:S(2)}) %collective-permute-start.5) | collective-permute-done | bytes 524320 | tf_op jit(solution)/shard_map/ppermute | solution.py:26
  98.3 1.2 collective-permute-done.4.refs_1_
  99.5 0.5 collective-permute-start.6
  100.0 2.7 %collective-permute-start.7 = (bf16[8,16,2048]{2,1,0:T(8,128)(2,1)S(1)}, bf16[8,16,2048]{2,1,0:T(8,128)(2,1)S(1)}, u32[]{:S(2)}, u32[]{:S(2)}) collective-permute-start(bf16[8,16,2048]{2,1,0:T(8,128)(2,1)S(1)} %collective-permute-done.5.refs_2_), channel_id=1, source_target_pairs={{0,56},{4,60},{8,0},{12,4},{16,8},{20,12},{24,16},{28,20},{32,24},... | collective-permute-start | bytes 1572872 | tf_op jit(solution)/shard_map/ppermute | solution.py:26
  102.8 0.3 all-to-all-done.3.refs_1_
  103.1 7.4 %lags_1.1.refs_7_ = bf16[1024,2048]{1,0:T(8,128)(2,1)} custom-call(s32[64]{0:T(128)S(1)} %add.167.place, f32[8,8,2048]{2,1,0:T(8,128)} %maximum_convert_fusion.refs_0_, bf16[8,16,2048]{2,1,0:T(8,128)(2,1)S(1)} %collective-permute-done.4.refs_1_, bf16[8,16,2048]{2,1,0:T(8,128)(2,1)S(1)} %collective-permute-done.5.refs_2_, ...), custom_call_target="tpu_custom_call" | custom-call | flops 4608000000 | bytes 393216 | tf_op jit(solution)/shard_map/lags_1/pallas_call | solution.py:203
  110.5 2.9 %collective-permute-done.6.refs_2_ = bf16[8,16,2048]{2,1,0:T(8,128)(2,1)S(1)} collective-permute-done((bf16[8,16,2048]{2,1,0:T(8,128)(2,1)S(1)}, bf16[8,16,2048]{2,1,0:T(8,128)(2,1)S(1)}, u32[]{:S(2)}, u32[]{:S(2)}) %collective-permute-start.6) | collective-permute-done | bytes 524320 | tf_op jit(solution)/shard_map/ppermute | solution.py:26
  113.3 3.2 %collective-permute-start.9 = (bf16[8,16,2048]{2,1,0:T(8,128)(2,1)S(1)}, bf16[8,16,2048]{2,1,0:T(8,128)(2,1)S(1)}, u32[]{:S(2)}, u32[]{:S(2)}) collective-permute-start(bf16[8,16,2048]{2,1,0:T(8,128)(2,1)S(1)} %collective-permute-done.7.refs_3_), channel_id=1, source_target_pairs={{0,56},{4,60},{8,0},{12,4},{16,8},{20,12},{24,16},{28,20},{32,24},... | collective-permute-start | bytes 1572872 | tf_op jit(solution)/shard_map/ppermute | solution.py:26
  116.6 8.6 %lags_2.1.refs_6_ = bf16[1024,2048]{1,0:T(8,128)(2,1)} custom-call(s32[64]{0:T(128)S(1)} %add.167.place, f32[8,8,2048]{2,1,0:T(8,128)} %maximum_convert_fusion.refs_0_, bf16[8,16,2048]{2,1,0:T(8,128)(2,1)S(1)} %all-to-all-done.3.refs_1_, bf16[8,16,2048]{2,1,0:T(8,128)(2,1)S(1)} %collective-permute-done.6.refs_2_, ...), custom_call_target="tpu_custom_call", output_to_operand_aliasing={{}: (8, {})} | custom-call | flops 4608000000 | bytes 393216 | tf_op jit(solution)/shard_map/lags_2/pallas_call | solution.py:203
  125.1 1.1 collective-permute-done.8.refs_1_
  126.2 6.6 %lags_3.1 = bf16[1024,2048]{1,0:T(8,128)(2,1)} custom-call(s32[64]{0:T(128)S(1)} %add.167.place, f32[8,8,2048]{2,1,0:T(8,128)} %maximum_convert_fusion.refs_0_, bf16[8,16,2048]{2,1,0:T(8,128)(2,1)S(1)} %collective-permute-done.8.refs_1_, bf16[8,16,2048]{2,1,0:T(8,128)(2,1)S(1)} %collective-permute-done.9.refs_2_, ...), custom_call_target="tpu_custom_call", output_to_operand_aliasing={{}: (7, {})} | custom-call | flops 3072000000 | bytes 262144 | tf_op jit(solution)/shard_map/lags_3/pallas_call | solution.py:203
  (32 shorter events, 0.2 us)
Async XLA Ops:
  6.7 7.9 %copy-start.1 = (s32[2]{0:T(128)S(1)}, s32[2]{0:T(128)}, u32[]{:S(2)}) copy-start(s32[2]{0:T(128)} %param.8) | copy-start | bytes 28
  6.7 7.9 %copy-start.3 = (s32[8]{0:T(128)S(1)}, s32[8]{0:T(128)}, u32[]{:S(2)}) copy-start(s32[8]{0:T(128)} %constant.173) | copy-start | bytes 100
  6.7 9.2 %copy-start.2 = (s32[8]{0:T(128)S(1)}, s32[8]{0:T(128)}, u32[]{:S(2)}) copy-start(s32[8]{0:T(128)} %param.10) | copy-start | bytes 100
  6.7 33.2 %all-to-all-start = ((bf16[32,16,2048]{2,1,0:T(8,128)(2,1)}), bf16[32,16,2048]{2,1,0:T(8,128)(2,1)S(1)}, u32[]{:S(2)}, u32[]{:S(2)}) async-start(bf16[32,16,2048]{2,1,0:T(8,128)(2,1)} %reshape.118), calls=%async_computation | async-start | bytes 4194304 | tf_op jit(solution)/shard_map/all_to_all | solution.py:237
  40.4 10.2 %copy-start = (bf16[8,2,2048]{2,1,0:T(2,128)(2,1)S(1)}, bf16[8,2,2048]{2,1,0:T(2,128)(2,1)}, u32[]{:S(2)}) copy-start(bf16[8,2,2048]{2,1,0:T(2,128)(2,1)} %param.7) | copy-start | bytes 196612
  42.2 26.2 %all-to-all-start.1 = ((bf16[8,16,2048]{2,1,0:T(8,128)(2,1)}), bf16[8,16,2048]{2,1,0:T(8,128)(2,1)S(1)}, u32[]{:S(2)}, u32[]{:S(2)}) async-start(bf16[8,16,2048]{2,1,0:T(8,128)(2,1)} %copy.39), calls=%async_computation.1 | async-start | bytes 1048576 | tf_op jit(solution)/shard_map/all_to_all | solution.py:262
  50.8 5.8 %collective-permute-start.1 = (bf16[2,8,2048]{2,1,0:T(8,128)(2,1)S(1)}, bf16[2,8,2048]{2,1,0:T(8,128)(2,1)S(1)}, u32[]{:S(2)}, u32[]{:S(2)}) collective-permute-start(bf16[2,8,2048]{2,1,0:T(8,128)(2,1)S(1)} %fusion.8), channel_id=1, source_target_pairs={{0,2},{1,3},{2,0},{3,1},{4,6},{5,7},{6,4},{7,5},{8,10},{9,11},{10,... | collective-permute-start | bytes 196616 | tf_op jit(solution)/shard_map/ppermute | solution.py:242
  52.5 4.1 %collective-permute-start.2 = (bf16[2,8,2048]{2,1,0:T(8,128)(2,1)S(1)}, bf16[2,8,2048]{2,1,0:T(8,128)(2,1)S(1)}, u32[]{:S(2)}, u32[]{:S(2)}) collective-permute-start(bf16[2,8,2048]{2,1,0:T(8,128)(2,1)S(1)} %fusion.8), channel_id=1, source_target_pairs={{0,3},{1,0},{2,1},{3,2},{4,7},{5,4},{6,5},{7,6},{8,11},{9,8},{10,9... | collective-permute-start | bytes 196616 | tf_op jit(solution)/shard_map/ppermute | solution.py:242
  53.4 5.3 %collective-permute-start = (bf16[2,8,2048]{2,1,0:T(8,128)(2,1)S(1)}, bf16[2,8,2048]{2,1,0:T(8,128)(2,1)S(1)}, u32[]{:S(2)}, u32[]{:S(2)}) collective-permute-start(bf16[2,8,2048]{2,1,0:T(8,128)(2,1)S(1)} %fusion.8), channel_id=1, source_target_pairs={{0,1},{1,2},{2,3},{3,0},{4,5},{5,6},{6,7},{7,4},{8,9},{9,10},{10,1... | collective-permute-start | bytes 196616 | tf_op jit(solution)/shard_map/ppermute | solution.py:242
  69.2 15.6 %all-to-all-start.2 = ((bf16[8,16,2048]{2,1,0:T(8,128)(2,1)}), bf16[8,16,2048]{2,1,0:T(8,128)(2,1)S(1)}, u32[]{:S(2)}, u32[]{:S(2)}) async-start(bf16[8,16,2048]{2,1,0:T(8,128)(2,1)} %broadcast_in_dim.16), calls=%async_computation.2 | async-start | bytes 1048576 | tf_op jit(solution)/shard_map/all_to_all | solution.py:268
  75.9 8.9 %collective-permute-start.3 = (bf16[16,2048]{1,0:T(8,128)(2,1)S(1)}, bf16[16,2048]{1,0:T(8,128)(2,1)S(1)}, u32[]{:S(2)}, u32[]{:S(2)}) collective-permute-start(bf16[16,2048]{1,0:T(8,128)(2,1)S(1)} %pad_maximum_fusion.2), channel_id=1, source_target_pairs={{0,32},{4,36},{8,40},{12,44},{16,48},{20,52},{24,56},{28,60},{32,0... | collective-permute-start | bytes 196616 | tf_op jit(solution)/shard_map/ppermute | solution.py:26
  84.8 13.5 %collective-permute-start.5 = (bf16[8,16,2048]{2,1,0:T(8,128)(2,1)S(1)}, bf16[8,16,2048]{2,1,0:T(8,128)(2,1)S(1)}, u32[]{:S(2)}, u32[]{:S(2)}) collective-permute-start(bf16[8,16,2048]{2,1,0:T(8,128)(2,1)S(1)} %all-to-all-done.2.refs_1_), channel_id=1, source_target_pairs={{0,56},{4,60},{8,0},{12,4},{16,8},{20,12},{24,16},{28,20},{32,24},... | collective-permute-start | bytes 1572872 | tf_op jit(solution)/shard_map/ppermute | solution.py:26
  84.8 14.7 %collective-permute-start.4 = (bf16[8,16,2048]{2,1,0:T(8,128)(2,1)S(1)}, bf16[8,16,2048]{2,1,0:T(8,128)(2,1)S(1)}, u32[]{:S(2)}, u32[]{:S(2)}) collective-permute-start(bf16[8,16,2048]{2,1,0:T(8,128)(2,1)S(1)} %all-to-all-done.2.refs_1_), channel_id=1, source_target_pairs={{0,8},{4,12},{8,16},{12,20},{16,24},{20,28},{24,32},{28,36},{32,40... | collective-permute-start | bytes 1572872 | tf_op jit(solution)/shard_map/ppermute | solution.py:26
  90.8 12.3 %all-to-all-start.3 = ((bf16[8,16,2048]{2,1,0:T(8,128)(2,1)}), bf16[8,16,2048]{2,1,0:T(8,128)(2,1)S(1)}, u32[]{:S(2)}, u32[]{:S(2)}) async-start(bf16[8,16,2048]{2,1,0:T(8,128)(2,1)} %broadcast_in_dim.17), calls=%async_computation.3 | async-start | bytes 1048576 | tf_op jit(solution)/shard_map/all_to_all | solution.py:268
  99.5 13.8 %collective-permute-start.6 = (bf16[8,16,2048]{2,1,0:T(8,128)(2,1)S(1)}, bf16[8,16,2048]{2,1,0:T(8,128)(2,1)S(1)}, u32[]{:S(2)}, u32[]{:S(2)}) collective-permute-start(bf16[8,16,2048]{2,1,0:T(8,128)(2,1)S(1)} %collective-permute-done.4.refs_1_), channel_id=1, source_target_pairs={{0,8},{4,12},{8,16},{12,20},{16,24},{20,28},{24,32},{28,36},{32,40... | collective-permute-start | bytes 1572872 | tf_op jit(solution)/shard_map/ppermute | solution.py:26
  100.0 13.3 %collective-permute-start.7 = (bf16[8,16,2048]{2,1,0:T(8,128)(2,1)S(1)}, bf16[8,16,2048]{2,1,0:T(8,128)(2,1)S(1)}, u32[]{:S(2)}, u32[]{:S(2)}) collective-permute-start(bf16[8,16,2048]{2,1,0:T(8,128)(2,1)S(1)} %collective-permute-done.5.refs_2_), channel_id=1, source_target_pairs={{0,56},{4,60},{8,0},{12,4},{16,8},{20,12},{24,16},{28,20},{32,24},... | collective-permute-start | bytes 1572872 | tf_op jit(solution)/shard_map/ppermute | solution.py:26
  113.3 12.9 %collective-permute-start.8 = (bf16[8,16,2048]{2,1,0:T(8,128)(2,1)S(1)}, bf16[8,16,2048]{2,1,0:T(8,128)(2,1)S(1)}, u32[]{:S(2)}, u32[]{:S(2)}) collective-permute-start(bf16[8,16,2048]{2,1,0:T(8,128)(2,1)S(1)} %collective-permute-done.6.refs_2_), channel_id=1, source_target_pairs={{0,8},{4,12},{8,16},{12,20},{16,24},{20,28},{24,32},{28,36},{32,40... | collective-permute-start | bytes 1572872 | tf_op jit(solution)/shard_map/ppermute | solution.py:26
  113.3 12.9 %collective-permute-start.9 = (bf16[8,16,2048]{2,1,0:T(8,128)(2,1)S(1)}, bf16[8,16,2048]{2,1,0:T(8,128)(2,1)S(1)}, u32[]{:S(2)}, u32[]{:S(2)}) collective-permute-start(bf16[8,16,2048]{2,1,0:T(8,128)(2,1)S(1)} %collective-permute-done.7.refs_3_), channel_id=1, source_target_pairs={{0,56},{4,60},{8,0},{12,4},{16,8},{20,12},{24,16},{28,20},{32,24},... | collective-permute-start | bytes 1572872 | tf_op jit(solution)/shard_map/ppermute | solution.py:26
